TPU v7x, 256 devices: a whole 4x4x8 slice. The times are simulated.
256 devices in a mesh: wide: 32 (over x, z), narrow: 8 (over y, core).
Axes of the slice: x: 4, y: 4, z: 8, core: 2. Of those that a mesh axis runs over, the one named last changes fastest.
Arguments:
- tokens: bfloat16 [65536, 4096], P(('wide', 'narrow')), may hold values from -6 to 6
- block_scales: float32 [65536, 32], P(('wide', 'narrow')), may hold values from 0.5 to 2
- pick_index: int32 [32, 384], replicated, may hold values from 0 to 65535, as said below
- pick_gates: float32 [32, 384], replicated, may hold values from 0.1 to 1
- pick_counts: int32 [65536], P(('wide', 'narrow')), may hold values from 0 to 32, as said below
- gate_weight: bfloat16 [32, 4096, 1536], P('wide', None, 'narrow'), may hold values from -0.09375 to 0.09375
- up_weight: bfloat16 [32, 4096, 1536], P('wide', None, 'narrow'), may hold values from -0.09375 to 0.09375
- down_weight: bfloat16 [32, 1536, 4096], P('wide', 'narrow'), may hold values from -0.15625 to 0.15625
Outputs:
- mixed: bfloat16 [65536, 4096], P(('wide', 'narrow'))
Inputs may be any that keep to these rules, and one draw needn't show every extreme that they name: `pick_index`: each row names 384 different tokens; at most 3 of them lie among the 256 tokens of one device (tokens d * 256 to (d + 1) * 256 - 1), and in every row some device has exactly 3. `pick_counts`: the number of times the token appears in pick_index.
All inputs are finite; a program needn't handle non-finite values.
Results may differ from a plain program's by a relative error of at most 0.0041.
Values may be sent and summed in bfloat16 or wider, within the bound.
No kernel may reach another device: no remote copies, remote signals or barrier semaphores. Data moves between devices by JAX's collectives and lax.ppermute only.
A program may use at most 128 MiB of HBM per device.

v0:
```python
import jax
import jax.numpy as jnp
from jax import lax
from jax.sharding import PartitionSpec as P

BLOCK = 128
MOST = 3


def local(
    tokens, block_scales, pick_index, pick_gates, pick_counts, gate_weight, up_weight, down_weight
):
    tok_rows = tokens.shape[0]
    width = tokens.shape[1]
    n_wide = lax.axis_size("wide")
    n_narrow = lax.axis_size("narrow")
    my_rank = lax.axis_index("wide") * n_narrow + lax.axis_index("narrow")
    scaled = (
        tokens.astype(jnp.float32).reshape(tok_rows, width // BLOCK, BLOCK)
        * block_scales[:, :, None]
    )
    rows = scaled.reshape(tok_rows, width).astype(jnp.bfloat16)
    owners = pick_index // tok_rows
    mine = owners == my_rank
    order_in = jnp.cumsum(mine.astype(jnp.int32), axis=1) - 1
    slots = jnp.arange(MOST, dtype=jnp.int32)
    matched = mine[:, :, None] & (order_in[:, :, None] == slots[None, None, :])
    local_ids = pick_index - my_rank * tok_rows
    slot_token = jnp.sum(jnp.where(matched, local_ids[:, :, None], 0), axis=1)
    slot_valid = jnp.any(matched, axis=1)
    slot_gate = jnp.sum(jnp.where(matched, pick_gates[:, :, None], 0.0), axis=1)
    outgoing = rows[slot_token.reshape(-1)].reshape(n_wide, MOST, width)
    outgoing = jnp.where(slot_valid[:, :, None], outgoing, jnp.zeros_like(outgoing))
    arrived = lax.all_to_all(outgoing, "wide", split_axis=0, concat_axis=0, tiled=True)
    piece = lax.all_gather(arrived[None], "narrow", axis=0, tiled=True)
    count = piece.shape[0]
    flat_rows = piece.reshape(-1, width)
    gate = jnp.dot(flat_rows, gate_weight[0], preferred_element_type=jnp.float32)
    upper = jnp.dot(flat_rows, up_weight[0], preferred_element_type=jnp.float32)
    hidden_piece = (jax.nn.silu(gate) * upper).astype(jnp.bfloat16)
    hidden = hidden_piece.reshape(count, n_wide, MOST, -1)
    partial_out = jnp.einsum(
        "abkh,hd->abkd", hidden, down_weight[0], preferred_element_type=jnp.float32
    )
    returned = lax.all_to_all(partial_out, "wide", split_axis=1, concat_axis=1, tiled=True)
    summed = lax.psum_scatter(returned, "narrow", scatter_dimension=0, tiled=True)
    expert_out = summed.astype(jnp.bfloat16)[0]
    token_ids = jnp.arange(tok_rows, dtype=jnp.int32)
    placing = (slot_token.reshape(-1)[:, None] == token_ids[None, :]) & slot_valid.reshape(-1)[
        :, None
    ]
    weights = jnp.where(placing, slot_gate.reshape(-1)[:, None], 0.0)
    branch = jnp.dot(
        weights.T,
        expert_out.reshape(-1, width).astype(jnp.float32),
        precision=lax.Precision.HIGHEST,
    )
    divisor = jnp.maximum(pick_counts, 1).astype(jnp.float32)
    return (rows.astype(jnp.float32) + branch / divisor[:, None]).astype(jnp.bfloat16)


def solution(mesh):
    return jax.shard_map(
        local,
        mesh=mesh,
        in_specs=(
            P(("wide", "narrow"), None),
            P(("wide", "narrow"), None),
            P(),
            P(),
            P(("wide", "narrow")),
            P("wide", None, "narrow"),
            P("wide", None, "narrow"),
            P("wide", "narrow", None),
        ),
        out_specs=P(("wide", "narrow"), None),
        check_vma=False,
    )
```

profile of v0, /device:TPU:32, one launch (start us, length us, event | category | flops | bytes accessed | tf_op | source)
XLA Modules:
  0.0 525.2 jit_solution(4453136809016714768)
XLA Ops:
  6.5 0.0 copy-start
  6.5 0.0 all-gather.3.cloned.1.call-start
  6.5 1.0 convert_bitcast_fusion
  7.5 0.8 broadcast_subtract_fusion
  8.3 0.9 reduce-window.6
  9.2 0.2 slice_reduce_fusion
  9.5 0.1 copy_bitcast_fusion
  9.5 0.1 fusion.17
  9.7 0.2 select_reduce_fusion.1
  9.9 0.1 copy.40
  10.0 0.1 copy.39
  10.0 0.1 reshape.77
  10.2 0.9 copy.36
  11.0 0.0 copy-start.3
  11.1 1.1 mul.24
  12.2 0.4 copy-done.3
  12.6 3.9 fusion.2
  16.5 3.6 gather_fusion
  20.2 0.5 reshape.78
  20.7 0.5 broadcast_select_fusion
  21.2 39.5 %all_to_all.10 = bf16[32,3,4096]{2,1,0:T(4,128)(2,1)S(1)} all-to-all(bf16[32,3,4096]{2,1,0:T(4,128)(2,1)S(1)} %broadcast_select_fusion), channel_id=1, replica_groups=mesh['wide'=32,'narrow'=8] {'wide'}, dimensions={0} | all-to-all | bytes 1572864 | tf_op jit(solution)/shard_map/all_to_all | solution.py:34
  60.7 1.5 copy.44
  62.2 0.0 all-gather.3.cloned.1.call-update
  62.2 0.2 reduce-scatter.2.cloned.1.call-start
  62.5 40.0 %all-gather.3.cloned.1.call-done = bf16[256,3,4096]{2,0,1:T(8,128)(2,1)} async-done(((bf16[32,3,4096]{2,0,1:T(8,128)(2,1)}), bf16[256,3,4096]{2,0,1:T(8,128)(2,1)}) %all-gather.3.cloned.1.call-update) | async-done | bytes 6291472 | tf_op jit(solution)/shard_map/all_gather | solution.py:35
  102.5 11.4 %copy.45 = bf16[256,3,4096]{2,1,0:T(4,128)(2,1)} copy(bf16[256,3,4096]{2,0,1:T(8,128)(2,1)} %all-gather.3.cloned.1.call-done) | data formatting | bytes 12582912 | tf_op jit(solution)/shard_map/all_gather | solution.py:35
  113.9 0.0 copy-start.6
  113.9 13.9 %reshape.79 = bf16[768,4096]{1,0:T(8,128)(2,1)} reshape(bf16[256,3,4096]{2,1,0:T(4,128)(2,1)} %copy.45) | data formatting | bytes 12582912 | tf_op jit(solution)/shard_map/reshape | solution.py:37
  127.8 0.0 copy-done.6
  127.8 0.0 copy-start.2
  127.8 0.0 copy-start.7
  127.8 5.2 fusion.7
  132.9 0.0 copy-done.2
  132.9 0.0 copy-done.7
  132.9 2.2 fusion.12
  135.2 0.2 copy.46
  135.4 0.2 reshape.80
  135.6 0.0 copy-done
  135.6 1.9 fusion.3
  137.5 285.9 %all_to_all.11 = f32[8,32,3,4096]{3,0,2,1:T(8,128)} all-to-all(f32[8,32,3,4096]{3,0,2,1:T(8,128)S(1)} %fusion.3), channel_id=1, replica_groups=mesh['wide'=32,'narrow'=8] {'wide'}, dimensions={1} | all-to-all | bytes 25165824 | tf_op jit(solution)/shard_map/all_to_all | solution.py:45
  423.3 16.4 %copy.49 = f32[8,32,3,4096]{3,1,2,0:T(8,128)} copy(f32[8,32,3,4096]{3,0,2,1:T(8,128)} %all_to_all.11) | data formatting | bytes 25165824 | tf_op jit(solution)/shard_map/all_to_all | solution.py:45
  439.8 0.0 copy-start.4
  439.8 0.0 copy-start.5
  439.8 0.0 reduce-scatter.2.cloned.1.call-update
  439.8 0.1 and.28
  439.9 0.1 eq.39
  440.0 0.6 copy-done.4
  440.6 0.1 select_reduce_fusion
  440.7 0.1 copy.41
  440.8 0.1 broadcast_in_dim.66
  440.9 0.0 copy-done.5
  440.9 69.4 %reduce-scatter.2.cloned.1.call-done = f32[1,32,3,4096]{3,1,2,0:T(8,128)} async-done(((f32[8,32,3,4096]{3,1,2,0:T(8,128)}), f32[1,32,3,4096]{3,1,2,0:T(8,128)}) %reduce-scatter.2.cloned.1.call-update) | async-done | bytes 1572880 | tf_op jit(solution)/shard_map/reduce_scatter | solution.py:46
  510.3 1.5 convert_element_type.27
  511.8 0.7 copy.50
  512.5 0.7 reshape_squeeze.3
  513.2 0.0 copy-start.1
  513.2 5.2 fusion.1
  518.4 0.0 copy-done.1
  (5 shorter events, 0.1 us)
Async XLA Ops:
  6.5 129.0 %copy-start = (bf16[1,192,4096]{2,1,0:T(8,128)(2,1)S(1)}, bf16[1,192,4096]{2,1,0:T(8,128)(2,1)}, u32[]{:S(2)}) copy-start(bf16[1,192,4096]{2,1,0:T(8,128)(2,1)} %param.15) | copy-start | bytes 4718596
  6.5 95.9 %all-gather.3.cloned.1.call-start = ((), (), s32[]{:S(2)}) async-start(), calls=%async_computation.4 | async-start | bytes 7077888 | tf_op jit(solution)/shard_map/all_gather | solution.py:35
  11.0 1.6 copy-start.3
  62.2 448.1 %reduce-scatter.2.cloned.1.call-start = ((), (), s32[]{:S(2)}) async-start(), calls=%async_computation.3 | async-start | bytes 14155776 | tf_op jit(solution)/shard_map/reduce_scatter | solution.py:46
  113.9 13.9 %copy-start.6 = (bf16[1,4096,192]{1,2,0:T(8,128)(2,1)S(1)}, bf16[1,4096,192]{1,2,0:T(8,128)(2,1)}, u32[]{:S(2)}) copy-start(bf16[1,4096,192]{1,2,0:T(8,128)(2,1)} %param.13) | copy-start | bytes 4718596
  127.8 5.2 copy-start.2
  127.8 5.2 copy-start.7
  439.8 0.8 copy-start.4
  439.8 1.1 copy-start.5
  513.2 5.2 copy-start.1
Sparse Core Ops, SparseCore 0:
  62.3 40.0 all-gather.2
  439.9 70.3 reduce-scatter.1
where the time goes:
time: 527 us; the launch traced here: 525 us
  blocking collectives  325 us (62%)
  waiting for transfers between devices  109 us (21%)
  local copies, waits for them, and re-layouts  53 us (10%)
  matrix products  14.5 us (3%)
  between operations  13.6 us (3%)
  other arithmetic  9.12 us (2%)
    all_to_all x1, blocking collectives, local(): lax.all_to_all(partial_out, 'wide', split_axis=1, concat_axis=1, tiled=True)  286 us
    reduce_scatter x1, waiting for transfers between devices, local(): lax.psum_scatter(returned, 'narrow', scatter_dimension=0, tiled=True)  69.4 us
    all_gather x1, waiting for transfers between devices, local(): piece = lax.all_gather(arrived[None], 'narrow', axis=0, tiled=True)  40 us
    all_to_all x1, blocking collectives, local(): lax.all_to_all(outgoing, 'wide', split_axis=0, concat_axis=0, tiled=True)  39.5 us
    all_to_all x1, local copies, waits for them, and re-layouts, local(): lax.all_to_all(partial_out, 'wide', split_axis=1, concat_axis=1, tiled=True)  16.4 us
    reshape x1, local copies, waits for them, and re-layouts, local(): flat_rows = piece.reshape(-1, width)  13.9 us
    all_gather x1, local copies, waits for them, and re-layouts, local(): piece = lax.all_gather(arrived[None], 'narrow', axis=0, tiled=True)  11.4 us
  transfers between devices with their start and end apart: 2, of which 2 were waited for; matrix products, arithmetic and copies ran while one was open for 0% of the time, Pallas kernels for 0%

commit v1 on v0

--- a/solution.py
+++ b/solution.py
@@ -32,19 +32,15 @@
     outgoing = rows[slot_token.reshape(-1)].reshape(n_wide, MOST, width)
     outgoing = jnp.where(slot_valid[:, :, None], outgoing, jnp.zeros_like(outgoing))
     arrived = lax.all_to_all(outgoing, "wide", split_axis=0, concat_axis=0, tiled=True)
-    piece = lax.all_gather(arrived[None], "narrow", axis=0, tiled=True)
-    count = piece.shape[0]
-    flat_rows = piece.reshape(-1, width)
+    arrived = arrived.reshape(n_wide * MOST, width)
+    flat_rows = lax.all_gather(arrived, "narrow", axis=0, tiled=True)
     gate = jnp.dot(flat_rows, gate_weight[0], preferred_element_type=jnp.float32)
     upper = jnp.dot(flat_rows, up_weight[0], preferred_element_type=jnp.float32)
-    hidden_piece = (jax.nn.silu(gate) * upper).astype(jnp.bfloat16)
-    hidden = hidden_piece.reshape(count, n_wide, MOST, -1)
-    partial_out = jnp.einsum(
-        "abkh,hd->abkd", hidden, down_weight[0], preferred_element_type=jnp.float32
-    )
-    returned = lax.all_to_all(partial_out, "wide", split_axis=1, concat_axis=1, tiled=True)
-    summed = lax.psum_scatter(returned, "narrow", scatter_dimension=0, tiled=True)
-    expert_out = summed.astype(jnp.bfloat16)[0]
+    hidden = (jax.nn.silu(gate) * upper).astype(jnp.bfloat16)
+    partial_out = jnp.dot(hidden, down_weight[0], preferred_element_type=jnp.float32)
+    summed = lax.psum_scatter(partial_out, "narrow", scatter_dimension=0, tiled=True)
+    summed = summed.astype(jnp.bfloat16).reshape(n_wide, MOST, width)
+    expert_out = lax.all_to_all(summed, "wide", split_axis=0, concat_axis=0, tiled=True)
     token_ids = jnp.arange(tok_rows, dtype=jnp.int32)
     placing = (slot_token.reshape(-1)[:, None] == token_ids[None, :]) & slot_valid.reshape(-1)[
         :, None

time: 527 us -> 250 us (0.47)
  blocking collectives: 325 us -> 39.5 us
  local copies, waits for them, and re-layouts: 53 us -> 11 us
  waiting for transfers between devices: 109 us -> 143 us
  starting transfers between devices: 0.22 us -> 10.3 us
  matrix products: 14.5 us -> 23.8 us
    all_to_all x1 -> x0, blocking collectives: 286 us -> none  [local(): lax.all_to_all(partial_out, 'wide', split_axis=1, concat_axis=1, tiled=True)]
    all_to_all x0 -> x1, waiting for transfers between devices: none -> 27.4 us  [local(): lax.all_to_all(summed, 'wide', split_axis=0, concat_axis=0, tiled=True)]
    all_to_all x2 -> x0, local copies, waits for them, and re-layouts: 17.9 us -> none  [the longest x1 16.4 us: local(): lax.all_to_all(partial_out, 'wide', split_axis=1, concat_axis=1, tiled=True)]
    all_gather x1 -> x0, local copies, waits for them, and re-layouts: 11.4 us -> none  [local(): piece = lax.all_gather(arrived[None], 'narrow', axis=0, tiled=True)]
    reshape x2 -> x3, local copies, waits for them, and re-layouts: 14.1 us -> 3.4 us  [the longest x1 1.42 us: local(): arrived = arrived.reshape(n_wide * MOST, width)]
    all_to_all x0 -> x1, starting transfers between devices: none -> 10.1 us  [local(): lax.all_to_all(summed, 'wide', split_axis=0, concat_axis=0, tiled=True)]
    dot_general x2 -> x1, matrix products: 4.14 us -> 12.5 us  [local(): jnp.dot(hidden, down_weight[0], preferred_element_type=jnp.float32)]
    reduce_scatter x1, waiting for transfers between devices: 69.4 us -> 75.2 us  [local(): lax.psum_scatter(partial_out, 'narrow', scatter_dimension=0, tiled=True)]
  transfers between devices with their start and end apart: 2 -> 3, of which waited for: 2 -> 3; matrix products, arithmetic and copies ran while one was open for 0% -> 0% of each run, Pallas kernels for 0% -> 0%
where the time goes in v1:
time: 250 us
  waiting for transfers between devices  143 us (57%)
  blocking collectives  39.5 us (16%)
  matrix products  23.8 us (10%)
  between operations  13.5 us (5%)
  local copies, waits for them, and re-layouts  11 us (4%)
  starting transfers between devices  10.3 us (4%)
  other arithmetic  9.12 us (4%)
    reduce_scatter x1, waiting for transfers between devices, local(): lax.psum_scatter(partial_out, 'narrow', scatter_dimension=0, tiled=True)  75.2 us
    all_gather x1, waiting for transfers between devices, local(): flat_rows = lax.all_gather(arrived, 'narrow', axis=0, tiled=True)  40 us
    all_to_all x1, blocking collectives, local(): lax.all_to_all(outgoing, 'wide', split_axis=0, concat_axis=0, tiled=True)  39.5 us
    all_to_all x1, waiting for transfers between devices, local(): lax.all_to_all(summed, 'wide', split_axis=0, concat_axis=0, tiled=True)  27.4 us
    dot_general x1, matrix products, local(): jnp.dot(hidden, down_weight[0], preferred_element_type=jnp.float32)  12.5 us
    all_to_all x1, starting transfers between devices, local(): lax.all_to_all(summed, 'wide', split_axis=0, concat_axis=0, tiled=True)  10.1 us
    dot_general x1, matrix products, local(): jnp.dot(flat_rows, gate_weight[0], preferred_element_type=jnp.float32)  6.26 us
    dot_general x1, matrix products, local(): jnp.dot(weights.T, expert_out.reshape(-1, width).astype(jnp.float32), pre...  5.05 us
  transfers between devices with their start and end apart: 3, of which 3 were waited for; matrix products, arithmetic and copies ran while one was open for 0% of the time, Pallas kernels for 0%

profile of v1, /device:TPU:32, one launch (start us, length us, event | category | flops | bytes accessed | tf_op | source)
XLA Modules:
  0.0 249.8 jit_solution(10874531708686188546)
XLA Ops:
  6.5 0.0 copy-start
  6.5 0.0 all-gather.2.cloned.1.call-start
  6.5 1.0 convert_bitcast_fusion
  7.5 0.8 broadcast_subtract_fusion
  8.3 0.9 reduce-window.6
  9.2 0.2 slice_reduce_fusion
  9.5 0.1 copy_bitcast_fusion
  9.5 0.1 fusion.24
  9.7 0.2 select_reduce_fusion.1
  9.9 0.1 copy.18
  10.0 0.1 copy.17
  10.0 0.1 reshape.80
  10.2 0.9 copy.14
  11.0 0.0 copy-start.1
  11.1 1.1 mul.24
  12.2 0.4 copy-done.1
  12.6 3.9 %fusion.2 = bf16[256,4096]{1,0:T(8,128)(2,1)} fusion(f32[32,8,32,128]{3,2,1,0:T(8,128)S(1)} %bitcast.36, bf16[256,4096]{1,0:T(8,128)(2,1)S(1)} %copy-done.1), kind=kLoop, calls=%fused_computation.5 | loop fusion | flops 3145728 | bytes 8388608 | tf_op jit(solution)/shard_map/convert_element_type | solution.py:22
  16.5 3.6 %gather_fusion = bf16[96,4096]{1,0:T(8,128)(2,1)S(1)} fusion(bf16[256,4096]{1,0:T(8,128)(2,1)} %fusion.2, s32[1024]{0:T(1024)S(1)} %pad_clamp_fusion), kind=kCustom, calls=%fused_computation | custom fusion | bytes 1573248 | tf_op jit(solution)/shard_map/gather | solution.py:32
  20.2 0.5 reshape.81
  20.7 0.5 broadcast_select_fusion
  21.2 39.5 %all_to_all.10 = bf16[32,3,4096]{2,1,0:T(4,128)(2,1)S(1)} all-to-all(bf16[32,3,4096]{2,1,0:T(4,128)(2,1)S(1)} %broadcast_select_fusion), channel_id=1, replica_groups=mesh['wide'=32,'narrow'=8] {'wide'}, dimensions={0} | all-to-all | bytes 1572864 | tf_op jit(solution)/shard_map/all_to_all | solution.py:34
  60.7 1.4 reshape.82
  62.2 0.0 all-gather.2.cloned.1.call-update
  62.2 0.0 copy-start.2
  62.2 0.2 reduce-scatter.2.cloned.1.call-start
  62.4 40.0 %all-gather.2.cloned.1.call-done = bf16[768,4096]{1,0:T(8,128)(2,1)} async-done(((bf16[96,4096]{1,0:T(8,128)(2,1)}), bf16[768,4096]{1,0:T(8,128)(2,1)}) %all-gather.2.cloned.1.call-update) | async-done | bytes 6291472 | tf_op jit(solution)/shard_map/all_gather | solution.py:36
  102.4 6.3 %fusion.7 = f32[768,192]{0,1:T(8,128)} fusion(bf16[768,4096]{1,0:T(8,128)(2,1)} %all-gather.2.cloned.1.call-done, bf16[1,4096,192]{1,2,0:T(8,128)(2,1)} %param.13), kind=kOutput, calls=%fused_computation.10 | convolution fusion | flops 1207959552 | bytes 8454144 | tf_op jit(solution)/shard_map/dot_general | solution.py:37
  108.7 0.0 copy-done
  108.7 0.0 copy-done.2
  108.7 12.5 %fusion.3 = f32[768,4096]{1,0:T(8,128)} fusion(bf16[1,192,4096]{2,1,0:T(8,128)(2,1)S(1)} %copy-done, bf16[768,4096]{1,0:T(8,128)(2,1)} %all-gather.2.cloned.1.call-done, bf16[1,4096,192]{1,2,0:T(8,128)(2,1)S(1)} %copy-done.2, f32[768,192]{0,1:T(8,128)} %fusion.7), kind=kOutput, calls=%fused_computation.6 | convolution fusion | flops 2416803840 | bytes 22609920 | tf_op jit(solution)/shard_map/dot_general | solution.py:40
  121.2 0.0 reduce-scatter.2.cloned.1.call-update
  121.2 75.2 %reduce-scatter.2.cloned.1.call-done = f32[96,4096]{1,0:T(8,128)} async-done(((f32[768,4096]{1,0:T(8,128)}), f32[96,4096]{1,0:T(8,128)}) %reduce-scatter.2.cloned.1.call-update) | async-done | bytes 1572880 | tf_op jit(solution)/shard_map/reduce_scatter | solution.py:41
  196.4 1.5 convert_element_type.27
  197.9 0.0 copy-start.3
  197.9 0.0 copy-start.4
  197.9 1.3 reshape.83
  199.2 10.1 %all-to-all-start.1 = ((bf16[32,3,4096]{2,1,0:T(4,128)(2,1)}), bf16[32,3,4096]{2,1,0:T(4,128)(2,1)S(1)}, u32[]{:S(2)}, u32[]{:S(2)}) async-start(bf16[32,3,4096]{2,1,0:T(4,128)(2,1)} %reshape.83), calls=%async_computation.2 | async-start | bytes 2097152 | tf_op jit(solution)/shard_map/all_to_all | solution.py:43
  209.3 0.1 and.28
  209.4 0.1 eq.39
  209.5 0.0 copy-done.3
  209.5 0.1 select_reduce_fusion
  209.6 0.1 copy.19
  209.7 0.1 broadcast_in_dim.63
  209.8 0.0 copy-done.4
  209.8 27.4 %all-to-all-done.1 = bf16[32,3,4096]{2,1,0:T(4,128)(2,1)S(1)} async-done(((bf16[32,3,4096]{2,1,0:T(4,128)(2,1)}), bf16[32,3,4096]{2,1,0:T(4,128)(2,1)S(1)}, u32[]{:S(2)}, u32[]{:S(2)}) %all-to-all-start.1) | async-done | bytes 786464 | tf_op jit(solution)/shard_map/all_to_all | solution.py:43
  237.2 0.7 reshape.84
  237.9 5.0 %fusion.1 = bf16[256,4096]{1,0:T(8,128)(2,1)} fusion(bf16[96,4096]{1,0:T(8,128)(2,1)S(1)} %reshape.84, bf16[256,4096]{1,0:T(8,128)(2,1)} %fusion.2, f32[256]{0:T(256)S(1)} %maximum_convert_fusion, f32[96]{0:T(128)S(1)} %broadcast_in_dim.63, s32[96]{0:T(128)S(1)} %eq.39, pred[96]{0:T(512)(128)(4,1)S(1)} %and.28), kind=kOutput, calls=%fused_computation.3 | convolution fusion | flops 1212227584 | bytes 4982624 | tf_op jit(solution)/shard_map/dot_general | solution.py:49
  (5 shorter events, 0.1 us)
Async XLA Ops:
  6.5 102.2 %copy-start = (bf16[1,192,4096]{2,1,0:T(8,128)(2,1)S(1)}, bf16[1,192,4096]{2,1,0:T(8,128)(2,1)}, u32[]{:S(2)}) copy-start(bf16[1,192,4096]{2,1,0:T(8,128)(2,1)} %param.15) | copy-start | bytes 4718596
  6.5 95.9 %all-gather.2.cloned.1.call-start = ((), (), s32[]{:S(2)}) async-start(), calls=%async_computation.3 | async-start | bytes 7077888 | tf_op jit(solution)/shard_map/all_gather | solution.py:36
  11.0 1.6 copy-start.1
  62.2 46.5 %copy-start.2 = (bf16[1,4096,192]{1,2,0:T(8,128)(2,1)S(1)}, bf16[1,4096,192]{1,2,0:T(8,128)(2,1)}, u32[]{:S(2)}) copy-start(bf16[1,4096,192]{1,2,0:T(8,128)(2,1)} %param.14) | copy-start | bytes 4718596
  62.2 134.2 %reduce-scatter.2.cloned.1.call-start = ((), (), s32[]{:S(2)}) async-start(), calls=%async_computation.4 | async-start | bytes 14155776 | tf_op jit(solution)/shard_map/reduce_scatter | solution.py:41
  197.9 11.6 %copy-start.3 = (f32[32,384]{1,0:T(8,128)S(1)}, f32[32,384]{1,0:T(8,128)}, u32[]{:S(2)}) copy-start(f32[32,384]{1,0:T(8,128)} %param.11) | copy-start | bytes 147460
  197.9 11.9 %copy-start.4 = (s32[256]{0:T(256)S(1)}, s32[256]{0:T(256)}, u32[]{:S(2)}) copy-start(s32[256]{0:T(256)} %param.12) | copy-start | bytes 3076
  199.2 38.0 %all-to-all-start.1 = ((bf16[32,3,4096]{2,1,0:T(4,128)(2,1)}), bf16[32,3,4096]{2,1,0:T(4,128)(2,1)S(1)}, u32[]{:S(2)}, u32[]{:S(2)}) async-start(bf16[32,3,4096]{2,1,0:T(4,128)(2,1)} %reshape.83), calls=%async_computation.2 | async-start | bytes 2097152 | tf_op jit(solution)/shard_map/all_to_all | solution.py:43
Sparse Core Ops, SparseCore 0:
  62.3 40.0 all-gather.1
  121.3 75.0 reduce-scatter.1

commit v2 on v1

v2 whole, which is shorter than its diff:
```python
import functools

import jax
import jax.numpy as jnp
from jax import lax
from jax.experimental import pallas as pl
from jax.experimental.pallas import tpu as pltpu
from jax.sharding import PartitionSpec as P

BLOCK = 128
MOST = 3
PIECE = 512
BF16 = jnp.bfloat16
F32 = jnp.float32
I32 = jnp.int32
MIB = 1024 * 1024


def mul(a, b):
    return jnp.dot(a, b, preferred_element_type=F32)


def mul_t(a, b):
    return lax.dot_general(a, b, (((1,), (1,)), ((), ())), preferred_element_type=F32)


def iota(shape, dim):
    return lax.broadcasted_iota(I32, shape, dim)


def third(q):
    return lax.shift_right_logical(q * 11, 5)


def slots_of(index, base, tok_rows, gates=None):
    cap = index.shape[1]
    local = index - base
    mine = (local >= 0) & (local < tok_rows)
    upper = (iota((cap, cap), 0) <= iota((cap, cap), 1)).astype(F32).astype(BF16)
    rank = mul(mine.astype(F32).astype(BF16), upper)
    hot = []
    for s in range(MOST):
        hit = mine & (rank == float(s + 1))
        token = jnp.sum(jnp.where(hit, local + 1, 0), axis=1, keepdims=True) - 1
        here = iota((index.shape[0], tok_rows), 1) == token
        value = 1.0
        if gates is not None:
            value = jnp.sum(jnp.where(hit, gates, 0.0), axis=1, keepdims=True)
        hot.append(jnp.where(here, value, 0.0))
    return jnp.concatenate(hot, axis=0)


def scale_columns(scales_ref, column_ref):
    scales = scales_ref[...]
    blank = jnp.zeros((BLOCK - scales.shape[0], scales.shape[1]), F32)
    column_ref[...] = jnp.transpose(jnp.concatenate([scales, blank], axis=0))


def scaled_piece(tokens, column, first):
    lane = iota(column.shape, 1)
    parts = []
    for b in range(tokens.shape[1] // BLOCK):
        part = tokens[:, b * BLOCK : (b + 1) * BLOCK].astype(F32)
        scale = jnp.sum(jnp.where(lane == first + b, column, 0.0), axis=1, keepdims=True)
        parts.append((part * scale).astype(BF16))
    return jnp.concatenate(parts, axis=1)


def put_piece(wide_ref, piece, experts, value):
    per = wide_ref.shape[1] // experts
    for s in range(MOST):
        at = pl.ds(piece * MOST + s, experts, stride=per)
        for q in range(PIECE // BLOCK):
            wide_ref[q, at, :] = value[
                s * experts : (s + 1) * experts, q * BLOCK : (q + 1) * BLOCK
            ]


def get_piece(wide_ref, piece, experts):
    per = wide_ref.shape[1] // experts
    lanes = []
    for q in range(PIECE // BLOCK):
        lanes.append(
            jnp.concatenate(
                [
                    wide_ref[q, pl.ds(piece * MOST + s, experts, stride=per), :]
                    for s in range(MOST)
                ],
                axis=0,
            )
        )
    return jnp.concatenate(lanes, axis=1).astype(BF16)


def narrow_raw(wide_ref, out_ref):
    for q in range(PIECE // BLOCK):
        out_ref[:, q * BLOCK : (q + 1) * BLOCK] = wide_ref[q].astype(BF16)


def widen_raw(raw_ref, wide_ref):
    for q in range(PIECE // BLOCK):
        wide_ref[q] = raw_ref[:, q * BLOCK : (q + 1) * BLOCK].astype(F32)


def dispatch_kernel(where_ref, index_ref, tokens_ref, scales_ref, out_ref, hot_ref, column_ref, raw_ref):
    step = pl.program_id(0)
    experts = index_ref.shape[0]
    tok_rows, chunk = tokens_ref.shape

    @pl.when(step == 0)
    def _():
        hot_ref[...] = slots_of(index_ref[...], where_ref[2], tok_rows).astype(BF16)
        scale_columns(scales_ref, column_ref)

    rows = scaled_piece(tokens_ref[...], column_ref[...], step * (chunk // BLOCK))
    picked = mul(hot_ref[...], rows)
    for k in range(chunk // PIECE):
        piece = step * (chunk // PIECE) + k
        put_piece(raw_ref, piece, experts, picked[:, k * PIECE : (k + 1) * PIECE])

    @pl.when(step == pl.num_programs(0) - 1)
    def _():
        narrow_raw(raw_ref, out_ref)


def here_mask(where_ref, index_ref, wide):
    mine = index_ref[pl.ds(where_ref[0], 1), :]
    tok_rows = where_ref[3]
    first = (iota((wide, mine.shape[1]), 0) * where_ref[4] + where_ref[1]) * tok_rows
    return ((mine >= first) & (mine < first + tok_rows)).astype(F32).astype(BF16)


def unpack_kernel(where_ref, index_ref, raw_ref, *refs):
    out_refs, wide_ref = refs[:-1], refs[-1]
    rows, half = out_refs[0].shape
    wide = index_ref.shape[0]
    widen_raw(raw_ref, wide_ref)
    for j in range(2 * half // PIECE):
        at = j * PIECE % half
        out_refs[j * PIECE // half][:, at : at + PIECE] = get_piece(wide_ref, j, wide)


def expert_kernel(blocks, steps, *refs):
    i = pl.program_id(0)
    xs, refs = refs[: 2 * blocks], refs[2 * blocks :]
    ws, downs, refs = refs[:8], refs[8:10], refs[10:]
    outs, accs = refs[: 2 * blocks], refs[2 * blocks :]
    left = jnp.concatenate([x[...] for x in xs[0::2]], axis=0)
    right = jnp.concatenate([x[...] for x in xs[1::2]], axis=0)

    @pl.when(i == 0)
    def _():
        for acc in accs:
            acc[...] = jnp.zeros_like(acc)

    for k, acc in enumerate(accs):
        acc[...] += mul_t(left, ws[2 * k][...]) + mul_t(right, ws[2 * k + 1][...])

    @pl.when(i == steps - 1)
    def _():
        hidden = []
        for gate, upper in ((accs[0], accs[1]), (accs[2], accs[3])):
            v = gate[...]
            hidden.append((v / (1.0 + jnp.exp(-v)) * upper[...]).astype(BF16))
        rows, half = outs[0].shape
        for c in range(2 * half // PIECE):
            cols = slice(c * PIECE, (c + 1) * PIECE)
            part = mul(hidden[0], downs[0][:, cols]) + mul(hidden[1], downs[1][:, cols])
            at = c * PIECE % half
            for b in range(blocks):
                out = outs[2 * b + c * PIECE // half]
                value = part[b * rows : (b + 1) * rows]
                out[:, at : at + PIECE] = value.astype(out.dtype)


def expert(xs, own, sibling, out_types):
    rows, half = xs[0][0].shape
    blocks = len(xs)
    hid = own[0].shape[0]
    width = 2 * half
    steps = 4
    deep = half // steps
    x_specs, w_specs, args, w_args = [], [], [], []
    for pair in xs:
        for x in pair:
            x_specs.append(pl.BlockSpec((rows, deep), lambda i: (0, i)))
            args.append(x)
    for w in (own[0], own[1], sibling[0], sibling[1]):
        w_specs.append(pl.BlockSpec((hid, deep), lambda i: (0, i)))
        w_specs.append(pl.BlockSpec((hid, deep), lambda i: (0, i + steps)))
        w_args += [w, w]
    d_specs = [pl.BlockSpec((hid, width), lambda i: (0, 0))] * 2
    return pl.pallas_call(
        functools.partial(expert_kernel, blocks, steps),
        grid=(steps,),
        in_specs=x_specs + w_specs + d_specs,
        out_specs=[pl.BlockSpec((rows, half), lambda i: (0, 0))] * (2 * blocks),
        out_shape=[jax.ShapeDtypeStruct((rows, half), t) for t in out_types],
        scratch_shapes=[pltpu.VMEM((rows * blocks, hid), F32)] * 4,
        compiler_params=pltpu.CompilerParams(vmem_limit_bytes=32 * MIB),
        cost_estimate=pl.CostEstimate(
            flops=2 * blocks * rows * hid * width * 6,
            bytes_accessed=hid * width * 12 + blocks * rows * width * 6,
            transcendentals=blocks * rows * hid * 2,
        ),
    )(*args, *w_args, own[2], sibling[2])


def pack_kernel(where_ref, index_ref, *refs):
    parts, out_ref, raw_ref = refs[:-2], refs[-2], refs[-1]
    rows, half = parts[0].shape
    wide = index_ref.shape[0]
    for j in range(2 * half // PIECE):
        at = j * PIECE % half
        summed = sum(p[:, at : at + PIECE].astype(F32) for p in parts[j * PIECE // half :: 2])
        put_piece(raw_ref, j, wide, summed)
    narrow_raw(raw_ref, out_ref)


def combine_kernel(
    where_ref, index_ref, gates_ref, counts_ref, tokens_ref, scales_ref, raw_ref, out_ref, weight_ref, column_ref, wide_ref
):
    step = pl.program_id(0)
    experts = index_ref.shape[0]
    tok_rows, chunk = tokens_ref.shape

    @pl.when(step == 0)
    def _():
        weight = slots_of(index_ref[...], where_ref[2], tok_rows, gates_ref[...])
        weight = weight / jnp.maximum(counts_ref[...], 1).astype(F32)
        high = weight.astype(BF16).astype(F32)
        both = jnp.concatenate([high, weight - high], axis=0)
        weight_ref[...] = jnp.transpose(both).astype(BF16)
        scale_columns(scales_ref, column_ref)
        widen_raw(raw_ref, wide_ref)

    pieces = chunk // PIECE
    got = [get_piece(wide_ref, step * pieces + k, experts) for k in range(pieces)]
    got = jnp.concatenate(got, axis=1)
    branch = mul(weight_ref[...], jnp.concatenate([got, got], axis=0))
    rows = scaled_piece(tokens_ref[...], column_ref[...], step * (chunk // BLOCK))
    out_ref[...] = (rows.astype(F32) + branch).astype(BF16)


def local(
    tokens, block_scales, pick_index, pick_gates, pick_counts, gate_weight, up_weight, down_weight
):
    tok_rows, width = tokens.shape
    n_wide = lax.axis_size("wide")
    n_narrow = lax.axis_size("narrow")
    at_wide = lax.axis_index("wide")
    at_narrow = lax.axis_index("narrow")
    other_core = [(i, i ^ 1) for i in range(n_narrow)]
    base = (at_wide * n_narrow + at_narrow) * tok_rows
    where = jnp.stack(
        [jnp.asarray(v, I32) for v in (at_wide, at_narrow, base, tok_rows, n_narrow)]
    )
    pieces = width // PIECE
    per = MOST * pieces
    total = n_wide * per
    scales = block_scales.T
    chunk = 2 * PIECE
    steps = width // chunk
    smem = pl.BlockSpec(memory_space=pltpu.SMEM)
    vmem = pl.BlockSpec(memory_space=pltpu.VMEM)

    def whole(a):
        return pl.BlockSpec(a.shape, lambda j: (0,) * a.ndim)

    def along_y(x, step):
        return lax.ppermute(
            x, "narrow", [(i, (i + 2 * step) % n_narrow) for i in range(n_narrow)]
        )

    own = (gate_weight[0].T, up_weight[0].T, down_weight[0])
    sibling = tuple(lax.ppermute(v, "narrow", other_core) for v in own)

    tokens_spec = pl.BlockSpec((tok_rows, chunk), lambda j: (0, j))
    column = pltpu.VMEM((tok_rows, BLOCK), F32)
    raw_f32 = pltpu.VMEM((PIECE // BLOCK, total, BLOCK), F32)
    raw_shape = jax.ShapeDtypeStruct((total, PIECE), BF16)
    outgoing = pl.pallas_call(
        dispatch_kernel,
        grid=(steps,),
        in_specs=[smem, whole(pick_index), tokens_spec, whole(scales)],
        out_specs=pl.BlockSpec((total, PIECE), lambda j: (0, 0)),
        out_shape=raw_shape,
        scratch_shapes=[pltpu.VMEM((MOST * n_wide, tok_rows), BF16), column, raw_f32],
        compiler_params=pltpu.CompilerParams(vmem_limit_bytes=56 * MIB),
    )(where, pick_index, tokens, scales)

    def exchange(raw):
        raw = raw.reshape(n_wide, per, PIECE)
        raw = lax.all_to_all(raw, "wide", split_axis=0, concat_axis=0, tiled=True)
        return raw.reshape(total, PIECE)

    arrived = exchange(outgoing)
    rows = n_wide * MOST
    half_shape = jax.ShapeDtypeStruct((rows, width // 2), BF16)
    x0 = pl.pallas_call(
        unpack_kernel,
        in_specs=[smem, vmem, vmem],
        out_specs=[vmem, vmem],
        out_shape=[half_shape, half_shape],
        scratch_shapes=[raw_f32],
        compiler_params=pltpu.CompilerParams(vmem_limit_bytes=24 * MIB),
    )(where, pick_index, arrived)

    xm = [None, None]
    xp = [None, None]
    xm[0] = along_y(x0[0], 1)
    xp[1] = along_y(x0[1], -1)
    xm[1] = along_y(x0[1], 1)
    xp[0] = along_y(x0[0], -1)
    x2 = (along_y(xm[0], 1), along_y(xp[1], -1))

    p0 = expert([x0], own, sibling, (F32, F32))
    pp_a, pp_b, pm_a, pm_b = expert([xp, xm], own, sibling, (F32, BF16, BF16, F32))
    p2 = expert([x2], own, sibling, (BF16, BF16))
    from_m = along_y(p2[0], 1)
    from_p = along_y(p2[1], -1)
    got_mb = along_y(pp_b, 1)
    got_pa = along_y(pm_a, -1)
    got_ma = along_y((pp_a + from_m.astype(F32)).astype(BF16), 1)
    got_pb = along_y((pm_b + from_p.astype(F32)).astype(BF16), -1)
    packed = pl.pallas_call(
        pack_kernel,
        in_specs=[smem] + [vmem] * 7,
        out_specs=vmem,
        out_shape=raw_shape,
        scratch_shapes=[raw_f32],
        compiler_params=pltpu.CompilerParams(vmem_limit_bytes=32 * MIB),
    )(where, pick_index, p0[0], p0[1], got_ma, got_mb, got_pa, got_pb)
    returned = exchange(packed)
    counts = pick_counts.reshape(1, tok_rows)
    return pl.pallas_call(
        combine_kernel,
        grid=(steps,),
        in_specs=[
            smem,
            whole(pick_index),
            whole(pick_gates),
            whole(counts),
            tokens_spec,
            whole(scales),
            whole(returned),
        ],
        out_specs=tokens_spec,
        out_shape=jax.ShapeDtypeStruct((tok_rows, width), BF16),
        scratch_shapes=[pltpu.VMEM((tok_rows, 2 * MOST * n_wide), BF16), column, raw_f32],
        compiler_params=pltpu.CompilerParams(vmem_limit_bytes=24 * MIB),
    )(where, pick_index, pick_gates, counts, tokens, scales, returned)


def solution(mesh):
    return jax.shard_map(
        local,
        mesh=mesh,
        in_specs=(
            P(("wide", "narrow"), None),
            P(("wide", "narrow"), None),
            P(),
            P(),
            P(("wide", "narrow")),
            P("wide", None, "narrow"),
            P("wide", None, "narrow"),
            P("wide", "narrow", None),
        ),
        out_specs=P(("wide", "narrow"), None),
        check_vma=False,
    )
```

time: 250 us -> 138 us (0.55)
  waiting for transfers between devices: 143 us -> 50.7 us
  Pallas kernels: 0 us -> 30 us
  matrix products: 23.8 us -> 0 us
  starting transfers between devices: 10.3 us -> 30.5 us
  blocking collectives: 39.5 us -> 24.1 us
  between operations: 13.5 us -> 0.18 us
  other arithmetic: 9.12 us -> 0.15 us
  local copies, waits for them, and re-layouts: 11 us -> 2.05 us
    reduce_scatter x1 -> x0, waiting for transfers between devices: 75.2 us -> none  [local(): lax.psum_scatter(partial_out, 'narrow', scatter_dimension=0, tiled=True)]
    all_gather x1 -> x0, waiting for transfers between devices: 40 us -> none  [local(): flat_rows = lax.all_gather(arrived, 'narrow', axis=0, tiled=True)]
    pallas_call x0 -> x7, Pallas kernels: none -> 30 us  [the longest x3 18.1 us: expert(): pl.pallas_call(functools.partial(expert_kernel, blocks, steps), grid=(ste...]
    ppermute x0 -> x15, waiting for transfers between devices: none -> 28.2 us  [the longest x12 28.2 us: along_y(): lax.ppermute(x, 'narrow', [(i, (i + 2 * step) % n_narrow) for i in range(...]
    dot_general x3 -> x0, matrix products: 23.8 us -> none  [the longest x1 12.5 us: local(): jnp.dot(hidden, down_weight[0], preferred_element_type=jnp.float32)]
    ppermute x0 -> x15, starting transfers between devices: none -> 19.2 us  [the longest x12 18.5 us: along_y(): lax.ppermute(x, 'narrow', [(i, (i + 2 * step) % n_narrow) for i in range(...]
    all_to_all x1, blocking collectives: 39.5 us -> 24.1 us  [exchange(): raw = lax.all_to_all(raw, 'wide', split_axis=0, concat_axis=0, tiled=True)]
    convert_element_type x3 -> x2, other arithmetic: 5.39 us -> 0.15 us  [the longest x1 0.07 us: local(): got_pb = along_y((pm_b + from_p.astype(F32)).astype(BF16), -1)]
  transfers between devices with their start and end apart: 3 -> 16, of which waited for: 3 -> 5; matrix products, arithmetic and copies ran while one was open for 0% -> 0% of each run, Pallas kernels for 0% -> 14%
where the time goes in v2:
time: 138 us
  waiting for transfers between devices  50.7 us (37%)
  starting transfers between devices  30.5 us (22%)
  Pallas kernels  30 us (22%)
  blocking collectives  24.1 us (17%)
  local copies, waits for them, and re-layouts  2.05 us (1%)
    ppermute x12, waiting for transfers between devices, along_y(): lax.ppermute(x, 'narrow', [(i, (i + 2 * step) % n_narrow) for i in range(...  28.2 us
    all_to_all x1, blocking collectives, exchange(): raw = lax.all_to_all(raw, 'wide', split_axis=0, concat_axis=0, tiled=True)  24.1 us
    all_to_all x1, waiting for transfers between devices, exchange(): raw = lax.all_to_all(raw, 'wide', split_axis=0, concat_axis=0, tiled=True)  22.5 us
    ppermute x12, starting transfers between devices, along_y(): lax.ppermute(x, 'narrow', [(i, (i + 2 * step) % n_narrow) for i in range(...  18.5 us
    pallas_call x3, Pallas kernels, expert(): pl.pallas_call(functools.partial(expert_kernel, blocks, steps), grid=(ste...  18.1 us
    all_to_all x1, starting transfers between devices, exchange(): raw = lax.all_to_all(raw, 'wide', split_axis=0, concat_axis=0, tiled=True)  11.2 us
    pallas_call x1, Pallas kernels, local(): pl.pallas_call(dispatch_kernel, grid=(steps,), in_specs=[smem, whole(pick...  5.23 us
    pallas_call x1, Pallas kernels, local(): pl.pallas_call(combine_kernel, grid=(steps,), in_specs=[smem, whole(pick_...  3.97 us
  transfers between devices with their start and end apart: 16, of which 5 were waited for; matrix products, arithmetic and copies ran while one was open for 0% of the time, Pallas kernels for 14%

profile of v2, /device:TPU:32, one launch (start us, length us, event | category | flops | bytes accessed | tf_op | source)
XLA Modules:
  0.0 137.6 jit_solution(528353462186897218)
XLA Ops:
  0.0 0.6 stack.15.where_ref
  0.6 0.0 copy-start
  0.6 0.0 copy-start.1
  0.6 0.0 copy-start.4
  0.6 0.0 copy-start.7
  0.6 5.2 %shard_map.82 = bf16[768,512]{1,0:T(8,128)(2,1)} custom-call(s32[5]{0:T(128)} %stack.15.where_ref, s32[32,384]{1,0:T(8,128)} %index_ref.7, bf16[256,4096]{1,0:T(8,128)(2,1)} %tokens_ref.3, f32[32,256]{1,0:T(8,128)} %bitcast.36), custom_call_target="tpu_custom_call" | custom-call | tf_op jit(solution)/shard_map/pallas_call | solution.py:282
  5.8 11.2 %all-to-all-start = ((bf16[32,24,512]{2,1,0:T(8,128)(2,1)}), bf16[32,24,512]{2,1,0:T(8,128)(2,1)}, u32[]{:S(2)}, u32[]{:S(2)}) async-start(bf16[32,24,512]{2,1,0:T(8,128)(2,1)} %bitcast.39), calls=%async_computation | async-start | bytes 1572864 | tf_op jit(solution)/shard_map/all_to_all | solution.py:294
  17.1 0.0 copy-done
  17.1 0.1 collective-permute-start
  17.2 0.0 copy-done.1
  17.2 0.5 collective-permute-start.1
  17.7 0.1 collective-permute-start.2
  17.8 22.5 %all-to-all-done = bf16[32,24,512]{2,1,0:T(8,128)(2,1)} async-done(((bf16[32,24,512]{2,1,0:T(8,128)(2,1)}), bf16[32,24,512]{2,1,0:T(8,128)(2,1)}, u32[]{:S(2)}, u32[]{:S(2)}) %all-to-all-start) | async-done | bytes 786464 | tf_op jit(solution)/shard_map/all_to_all | solution.py:294
  40.3 0.0 copy-done.4
  40.3 0.0 copy-done.7
  40.3 1.5 %shard_map.83 = (bf16[96,2048]{1,0:T(8,128)(2,1)S(1)}, bf16[96,2048]{1,0:T(8,128)(2,1)S(1)}) custom-call(s32[5]{0:T(128)S(1)} %copy-done.7, s32[32,384]{1,0:T(8,128)S(1)} %copy-done.4, bf16[768,512]{1,0:T(8,128)(2,1)} %bitcast.6.raw_ref), custom_call_target="tpu_custom_call" | custom-call | tf_op jit(solution)/shard_map/pallas_call | solution.py:300
  41.8 1.7 %collective-permute-start.5 = (bf16[96,2048]{1,0:T(8,128)(2,1)S(1)}, bf16[96,2048]{1,0:T(8,128)(2,1)S(1)}, u32[]{:S(2)}, u32[]{:S(2)}) collective-permute-start(bf16[96,2048]{1,0:T(8,128)(2,1)S(1)} %get-tuple-element.15.refs_0_), channel_id=1, source_target_pairs={{0,2},{1,3},{2,4},{3,5},{4,6},{5,7},{6,0},{7,1},{8,10},{9,11},{10,... | collective-permute-start | bytes 1179656 | tf_op jit(solution)/shard_map/ppermute | solution.py:271
  43.5 1.7 %collective-permute-start.4 = (bf16[96,2048]{1,0:T(8,128)(2,1)S(1)}, bf16[96,2048]{1,0:T(8,128)(2,1)S(1)}, u32[]{:S(2)}, u32[]{:S(2)}) collective-permute-start(bf16[96,2048]{1,0:T(8,128)(2,1)S(1)} %get-tuple-element.16.refs_1_), channel_id=1, source_target_pairs={{0,6},{1,7},{2,0},{3,1},{4,2},{5,3},{6,4},{7,5},{8,14},{9,15},{10,... | collective-permute-start | bytes 1179656 | tf_op jit(solution)/shard_map/ppermute | solution.py:271
  45.1 6.6 %collective-permute-done.5.refs_2_ = bf16[96,2048]{1,0:T(8,128)(2,1)S(1)} collective-permute-done((bf16[96,2048]{1,0:T(8,128)(2,1)S(1)}, bf16[96,2048]{1,0:T(8,128)(2,1)S(1)}, u32[]{:S(2)}, u32[]{:S(2)}) %collective-permute-start.5) | collective-permute-done | bytes 393248 | tf_op jit(solution)/shard_map/ppermute | solution.py:271
  51.8 0.9 collective-permute-start.7
  52.7 0.0 collective-permute-done.4.refs_1_
  52.7 2.3 %collective-permute-start.8 = (bf16[96,2048]{1,0:T(8,128)(2,1)S(1)}, bf16[96,2048]{1,0:T(8,128)(2,1)S(1)}, u32[]{:S(2)}, u32[]{:S(2)}) collective-permute-start(bf16[96,2048]{1,0:T(8,128)(2,1)S(1)} %collective-permute-done.4.refs_1_), channel_id=1, source_target_pairs={{0,6},{1,7},{2,0},{3,1},{4,2},{5,3},{6,4},{7,5},{8,14},{9,15},{10,... | collective-permute-start | bytes 1179656 | tf_op jit(solution)/shard_map/ppermute | solution.py:271
  55.0 0.0 collective-permute-done.refs_6_.refs_7_.refs_8_.refs_9_
  55.0 1.2 collective-permute-start.3
  56.2 0.0 collective-permute-done.1.refs_8_.refs_9_.refs_10_.refs_11_
  56.2 0.8 collective-permute-start.6
  57.0 0.0 collective-permute-done.2.refs_11_.refs_13_
  57.1 7.9 %collective-permute-done.7.refs_0_ = bf16[96,2048]{1,0:T(8,128)(2,1)S(1)} collective-permute-done((bf16[96,2048]{1,0:T(8,128)(2,1)S(1)}, bf16[96,2048]{1,0:T(8,128)(2,1)S(1)}, u32[]{:S(2)}, u32[]{:S(2)}) %collective-permute-start.7) | collective-permute-done | bytes 393248 | tf_op jit(solution)/shard_map/ppermute | solution.py:271
  64.9 0.0 collective-permute-done.8.refs_1_
  65.0 0.0 copy-start.2
  65.0 1.4 %copy-done.2 = bf16[1,192,4096]{2,1,0:T(8,128)(2,1)S(1)} copy-done((bf16[1,192,4096]{2,1,0:T(8,128)(2,1)S(1)}, bf16[1,192,4096]{2,1,0:T(8,128)(2,1)}, u32[]{:S(2)}) %copy-start.2) | copy-done | bytes 1572888
  66.4 5.9 %shard_map.86 = (bf16[96,2048]{1,0:T(8,128)(2,1)S(1)}, bf16[96,2048]{1,0:T(8,128)(2,1)S(1)}) custom-call(bf16[96,2048]{1,0:T(8,128)(2,1)S(1)} %collective-permute-done.7.refs_0_, bf16[96,2048]{1,0:T(8,128)(2,1)S(1)} %collective-permute-done.8.refs_1_, bf16[192,4096]{1,0:T(8,128)(2,1)S(1)} %bitcast.17, bf16[192,4096]{1,0:T(8,128)(2,1)S(1)} %bitcast.18, ...), custom_call_target="tpu_custom_call" | custom-call | flops 905969664 | bytes 11796480 | tf_op jit(solution)/shard_map/pallas_call | solution.py:193
  72.2 3.0 %collective-permute-start.13 = (bf16[96,2048]{1,0:T(8,128)(2,1)S(1)}, bf16[96,2048]{1,0:T(8,128)(2,1)S(1)}, u32[]{:S(2)}, u32[]{:S(2)}) collective-permute-start(bf16[96,2048]{1,0:T(8,128)(2,1)S(1)} %get-tuple-element.24), channel_id=1, source_target_pairs={{0,6},{1,7},{2,0},{3,1},{4,2},{5,3},{6,4},{7,5},{8,14},{9,15},{10,... | collective-permute-start | bytes 1179656 | tf_op jit(solution)/shard_map/ppermute | solution.py:271
  75.3 0.0 collective-permute-done.3.refs_0_
  75.3 0.0 collective-permute-done.6.refs_3_
  75.3 6.3 %shard_map.85 = (f32[96,2048]{1,0:T(8,128)S(1)}, bf16[96,2048]{1,0:T(8,128)(2,1)S(1)}, bf16[96,2048]{1,0:T(8,128)(2,1)S(1)}, f32[96,2048]{1,0:T(8,128)S(1)}) custom-call(bf16[96,2048]{1,0:T(8,128)(2,1)S(1)} %collective-permute-done.3.refs_0_, bf16[96,2048]{1,0:T(8,128)(2,1)S(1)} %collective-permute-done.4.refs_1_, ...), custom_call_target="tpu_custom_call" | custom-call | flops 1811939328 | bytes 14155776 | tf_op jit(solution)/shard_map/pallas_call | solution.py:193
  81.6 0.1 collective-permute-start.11
  81.7 3.2 %collective-permute-start.12 = (bf16[96,2048]{1,0:T(8,128)(2,1)S(1)}, bf16[96,2048]{1,0:T(8,128)(2,1)S(1)}, u32[]{:S(2)}, u32[]{:S(2)}) collective-permute-start(bf16[96,2048]{1,0:T(8,128)(2,1)S(1)} %get-tuple-element.22), channel_id=1, source_target_pairs={{0,6},{1,7},{2,0},{3,1},{4,2},{5,3},{6,4},{7,5},{8,14},{9,15},{10,... | collective-permute-start | bytes 1179656 | tf_op jit(solution)/shard_map/ppermute | solution.py:271
  84.9 0.0 collective-permute-start.9
  84.9 0.0 collective-permute-done.13
  84.9 0.1 add_convert_fusion
  85.0 3.5 %collective-permute-start.14 = (bf16[96,2048]{1,0:T(8,128)(2,1)S(1)}, bf16[96,2048]{1,0:T(8,128)(2,1)S(1)}, u32[]{:S(2)}, u32[]{:S(2)}) collective-permute-start(bf16[96,2048]{1,0:T(8,128)(2,1)S(1)} %add_convert_fusion), channel_id=1, source_target_pairs={{0,6},{1,7},{2,0},{3,1},{4,2},{5,3},{6,4},{7,5},{8,14},{9,15},{10,... | collective-permute-start | bytes 1179656 | tf_op jit(solution)/shard_map/ppermute | solution.py:271
  88.5 10.6 %collective-permute-done.9 = bf16[96,2048]{1,0:T(8,128)(2,1)S(1)} collective-permute-done((bf16[96,2048]{1,0:T(8,128)(2,1)S(1)}, bf16[96,2048]{1,0:T(8,128)(2,1)S(1)}, u32[]{:S(2)}, u32[]{:S(2)}) %collective-permute-start.9) | collective-permute-done | bytes 393248 | tf_op jit(solution)/shard_map/ppermute | solution.py:271
  99.1 0.1 add_convert_fusion.1
  99.2 0.1 collective-permute-start.10
  99.3 5.9 %shard_map.84 = (f32[96,2048]{1,0:T(8,128)S(1)}, f32[96,2048]{1,0:T(8,128)S(1)}) custom-call(bf16[96,2048]{1,0:T(8,128)(2,1)S(1)} %get-tuple-element.15.refs_0_, bf16[96,2048]{1,0:T(8,128)(2,1)S(1)} %get-tuple-element.16.refs_1_, bf16[192,4096]{1,0:T(8,128)(2,1)S(1)} %bitcast.21, bf16[192,4096]{1,0:T(8,128)(2,1)S(1)} %bitcast.22, ...), custom_call_target="tpu_custom_call" | custom-call | flops 905969664 | bytes 11796480 | tf_op jit(solution)/shard_map/pallas_call | solution.py:193
  105.2 0.0 collective-permute-done.11.refs_3_
  105.2 0.0 collective-permute-done.12.refs_4_
  105.2 0.0 collective-permute-done.14.refs_5_
  105.2 3.0 %collective-permute-done.10.refs_2_ = bf16[96,2048]{1,0:T(8,128)(2,1)S(1)} collective-permute-done((bf16[96,2048]{1,0:T(8,128)(2,1)S(1)}, bf16[96,2048]{1,0:T(8,128)(2,1)S(1)}, u32[]{:S(2)}, u32[]{:S(2)}) %collective-permute-start.10) | collective-permute-done | bytes 393248 | tf_op jit(solution)/shard_map/ppermute | solution.py:271
  108.2 0.0 copy-start.3
  108.2 1.2 shard_map.87
  109.4 0.0 copy-start.5
  109.5 0.0 copy-start.6
  109.5 0.0 copy-start.8
  109.5 24.1 %all_to_all.10 = bf16[32,24,512]{2,1,0:T(8,128)(2,1)S(1)} all-to-all(bf16[32,24,512]{2,1,0:T(8,128)(2,1)S(1)} %bitcast.34), channel_id=1, replica_groups=mesh['wide'=32,'narrow'=8] {'wide'}, dimensions={0} | all-to-all | bytes 1572864 | tf_op jit(solution)/shard_map/all_to_all | solution.py:294
  133.6 0.0 copy-done.3
  133.6 0.0 copy-done.5
  133.6 0.0 copy-done.6
  133.6 0.0 copy-done.8
  133.6 4.0 %shard_map.88 = bf16[256,4096]{1,0:T(8,128)(2,1)} custom-call(s32[5]{0:T(128)S(1)} %copy-done.7, s32[32,384]{1,0:T(8,128)S(1)} %copy-done.4, f32[32,384]{1,0:T(8,128)S(1)} %copy-done.6, s32[1,256]{1,0:T(1,128)S(1)} %bitcast.38, bf16[256,4096]{1,0:T(8,128)(2,1)S(1)} %copy-done.3, f32[32,256]{1,0:T(8,128)S(1)} %bitcast.37, bf16[768,512]{1,0:T(8,128)(2,1)S(1)} %bitcast.35), custom_call_target="tpu_custom_call" | custom-call | tf_op jit(solution)/shard_map/pallas_call | solution.py:336
Async XLA Ops:
  0.6 16.5 %copy-start = (bf16[1,4096,192]{1,2,0:T(8,128)(2,1)S(1)}, bf16[1,4096,192]{1,2,0:T(8,128)(2,1)}, u32[]{:S(2)}) copy-start(bf16[1,4096,192]{1,2,0:T(8,128)(2,1)} %param.13) | copy-start | bytes 4718596
  0.6 16.6 %copy-start.1 = (bf16[1,4096,192]{1,2,0:T(8,128)(2,1)S(1)}, bf16[1,4096,192]{1,2,0:T(8,128)(2,1)}, u32[]{:S(2)}) copy-start(bf16[1,4096,192]{1,2,0:T(8,128)(2,1)} %param.14) | copy-start | bytes 4718596
  0.6 39.7 %copy-start.4 = (s32[32,384]{1,0:T(8,128)S(1)}, s32[32,384]{1,0:T(8,128)}, u32[]{:S(2)}) copy-start(s32[32,384]{1,0:T(8,128)} %index_ref.7) | copy-start | bytes 147460
  0.6 39.7 %copy-start.7 = (s32[5]{0:T(128)S(1)}, s32[5]{0:T(128)}, u32[]{:S(2)}) copy-start(s32[5]{0:T(128)} %stack.15.where_ref) | copy-start | bytes 64
  5.8 34.5 %all-to-all-start = ((bf16[32,24,512]{2,1,0:T(8,128)(2,1)}), bf16[32,24,512]{2,1,0:T(8,128)(2,1)}, u32[]{:S(2)}, u32[]{:S(2)}) async-start(bf16[32,24,512]{2,1,0:T(8,128)(2,1)} %bitcast.39), calls=%async_computation | async-start | bytes 1572864 | tf_op jit(solution)/shard_map/all_to_all | solution.py:294
  17.1 37.9 %collective-permute-start = (bf16[192,4096]{1,0:T(8,128)(2,1)S(1)}, bf16[192,4096]{1,0:T(8,128)(2,1)}, u32[]{:S(2)}, u32[]{:S(2)}) collective-permute-start(bf16[192,4096]{1,0:T(8,128)(2,1)S(1)} %bitcast.16), channel_id=1, source_target_pairs={{0,1},{1,0},{2,3},{3,2},{4,5},{5,4},{6,7},{7,6},{8,9},{9,8},{10,11... | collective-permute-start | bytes 4718600 | tf_op jit(solution)/shard_map/ppermute | solution.py:276
  17.2 39.0 %collective-permute-start.1 = (bf16[192,4096]{1,0:T(8,128)(2,1)S(1)}, bf16[192,4096]{1,0:T(8,128)(2,1)}, u32[]{:S(2)}, u32[]{:S(2)}) collective-permute-start(bf16[192,4096]{1,0:T(8,128)(2,1)S(1)} %bitcast.23), channel_id=1, source_target_pairs={{0,1},{1,0},{2,3},{3,2},{4,5},{5,4},{6,7},{7,6},{8,9},{9,8},{10,11... | collective-permute-start | bytes 4718600 | tf_op jit(solution)/shard_map/ppermute | solution.py:276
  17.7 39.4 %collective-permute-start.2 = (bf16[192,4096]{1,0:T(8,128)(2,1)}, bf16[192,4096]{1,0:T(8,128)(2,1)}, u32[]{:S(2)}, u32[]{:S(2)}) collective-permute-start(bf16[192,4096]{1,0:T(8,128)(2,1)} %bitcast.30), channel_id=1, source_target_pairs={{0,1},{1,0},{2,3},{3,2},{4,5},{5,4},{6,7},{7,6},{8,9},{9,8},{10,11... | collective-permute-start | bytes 4718600 | tf_op jit(solution)/shard_map/ppermute | solution.py:276
  41.8 10.0 %collective-permute-start.5 = (bf16[96,2048]{1,0:T(8,128)(2,1)S(1)}, bf16[96,2048]{1,0:T(8,128)(2,1)S(1)}, u32[]{:S(2)}, u32[]{:S(2)}) collective-permute-start(bf16[96,2048]{1,0:T(8,128)(2,1)S(1)} %get-tuple-element.15.refs_0_), channel_id=1, source_target_pairs={{0,2},{1,3},{2,4},{3,5},{4,6},{5,7},{6,0},{7,1},{8,10},{9,11},{10,... | collective-permute-start | bytes 1179656 | tf_op jit(solution)/shard_map/ppermute | solution.py:271
  43.5 9.2 %collective-permute-start.4 = (bf16[96,2048]{1,0:T(8,128)(2,1)S(1)}, bf16[96,2048]{1,0:T(8,128)(2,1)S(1)}, u32[]{:S(2)}, u32[]{:S(2)}) collective-permute-start(bf16[96,2048]{1,0:T(8,128)(2,1)S(1)} %get-tuple-element.16.refs_1_), channel_id=1, source_target_pairs={{0,6},{1,7},{2,0},{3,1},{4,2},{5,3},{6,4},{7,5},{8,14},{9,15},{10,... | collective-permute-start | bytes 1179656 | tf_op jit(solution)/shard_map/ppermute | solution.py:271
  51.8 13.2 %collective-permute-start.7 = (bf16[96,2048]{1,0:T(8,128)(2,1)S(1)}, bf16[96,2048]{1,0:T(8,128)(2,1)S(1)}, u32[]{:S(2)}, u32[]{:S(2)}) collective-permute-start(bf16[96,2048]{1,0:T(8,128)(2,1)S(1)} %collective-permute-done.5.refs_2_), channel_id=1, source_target_pairs={{0,2},{1,3},{2,4},{3,5},{4,6},{5,7},{6,0},{7,1},{8,10},{9,11},{10,... | collective-permute-start | bytes 1179656 | tf_op jit(solution)/shard_map/ppermute | solution.py:271
  52.7 12.2 %collective-permute-start.8 = (bf16[96,2048]{1,0:T(8,128)(2,1)S(1)}, bf16[96,2048]{1,0:T(8,128)(2,1)S(1)}, u32[]{:S(2)}, u32[]{:S(2)}) collective-permute-start(bf16[96,2048]{1,0:T(8,128)(2,1)S(1)} %collective-permute-done.4.refs_1_), channel_id=1, source_target_pairs={{0,6},{1,7},{2,0},{3,1},{4,2},{5,3},{6,4},{7,5},{8,14},{9,15},{10,... | collective-permute-start | bytes 1179656 | tf_op jit(solution)/shard_map/ppermute | solution.py:271
  55.0 20.2 %collective-permute-start.3 = (bf16[96,2048]{1,0:T(8,128)(2,1)S(1)}, bf16[96,2048]{1,0:T(8,128)(2,1)S(1)}, u32[]{:S(2)}, u32[]{:S(2)}) collective-permute-start(bf16[96,2048]{1,0:T(8,128)(2,1)S(1)} %get-tuple-element.15.refs_0_), channel_id=1, source_target_pairs={{0,6},{1,7},{2,0},{3,1},{4,2},{5,3},{6,4},{7,5},{8,14},{9,15},{10,... | collective-permute-start | bytes 1179656 | tf_op jit(solution)/shard_map/ppermute | solution.py:271
  56.2 19.0 %collective-permute-start.6 = (bf16[96,2048]{1,0:T(8,128)(2,1)S(1)}, bf16[96,2048]{1,0:T(8,128)(2,1)S(1)}, u32[]{:S(2)}, u32[]{:S(2)}) collective-permute-start(bf16[96,2048]{1,0:T(8,128)(2,1)S(1)} %get-tuple-element.16.refs_1_), channel_id=1, source_target_pairs={{0,2},{1,3},{2,4},{3,5},{4,6},{5,7},{6,0},{7,1},{8,10},{9,11},{10,... | collective-permute-start | bytes 1179656 | tf_op jit(solution)/shard_map/ppermute | solution.py:271
  65.0 1.4 %copy-start.2 = (bf16[1,192,4096]{2,1,0:T(8,128)(2,1)S(1)}, bf16[1,192,4096]{2,1,0:T(8,128)(2,1)}, u32[]{:S(2)}) copy-start(bf16[1,192,4096]{2,1,0:T(8,128)(2,1)} %param.15) | copy-start | bytes 4718596
  72.2 12.7 %collective-permute-start.13 = (bf16[96,2048]{1,0:T(8,128)(2,1)S(1)}, bf16[96,2048]{1,0:T(8,128)(2,1)S(1)}, u32[]{:S(2)}, u32[]{:S(2)}) collective-permute-start(bf16[96,2048]{1,0:T(8,128)(2,1)S(1)} %get-tuple-element.24), channel_id=1, source_target_pairs={{0,6},{1,7},{2,0},{3,1},{4,2},{5,3},{6,4},{7,5},{8,14},{9,15},{10,... | collective-permute-start | bytes 1179656 | tf_op jit(solution)/shard_map/ppermute | solution.py:271
  81.6 23.6 %collective-permute-start.11 = (bf16[96,2048]{1,0:T(8,128)(2,1)S(1)}, bf16[96,2048]{1,0:T(8,128)(2,1)S(1)}, u32[]{:S(2)}, u32[]{:S(2)}) collective-permute-start(bf16[96,2048]{1,0:T(8,128)(2,1)S(1)} %get-tuple-element.21), channel_id=1, source_target_pairs={{0,2},{1,3},{2,4},{3,5},{4,6},{5,7},{6,0},{7,1},{8,10},{9,11},{10,... | collective-permute-start | bytes 1179656 | tf_op jit(solution)/shard_map/ppermute | solution.py:271
  81.7 23.5 %collective-permute-start.12 = (bf16[96,2048]{1,0:T(8,128)(2,1)S(1)}, bf16[96,2048]{1,0:T(8,128)(2,1)S(1)}, u32[]{:S(2)}, u32[]{:S(2)}) collective-permute-start(bf16[96,2048]{1,0:T(8,128)(2,1)S(1)} %get-tuple-element.22), channel_id=1, source_target_pairs={{0,6},{1,7},{2,0},{3,1},{4,2},{5,3},{6,4},{7,5},{8,14},{9,15},{10,... | collective-permute-start | bytes 1179656 | tf_op jit(solution)/shard_map/ppermute | solution.py:271
  84.9 14.2 %collective-permute-start.9 = (bf16[96,2048]{1,0:T(8,128)(2,1)S(1)}, bf16[96,2048]{1,0:T(8,128)(2,1)S(1)}, u32[]{:S(2)}, u32[]{:S(2)}) collective-permute-start(bf16[96,2048]{1,0:T(8,128)(2,1)S(1)} %get-tuple-element.20), channel_id=1, source_target_pairs={{0,2},{1,3},{2,4},{3,5},{4,6},{5,7},{6,0},{7,1},{8,10},{9,11},{10,... | collective-permute-start | bytes 1179656 | tf_op jit(solution)/shard_map/ppermute | solution.py:271
  85.0 20.2 %collective-permute-start.14 = (bf16[96,2048]{1,0:T(8,128)(2,1)S(1)}, bf16[96,2048]{1,0:T(8,128)(2,1)S(1)}, u32[]{:S(2)}, u32[]{:S(2)}) collective-permute-start(bf16[96,2048]{1,0:T(8,128)(2,1)S(1)} %add_convert_fusion), channel_id=1, source_target_pairs={{0,6},{1,7},{2,0},{3,1},{4,2},{5,3},{6,4},{7,5},{8,14},{9,15},{10,... | collective-permute-start | bytes 1179656 | tf_op jit(solution)/shard_map/ppermute | solution.py:271
  99.2 9.1 %collective-permute-start.10 = (bf16[96,2048]{1,0:T(8,128)(2,1)S(1)}, bf16[96,2048]{1,0:T(8,128)(2,1)S(1)}, u32[]{:S(2)}, u32[]{:S(2)}) collective-permute-start(bf16[96,2048]{1,0:T(8,128)(2,1)S(1)} %add_convert_fusion.1), channel_id=1, source_target_pairs={{0,2},{1,3},{2,4},{3,5},{4,6},{5,7},{6,0},{7,1},{8,10},{9,11},{10,... | collective-permute-start | bytes 1179656 | tf_op jit(solution)/shard_map/ppermute | solution.py:271
  108.2 25.4 %copy-start.3 = (bf16[256,4096]{1,0:T(8,128)(2,1)S(1)}, bf16[256,4096]{1,0:T(8,128)(2,1)}, u32[]{:S(2)}) copy-start(bf16[256,4096]{1,0:T(8,128)(2,1)} %tokens_ref.3) | copy-start | bytes 6291460
  109.4 24.2 %copy-start.5 = (f32[256,32]{0,1:T(8,128)S(1)}, f32[256,32]{0,1:T(8,128)}, u32[]{:S(2)}) copy-start(f32[256,32]{0,1:T(8,128)} %param.9) | copy-start | bytes 98308
  109.5 24.2 %copy-start.6 = (f32[32,384]{1,0:T(8,128)S(1)}, f32[32,384]{1,0:T(8,128)}, u32[]{:S(2)}) copy-start(f32[32,384]{1,0:T(8,128)} %gates_ref.1) | copy-start | bytes 147460
  109.5 24.2 %copy-start.8 = (s32[256]{0:T(256)S(1)}, s32[256]{0:T(256)}, u32[]{:S(2)}) copy-start(s32[256]{0:T(256)} %param.12) | copy-start | bytes 3076

commit v3 on v2

v3 whole, which is shorter than its diff:
```python
import functools

import jax
import jax.numpy as jnp
from jax import lax
from jax.experimental import pallas as pl
from jax.experimental.pallas import tpu as pltpu
from jax.sharding import PartitionSpec as P

BLOCK = 128
MOST = 3
PIECE = 512
BF16 = jnp.bfloat16
F32 = jnp.float32
I32 = jnp.int32
MIB = 1024 * 1024


def mul(a, b):
    return jnp.dot(a, b, preferred_element_type=F32)


def mul_t(a, b):
    return lax.dot_general(a, b, (((1,), (1,)), ((), ())), preferred_element_type=F32)


def iota(shape, dim):
    return lax.broadcasted_iota(I32, shape, dim)


def third(q):
    return lax.shift_right_logical(q * 11, 5)


def slots_of(index, base, tok_rows, gates=None):
    cap = index.shape[1]
    local = index - base
    mine = (local >= 0) & (local < tok_rows)
    upper = (iota((cap, cap), 0) <= iota((cap, cap), 1)).astype(F32).astype(BF16)
    rank = mul(mine.astype(F32).astype(BF16), upper)
    hot = []
    for s in range(MOST):
        hit = mine & (rank == float(s + 1))
        token = jnp.sum(jnp.where(hit, local + 1, 0), axis=1, keepdims=True) - 1
        here = iota((index.shape[0], tok_rows), 1) == token
        value = 1.0
        if gates is not None:
            value = jnp.sum(jnp.where(hit, gates, 0.0), axis=1, keepdims=True)
        hot.append(jnp.where(here, value, 0.0))
    return jnp.concatenate(hot, axis=0)


def scale_columns(scales_ref, column_ref):
    scales = scales_ref[...]
    blank = jnp.zeros((BLOCK - scales.shape[0], scales.shape[1]), F32)
    column_ref[...] = jnp.transpose(jnp.concatenate([scales, blank], axis=0))


def scaled_piece(tokens, column, first):
    lane = iota(column.shape, 1)
    parts = []
    for b in range(tokens.shape[1] // BLOCK):
        part = tokens[:, b * BLOCK : (b + 1) * BLOCK].astype(F32)
        scale = jnp.sum(jnp.where(lane == first + b, column, 0.0), axis=1, keepdims=True)
        parts.append((part * scale).astype(BF16))
    return jnp.concatenate(parts, axis=1)


def put_piece(wide_ref, piece, experts, value):
    per = wide_ref.shape[1] // experts
    for s in range(MOST):
        at = pl.ds(piece * MOST + s, experts, stride=per)
        for q in range(PIECE // BLOCK):
            wide_ref[q, at, :] = value[
                s * experts : (s + 1) * experts, q * BLOCK : (q + 1) * BLOCK
            ]


def get_piece(wide_ref, piece, experts):
    per = wide_ref.shape[1] // experts
    lanes = []
    for q in range(PIECE // BLOCK):
        lanes.append(
            jnp.concatenate(
                [
                    wide_ref[q, pl.ds(piece * MOST + s, experts, stride=per), :]
                    for s in range(MOST)
                ],
                axis=0,
            )
        )
    return jnp.concatenate(lanes, axis=1).astype(BF16)


def narrow_raw(wide_ref, out_ref):
    for q in range(PIECE // BLOCK):
        out_ref[:, q * BLOCK : (q + 1) * BLOCK] = wide_ref[q].astype(BF16)


def widen_raw(raw_ref, wide_ref):
    for q in range(PIECE // BLOCK):
        wide_ref[q] = raw_ref[:, q * BLOCK : (q + 1) * BLOCK].astype(F32)


def first_token(tok_rows):
    rank = lax.axis_index("wide") * lax.axis_size("narrow") + lax.axis_index("narrow")
    return rank * tok_rows


def most_rows(index, tok_rows, n_narrow):
    narrow = lax.shift_right_logical(index, tok_rows.bit_length() - 1) & (n_narrow - 1)
    most = jnp.zeros((index.shape[0], 1), F32)
    for n in range(n_narrow):
        held = jnp.sum(jnp.where(narrow == n, 1.0, 0.0), axis=1, keepdims=True)
        most = jnp.maximum(most, held)
    return jnp.max(most, axis=0, keepdims=True).astype(I32)


def dispatch_kernel(
    index_ref, tokens_ref, scales_ref, out_ref, most_ref, hot_ref, column_ref, raw_ref
):
    step = pl.program_id(0)
    experts = index_ref.shape[0]
    tok_rows, chunk = tokens_ref.shape

    @pl.when(step == 0)
    def _():
        hot_ref[...] = slots_of(index_ref[...], first_token(tok_rows), tok_rows).astype(BF16)
        scale_columns(scales_ref, column_ref)
        most_ref[...] = most_rows(index_ref[...], tok_rows, lax.axis_size("narrow"))

    rows = scaled_piece(tokens_ref[...], column_ref[...], step * (chunk // BLOCK))
    picked = mul(hot_ref[...], rows)
    for k in range(chunk // PIECE):
        piece = step * (chunk // PIECE) + k
        put_piece(raw_ref, piece, experts, picked[:, k * PIECE : (k + 1) * PIECE])

    @pl.when(step == pl.num_programs(0) - 1)
    def _():
        narrow_raw(raw_ref, out_ref)


def row_places(index_ref, tok_rows, first_row, rows):
    wide, cap = index_ref.shape
    n_narrow = lax.axis_size("narrow")
    mine = index_ref[pl.ds(lax.axis_index("wide"), 1), :]
    first = (iota((wide, cap), 0) * n_narrow + lax.axis_index("narrow")) * tok_rows
    inside = jnp.where((mine >= first) & (mine < first + tok_rows), 1.0, 0.0).astype(BF16)
    counts = mul_t(jnp.ones((8, cap), BF16), inside).astype(BF16)
    n = iota((wide, MOST * wide), 1)
    slot = (n >= wide).astype(I32) + (n >= 2 * wide).astype(I32)
    of, at = n - slot * wide, iota((wide, MOST * wide), 0)
    count = mul(counts, jnp.where(at == of, 1.0, 0.0).astype(BF16))[0:1]
    before = mul(counts, jnp.where(at < of, 1.0, 0.0).astype(BF16))[0:1]
    slot = slot[0:1].astype(F32)
    place = jnp.where(slot < count, before + slot, -1.0)
    hot = (iota((rows, MOST * wide), 0) + first_row).astype(F32) == place
    return jnp.where(hot, 1.0, 0.0).astype(BF16)


def unpack_kernel(tok_rows, first_row, index_ref, raw_ref, *refs):
    out_refs, wide_ref = refs[:-1], refs[-1]
    rows, half = out_refs[0].shape
    wide = index_ref.shape[0]
    widen_raw(raw_ref, wide_ref)
    places = row_places(index_ref, tok_rows, first_row, rows)
    for j in range(2 * half // PIECE):
        at = j * PIECE % half
        value = mul(places, get_piece(wide_ref, j, wide)).astype(BF16)
        out_refs[j * PIECE // half][:, at : at + PIECE] = value


def expert_kernel(blocks, *refs):
    xs, own, away, refs = (
        refs[: 2 * blocks],
        refs[2 * blocks : 2 * blocks + 2],
        refs[2 * blocks + 2 : 2 * blocks + 6],
        refs[2 * blocks + 6 :],
    )
    outs, held, sems = refs[: 2 * blocks], refs[2 * blocks : 2 * blocks + 4], refs[-1]
    copies = [pltpu.make_async_copy(away[k], held[k], sems.at[k]) for k in range(4)]
    for copy in copies:
        copy.start()
    left = jnp.concatenate([x[...] for x in xs[0::2]], axis=0)
    right = jnp.concatenate([x[...] for x in xs[1::2]], axis=0)
    rows, half = outs[0].shape
    hidden = []
    for gate_w, up_w in (own, held[:2]):
        if hidden:
            copies[0].wait()
            copies[1].wait()
        v = mul_t(gate_w[:, :half], left) + mul_t(gate_w[:, half:], right)
        u = mul_t(up_w[:, :half], left) + mul_t(up_w[:, half:], right)
        hidden.append(jnp.transpose(v / (1.0 + jnp.exp(-v)) * u).astype(BF16))
    copies[2].wait()
    copies[3].wait()
    for c in range(2 * half // PIECE):
        cols = slice(c * PIECE, (c + 1) * PIECE)
        part = mul(hidden[0], held[2][:, cols]) + mul(hidden[1], held[3][:, cols])
        at = c * PIECE % half
        for b in range(blocks):
            out = outs[2 * b + c * PIECE // half]
            out[:, at : at + PIECE] = part[b * rows : (b + 1) * rows].astype(out.dtype)


def expert(xs, own, sibling, out_types):
    rows, half = xs[0][0].shape
    blocks = len(xs)
    hid, width = own[2].shape
    args = [x for pair in xs for x in pair]
    away = [sibling[0], sibling[1], own[2], sibling[2]]
    args += [own[0], own[1], *away]
    vmem = pl.BlockSpec(memory_space=pltpu.VMEM)
    return pl.pallas_call(
        functools.partial(expert_kernel, blocks),
        in_specs=[vmem] * (len(args) - 4) + [pl.BlockSpec(memory_space=pl.ANY)] * 4,
        out_specs=[vmem] * (2 * blocks),
        out_shape=[jax.ShapeDtypeStruct((rows, half), t) for t in out_types],
        scratch_shapes=[pltpu.VMEM(w.shape, BF16) for w in away]
        + [pltpu.SemaphoreType.DMA((4,))],
        compiler_params=pltpu.CompilerParams(vmem_limit_bytes=30 * MIB),
        cost_estimate=pl.CostEstimate(flops=1, bytes_accessed=1, transcendentals=0),
    )(*args)


def pack_kernel(tok_rows, first_row, index_ref, *refs):
    parts, out_ref, raw_ref = refs[:6], refs[-2], refs[-1]
    rows, half = parts[0].shape
    wide = index_ref.shape[0]
    places = row_places(index_ref, tok_rows, first_row, rows)
    for j in range(2 * half // PIECE):
        at = j * PIECE % half
        summed = sum(p[:, at : at + PIECE].astype(F32) for p in parts[j * PIECE // half :: 2])
        summed = lax.dot_general(
            places,
            summed.astype(BF16),
            (((0,), (0,)), ((), ())),
            preferred_element_type=F32,
        )
        put_piece(raw_ref, j, wide, summed)
    narrow_raw(raw_ref, out_ref)
    if len(refs) > 8:
        out_ref[...] += refs[6][...]


def combine_kernel(
    index_ref, gates_ref, counts_ref, tokens_ref, scales_ref, raw_ref, out_ref, weight_ref, column_ref, wide_ref
):
    step = pl.program_id(0)
    experts = index_ref.shape[0]
    tok_rows, chunk = tokens_ref.shape

    @pl.when(step == 0)
    def _():
        weight = slots_of(index_ref[...], first_token(tok_rows), tok_rows, gates_ref[...])
        weight = weight / jnp.maximum(counts_ref[...], 1).astype(F32)
        high = weight.astype(BF16).astype(F32)
        both = jnp.concatenate([high, weight - high], axis=0)
        weight_ref[...] = jnp.transpose(both).astype(BF16)
        scale_columns(scales_ref, column_ref)
        widen_raw(raw_ref, wide_ref)

    pieces = chunk // PIECE
    got = [get_piece(wide_ref, step * pieces + k, experts) for k in range(pieces)]
    got = jnp.concatenate(got, axis=1)
    branch = mul(weight_ref[...], jnp.concatenate([got, got], axis=0))
    rows = scaled_piece(tokens_ref[...], column_ref[...], step * (chunk // BLOCK))
    out_ref[...] = (rows.astype(F32) + branch).astype(BF16)


def along_y(x, step):
    n = lax.axis_size("narrow")
    return lax.ppermute(x, "narrow", [(i, (i + 2 * step) % n) for i in range(n)])


def around_y(first_row, rows, tok_rows, arrived, pick_index, own, sibling, earlier=()):
    total = arrived.shape[0]
    width = own[2].shape[1]
    vmem = pl.BlockSpec(memory_space=pltpu.VMEM)
    raw_f32 = pltpu.VMEM((PIECE // BLOCK, total, BLOCK), F32)
    half_shape = jax.ShapeDtypeStruct((rows, width // 2), BF16)
    x0 = pl.pallas_call(
        functools.partial(unpack_kernel, tok_rows, first_row),
        in_specs=[vmem] * 2,
        out_specs=[vmem, vmem],
        out_shape=[half_shape, half_shape],
        scratch_shapes=[raw_f32],
        compiler_params=pltpu.CompilerParams(vmem_limit_bytes=24 * MIB),
    )(pick_index, arrived)

    xm, xp = [along_y(x0[0], 1), None], [None, along_y(x0[1], -1)]
    xm[1] = along_y(x0[1], 1)
    xp[0] = along_y(x0[0], -1)
    x2 = (along_y(xm[0], 1), along_y(xp[1], -1))

    p0 = expert([x0], own, sibling, (F32, F32))
    xp[0], xp[1], xm[0], xm[1] = lax.optimization_barrier((*xp, *xm, p0[0]))[:4]
    pp_a, pp_b, pm_a, pm_b = expert([xp, xm], own, sibling, (F32, BF16, BF16, F32))
    x2 = lax.optimization_barrier((*x2, pp_b))[:2]
    p2 = expert([x2], own, sibling, (BF16, BF16))
    got_mb = along_y(pp_b, 1)
    got_pa = along_y(pm_a, -1)
    from_m = along_y(p2[0], 1)
    from_p = along_y(p2[1], -1)
    from_m, got_mb = lax.optimization_barrier((from_m, got_mb))
    from_p, got_pa = lax.optimization_barrier((from_p, got_pa))
    got_ma = along_y((pp_a + from_m.astype(F32)).astype(BF16), 1)
    got_pb = along_y((pm_b + from_p.astype(F32)).astype(BF16), -1)
    return pl.pallas_call(
        functools.partial(pack_kernel, tok_rows, first_row),
        in_specs=[vmem] * (7 + len(earlier)),
        out_specs=vmem,
        out_shape=jax.ShapeDtypeStruct((total, PIECE), BF16),
        scratch_shapes=[raw_f32],
        compiler_params=pltpu.CompilerParams(vmem_limit_bytes=32 * MIB),
    )(pick_index, p0[0], p0[1], got_ma, got_mb, got_pa, got_pb, *earlier)


def local(
    tokens, block_scales, pick_index, pick_gates, pick_counts, gate_weight, up_weight, down_weight
):
    tok_rows, width = tokens.shape
    n_wide = lax.axis_size("wide")
    n_narrow = lax.axis_size("narrow")
    other_core = [(i, i ^ 1) for i in range(n_narrow)]
    pieces = width // PIECE
    per = MOST * pieces
    total = n_wide * per
    scales = block_scales.T
    chunk = 2 * PIECE
    steps = width // chunk

    def whole(a):
        return pl.BlockSpec(a.shape, lambda j: (0,) * a.ndim)

    own = (gate_weight[0].T, up_weight[0].T, down_weight[0])
    sibling = tuple(lax.ppermute(v, "narrow", other_core) for v in own)

    tokens_spec = pl.BlockSpec((tok_rows, chunk), lambda j: (0, j))
    column = pltpu.VMEM((tok_rows, BLOCK), F32)
    raw_f32 = pltpu.VMEM((PIECE // BLOCK, total, BLOCK), F32)
    raw_shape = jax.ShapeDtypeStruct((total, PIECE), BF16)
    outgoing, most = pl.pallas_call(
        dispatch_kernel,
        grid=(steps,),
        in_specs=[whole(pick_index), tokens_spec, whole(scales)],
        out_specs=[
            pl.BlockSpec((total, PIECE), lambda j: (0, 0)),
            pl.BlockSpec((1, 1), lambda j: (0, 0)),
        ],
        out_shape=[raw_shape, jax.ShapeDtypeStruct((1, 1), I32)],
        scratch_shapes=[pltpu.VMEM((MOST * n_wide, tok_rows), BF16), column, raw_f32],
        compiler_params=pltpu.CompilerParams(vmem_limit_bytes=56 * MIB),
    )(pick_index, tokens, scales)

    def exchange(raw):
        raw = raw.reshape(n_wide, per, PIECE)
        raw = lax.all_to_all(raw, "wide", split_axis=0, concat_axis=0, tiled=True)
        return raw.reshape(total, PIECE)

    arrived = exchange(outgoing)
    rows = MOST * n_wide * 3 // 4
    packed = around_y(0, rows, tok_rows, arrived, pick_index, own, sibling)

    def second(packed):
        return around_y(rows, rows // 2, tok_rows, arrived, pick_index, own, sibling, (packed,))

    packed = lax.cond(most[0, 0] > rows, second, lambda packed: packed, packed)
    returned = exchange(packed)
    counts = pick_counts.reshape(1, tok_rows)
    return pl.pallas_call(
        combine_kernel,
        grid=(steps,),
        in_specs=[
            whole(pick_index),
            whole(pick_gates),
            whole(counts),
            tokens_spec,
            whole(scales),
            whole(returned),
        ],
        out_specs=tokens_spec,
        out_shape=jax.ShapeDtypeStruct((tok_rows, width), BF16),
        scratch_shapes=[pltpu.VMEM((tok_rows, 2 * MOST * n_wide), BF16), column, raw_f32],
        compiler_params=pltpu.CompilerParams(vmem_limit_bytes=24 * MIB),
    )(pick_index, pick_gates, counts, tokens, scales, returned)


def solution(mesh):
    return jax.shard_map(
        local,
        mesh=mesh,
        in_specs=(
            P(("wide", "narrow"), None),
            P(("wide", "narrow"), None),
            P(),
            P(),
            P(("wide", "narrow")),
            P("wide", None, "narrow"),
            P("wide", None, "narrow"),
            P("wide", "narrow", None),
        ),
        out_specs=P(("wide", "narrow"), None),
        check_vma=False,
    )
```

time: 138 us -> 121 us (0.88)
  waiting for transfers between devices: 50.7 us -> 39.8 us
  Pallas kernels: 30 us -> 23.2 us
  local copies, waits for them, and re-layouts: 2.05 us -> 0.04 us
  blocking collectives: 24.1 us -> 25.8 us
    ppermute x12, waiting for transfers between devices: 28.2 us -> 17.3 us  [along_y(): lax.ppermute(x, 'narrow', [(i, (i + 2 * step) % n) for i in range(n)])]
    pallas_call x7, Pallas kernels: 30 us -> 23.2 us  [the longest x3 11.8 us: expert(): pl.pallas_call(functools.partial(expert_kernel, blocks), in_specs=[vmem]...]
    all_to_all x1, blocking collectives: 24.1 us -> 25.8 us  [exchange(): raw = lax.all_to_all(raw, 'wide', split_axis=0, concat_axis=0, tiled=True)]
    unnamed x18 -> x16, local copies, waits for them, and re-layouts: 1.45 us -> 0.04 us
  transfers between devices with their start and end apart: 16 -> 16, of which waited for: 5 -> 7; matrix products, arithmetic and copies ran while one was open for 0% -> 0% of each run, Pallas kernels for 14% -> 11%
where the time goes in v3:
time: 121 us; the launch traced here: 120 us
  waiting for transfers between devices  39.8 us (33%)
  starting transfers between devices  29.8 us (25%)
  blocking collectives  25.8 us (21%)
  Pallas kernels  23.2 us (19%)
    all_to_all x1, blocking collectives, exchange(): raw = lax.all_to_all(raw, 'wide', split_axis=0, concat_axis=0, tiled=True)  25.8 us
    all_to_all x1, waiting for transfers between devices, exchange(): raw = lax.all_to_all(raw, 'wide', split_axis=0, concat_axis=0, tiled=True)  22.5 us
    ppermute x12, starting transfers between devices, along_y(): lax.ppermute(x, 'narrow', [(i, (i + 2 * step) % n) for i in range(n)])  17.9 us
    ppermute x12, waiting for transfers between devices, along_y(): lax.ppermute(x, 'narrow', [(i, (i + 2 * step) % n) for i in range(n)])  17.3 us
    pallas_call x3, Pallas kernels, expert(): pl.pallas_call(functools.partial(expert_kernel, blocks), in_specs=[vmem]...  11.8 us
    all_to_all x1, starting transfers between devices, exchange(): raw = lax.all_to_all(raw, 'wide', split_axis=0, concat_axis=0, tiled=True)  11.2 us
    pallas_call x1, Pallas kernels, local(): pl.pallas_call(dispatch_kernel, grid=(steps,), in_specs=[whole(pick_index...  5.17 us
    pallas_call x1, Pallas kernels, local(): pl.pallas_call(combine_kernel, grid=(steps,), in_specs=[whole(pick_index)...  3.45 us
  transfers between devices with their start and end apart: 16, of which 7 were waited for; matrix products, arithmetic and copies ran while one was open for 0% of the time, Pallas kernels for 11%

profile of v3, /device:TPU:32, one launch (start us, length us, event | category | flops | bytes accessed | tf_op | source)
XLA Modules:
  0.0 119.9 jit_solution(17537095859995779210)
XLA Ops:
  0.0 0.0 copy-start.4
  0.0 0.0 copy-start.6
  0.0 0.0 copy-start.11
  0.0 5.2 %shard_map.82 = (bf16[768,512]{1,0:T(8,128)(2,1)}, s32[1,1]{1,0:T(1,128)}) custom-call(s32[32,384]{1,0:T(8,128)} %index_ref.7, bf16[256,4096]{1,0:T(8,128)(2,1)} %tokens_ref.3, f32[32,256]{1,0:T(8,128)} %bitcast.15), custom_call_target="tpu_custom_call" | custom-call | tf_op jit(solution)/shard_map/pallas_call | solution.py:343
  5.2 11.2 %all-to-all-start = ((bf16[32,24,512]{2,1,0:T(8,128)(2,1)}), bf16[32,24,512]{2,1,0:T(8,128)(2,1)}, u32[]{:S(2)}, u32[]{:S(2)}) async-start(bf16[32,24,512]{2,1,0:T(8,128)(2,1)} %bitcast.34), calls=%async_computation | async-start | bytes 1572864 | tf_op jit(solution)/shard_map/all_to_all | solution.py:358
  16.4 0.0 copy-done.4
  16.4 0.1 collective-permute-start.12
  16.5 0.0 copy-done.6
  16.5 0.5 collective-permute-start.13
  17.0 0.1 collective-permute-start.14
  17.1 22.5 %all-to-all-done = bf16[32,24,512]{2,1,0:T(8,128)(2,1)} async-done(((bf16[32,24,512]{2,1,0:T(8,128)(2,1)}), bf16[32,24,512]{2,1,0:T(8,128)(2,1)}, u32[]{:S(2)}, u32[]{:S(2)}) %all-to-all-start) | async-done | bytes 786464 | tf_op jit(solution)/shard_map/all_to_all | solution.py:358
  39.7 0.0 copy-done.11
  39.7 1.8 %shard_map.83 = (bf16[72,2048]{1,0:T(8,128)(2,1)S(1)}, bf16[72,2048]{1,0:T(8,128)(2,1)S(1)}) custom-call(s32[32,384]{1,0:T(8,128)S(1)} %copy-done.11, bf16[768,512]{1,0:T(8,128)(2,1)} %bitcast.4.raw_ref), custom_call_target="tpu_custom_call" | custom-call | tf_op jit(solution)/shard_map/pallas_call | solution.py:282
  41.5 1.7 %collective-permute-start.17 = (bf16[72,2048]{1,0:T(8,128)(2,1)S(1)}, bf16[72,2048]{1,0:T(8,128)(2,1)S(1)}, u32[]{:S(2)}, u32[]{:S(2)}) collective-permute-start(bf16[72,2048]{1,0:T(8,128)(2,1)S(1)} %get-tuple-element.80.refs_0_), channel_id=1, source_target_pairs={{0,2},{1,3},{2,4},{3,5},{4,6},{5,7},{6,0},{7,1},{8,10},{9,11},{10,... | collective-permute-start | bytes 884744 | tf_op jit(solution)/shard_map/ppermute | solution.py:273
  43.1 0.0 copy-start.8
  43.1 1.7 %collective-permute-start.16 = (bf16[72,2048]{1,0:T(8,128)(2,1)S(1)}, bf16[72,2048]{1,0:T(8,128)(2,1)S(1)}, u32[]{:S(2)}, u32[]{:S(2)}) collective-permute-start(bf16[72,2048]{1,0:T(8,128)(2,1)S(1)} %get-tuple-element.81.refs_1_), channel_id=1, source_target_pairs={{0,6},{1,7},{2,0},{3,1},{4,2},{5,3},{6,4},{7,5},{8,14},{9,15},{10,... | collective-permute-start | bytes 884744 | tf_op jit(solution)/shard_map/ppermute | solution.py:273
  44.8 0.0 collective-permute-done.12.refs_4_.refs_6_
  44.8 1.8 %collective-permute-start.15 = (bf16[72,2048]{1,0:T(8,128)(2,1)S(1)}, bf16[72,2048]{1,0:T(8,128)(2,1)S(1)}, u32[]{:S(2)}, u32[]{:S(2)}) collective-permute-start(bf16[72,2048]{1,0:T(8,128)(2,1)S(1)} %get-tuple-element.80.refs_0_), channel_id=1, source_target_pairs={{0,6},{1,7},{2,0},{3,1},{4,2},{5,3},{6,4},{7,5},{8,14},{9,15},{10,... | collective-permute-start | bytes 884744 | tf_op jit(solution)/shard_map/ppermute | solution.py:273
  46.6 0.0 collective-permute-done.13.refs_5_.refs_7_
  46.6 0.2 collective-permute-start.18
  46.8 5.0 %collective-permute-done.17.refs_2_ = bf16[72,2048]{1,0:T(8,128)(2,1)S(1)} collective-permute-done((bf16[72,2048]{1,0:T(8,128)(2,1)S(1)}, bf16[72,2048]{1,0:T(8,128)(2,1)S(1)}, u32[]{:S(2)}, u32[]{:S(2)}) %collective-permute-start.17) | collective-permute-done | bytes 294944 | tf_op jit(solution)/shard_map/ppermute | solution.py:273
  51.8 1.2 %collective-permute-start.19 = (bf16[72,2048]{1,0:T(8,128)(2,1)S(1)}, bf16[72,2048]{1,0:T(8,128)(2,1)S(1)}, u32[]{:S(2)}, u32[]{:S(2)}) collective-permute-start(bf16[72,2048]{1,0:T(8,128)(2,1)S(1)} %collective-permute-done.17.refs_2_), channel_id=1, source_target_pairs={{0,2},{1,3},{2,4},{3,5},{4,6},{5,7},{6,0},{7,1},{8,10},{9,11},{10,... | collective-permute-start | bytes 884744 | tf_op jit(solution)/shard_map/ppermute | solution.py:273
  53.1 0.0 collective-permute-done.16.refs_1_
  53.1 2.9 %collective-permute-start.20 = (bf16[72,2048]{1,0:T(8,128)(2,1)S(1)}, bf16[72,2048]{1,0:T(8,128)(2,1)S(1)}, u32[]{:S(2)}, u32[]{:S(2)}) collective-permute-start(bf16[72,2048]{1,0:T(8,128)(2,1)S(1)} %collective-permute-done.16.refs_1_), channel_id=1, source_target_pairs={{0,6},{1,7},{2,0},{3,1},{4,2},{5,3},{6,4},{7,5},{8,14},{9,15},{10,... | collective-permute-start | bytes 884744 | tf_op jit(solution)/shard_map/ppermute | solution.py:273
  56.0 0.0 collective-permute-done.14.refs_7_.refs_9_
  56.0 4.4 %shard_map.84 = (f32[72,2048]{1,0:T(8,128)S(1)}, f32[72,2048]{1,0:T(8,128)S(1)}) custom-call(bf16[72,2048]{1,0:T(8,128)(2,1)S(1)} %get-tuple-element.80.refs_0_, bf16[72,2048]{1,0:T(8,128)(2,1)S(1)} %get-tuple-element.81.refs_1_, bf16[192,4096]{1,0:T(8,128)(2,1)S(1)} %bitcast.20, bf16[192,4096]{1,0:T(8,128)(2,1)S(1)} %bitcast.25, ...), custom_call_target="tpu_custom_call" | custom-call | flops 1 | bytes 1 | tf_op jit(solution)/shard_map/pallas_call | solution.py:214
  60.4 0.0 collective-permute-done.15.refs_0_
  60.4 0.0 collective-permute-done.18.refs_3_
  60.4 0.0 copy-done.8
  60.4 3.8 %shard_map.85 = (f32[72,2048]{1,0:T(8,128)S(1)}, bf16[72,2048]{1,0:T(8,128)(2,1)S(1)}, bf16[72,2048]{1,0:T(8,128)(2,1)S(1)}, f32[72,2048]{1,0:T(8,128)S(1)}) custom-call(bf16[72,2048]{1,0:T(8,128)(2,1)S(1)} %collective-permute-done.15.refs_0_, bf16[72,2048]{1,0:T(8,128)(2,1)S(1)} %collective-permute-done.16.refs_1_, ...), custom_call_target="tpu_custom_call" | custom-call | flops 1 | bytes 1 | tf_op jit(solution)/shard_map/pallas_call | solution.py:214
  64.2 0.3 collective-permute-start.22
  64.5 0.0 collective-permute-done.19.refs_0_
  64.5 0.0 collective-permute-done.20.refs_1_
  64.5 3.6 %shard_map.86 = (bf16[72,2048]{1,0:T(8,128)(2,1)S(1)}, bf16[72,2048]{1,0:T(8,128)(2,1)S(1)}) custom-call(bf16[72,2048]{1,0:T(8,128)(2,1)S(1)} %collective-permute-done.19.refs_0_, bf16[72,2048]{1,0:T(8,128)(2,1)S(1)} %collective-permute-done.20.refs_1_, bf16[192,4096]{1,0:T(8,128)(2,1)S(1)} %bitcast.22, bf16[192,4096]{1,0:T(8,128)(2,1)S(1)} %bitcast.27, ...), custom_call_target="tpu_custom_call" | custom-call | flops 1 | bytes 1 | tf_op jit(solution)/shard_map/pallas_call | solution.py:214
  68.2 1.3 %collective-permute-start.21 = (bf16[72,2048]{1,0:T(8,128)(2,1)S(1)}, bf16[72,2048]{1,0:T(8,128)(2,1)S(1)}, u32[]{:S(2)}, u32[]{:S(2)}) collective-permute-start(bf16[72,2048]{1,0:T(8,128)(2,1)S(1)} %get-tuple-element.92), channel_id=1, source_target_pairs={{0,2},{1,3},{2,4},{3,5},{4,6},{5,7},{6,0},{7,1},{8,10},{9,11},{10,... | collective-permute-start | bytes 884744 | tf_op jit(solution)/shard_map/ppermute | solution.py:273
  69.4 2.1 %collective-permute-start.25 = (bf16[72,2048]{1,0:T(8,128)(2,1)S(1)}, bf16[72,2048]{1,0:T(8,128)(2,1)S(1)}, u32[]{:S(2)}, u32[]{:S(2)}) collective-permute-start(bf16[72,2048]{1,0:T(8,128)(2,1)S(1)} %get-tuple-element.96), channel_id=1, source_target_pairs={{0,6},{1,7},{2,0},{3,1},{4,2},{5,3},{6,4},{7,5},{8,14},{9,15},{10,... | collective-permute-start | bytes 884744 | tf_op jit(solution)/shard_map/ppermute | solution.py:273
  71.5 1.9 %collective-permute-start.24 = (bf16[72,2048]{1,0:T(8,128)(2,1)S(1)}, bf16[72,2048]{1,0:T(8,128)(2,1)S(1)}, u32[]{:S(2)}, u32[]{:S(2)}) collective-permute-start(bf16[72,2048]{1,0:T(8,128)(2,1)S(1)} %get-tuple-element.95), channel_id=1, source_target_pairs={{0,6},{1,7},{2,0},{3,1},{4,2},{5,3},{6,4},{7,5},{8,14},{9,15},{10,... | collective-permute-start | bytes 884744 | tf_op jit(solution)/shard_map/ppermute | solution.py:273
  73.5 0.2 collective-permute-done.22.refs_3_
  73.7 4.1 %collective-permute-done.21 = bf16[72,2048]{1,0:T(8,128)(2,1)S(1)} collective-permute-done((bf16[72,2048]{1,0:T(8,128)(2,1)S(1)}, bf16[72,2048]{1,0:T(8,128)(2,1)S(1)}, u32[]{:S(2)}, u32[]{:S(2)}) %collective-permute-start.21) | collective-permute-done | bytes 294944 | tf_op jit(solution)/shard_map/ppermute | solution.py:273
  77.8 0.1 add_convert_fusion.3
  77.9 0.4 collective-permute-start.23
  78.3 0.0 collective-permute-done.25.refs_4_
  78.3 4.1 %collective-permute-done.24 = bf16[72,2048]{1,0:T(8,128)(2,1)S(1)} collective-permute-done((bf16[72,2048]{1,0:T(8,128)(2,1)S(1)}, bf16[72,2048]{1,0:T(8,128)(2,1)S(1)}, u32[]{:S(2)}, u32[]{:S(2)}) %collective-permute-start.24) | collective-permute-done | bytes 294944 | tf_op jit(solution)/shard_map/ppermute | solution.py:273
  82.5 0.1 add_convert_fusion.2
  82.5 2.5 %collective-permute-start.26 = (bf16[72,2048]{1,0:T(8,128)(2,1)S(1)}, bf16[72,2048]{1,0:T(8,128)(2,1)S(1)}, u32[]{:S(2)}, u32[]{:S(2)}) collective-permute-start(bf16[72,2048]{1,0:T(8,128)(2,1)S(1)} %add_convert_fusion.2), channel_id=1, source_target_pairs={{0,6},{1,7},{2,0},{3,1},{4,2},{5,3},{6,4},{7,5},{8,14},{9,15},{10,... | collective-permute-start | bytes 884744 | tf_op jit(solution)/shard_map/ppermute | solution.py:273
  85.6 0.3 collective-permute-done.23.refs_2_
  85.9 3.4 %collective-permute-done.26.refs_5_ = bf16[72,2048]{1,0:T(8,128)(2,1)S(1)} collective-permute-done((bf16[72,2048]{1,0:T(8,128)(2,1)S(1)}, bf16[72,2048]{1,0:T(8,128)(2,1)S(1)}, u32[]{:S(2)}, u32[]{:S(2)}) %collective-permute-start.26) | collective-permute-done | bytes 294944 | tf_op jit(solution)/shard_map/ppermute | solution.py:273
  89.3 1.0 shard_map.87
  90.3 0.0 copy-start
  90.3 0.3 conditional.1
  90.6 0.0 copy-start.1
  90.6 0.0 copy-start.2
  90.6 0.0 copy-start.3
  90.6 25.8 %all_to_all.10 = bf16[32,24,512]{2,1,0:T(8,128)(2,1)S(1)} all-to-all(bf16[32,24,512]{2,1,0:T(8,128)(2,1)S(1)} %bitcast.33), channel_id=1, replica_groups=mesh['wide'=32,'narrow'=8] {'wide'}, dimensions={0} | all-to-all | bytes 1572864 | tf_op jit(solution)/shard_map/all_to_all | solution.py:358
  116.5 0.0 copy-done
  116.5 0.0 copy-done.1
  116.5 0.0 copy-done.2
  116.5 0.0 copy-done.3
  116.5 3.4 %shard_map.88 = bf16[256,4096]{1,0:T(8,128)(2,1)} custom-call(s32[32,384]{1,0:T(8,128)S(1)} %copy-done.11, f32[32,384]{1,0:T(8,128)S(1)} %copy-done.2, s32[1,256]{1,0:T(1,128)S(1)} %bitcast.17, bf16[256,4096]{1,0:T(8,128)(2,1)S(1)} %copy-done, f32[32,256]{1,0:T(8,128)S(1)} %bitcast.16, bf16[768,512]{1,0:T(8,128)(2,1)S(1)} %bitcast.14), custom_call_target="tpu_custom_call" | custom-call | tf_op jit(solution)/shard_map/pallas_call | solution.py:371
Async XLA Ops:
  0.0 16.4 %copy-start.4 = (bf16[1,4096,192]{1,2,0:T(8,128)(2,1)S(1)}, bf16[1,4096,192]{1,2,0:T(8,128)(2,1)}, u32[]{:S(2)}) copy-start(bf16[1,4096,192]{1,2,0:T(8,128)(2,1)} %param.15) | copy-start | bytes 4718596
  0.0 16.5 %copy-start.6 = (bf16[1,4096,192]{1,2,0:T(8,128)(2,1)S(1)}, bf16[1,4096,192]{1,2,0:T(8,128)(2,1)}, u32[]{:S(2)}) copy-start(bf16[1,4096,192]{1,2,0:T(8,128)(2,1)} %param.16) | copy-start | bytes 4718596
  0.0 39.7 %copy-start.11 = (s32[32,384]{1,0:T(8,128)S(1)}, s32[32,384]{1,0:T(8,128)}, u32[]{:S(2)}) copy-start(s32[32,384]{1,0:T(8,128)} %index_ref.7) | copy-start | bytes 147460
  5.2 34.5 %all-to-all-start = ((bf16[32,24,512]{2,1,0:T(8,128)(2,1)}), bf16[32,24,512]{2,1,0:T(8,128)(2,1)}, u32[]{:S(2)}, u32[]{:S(2)}) async-start(bf16[32,24,512]{2,1,0:T(8,128)(2,1)} %bitcast.34), calls=%async_computation | async-start | bytes 1572864 | tf_op jit(solution)/shard_map/all_to_all | solution.py:358
  16.4 28.4 %collective-permute-start.12 = (bf16[192,4096]{1,0:T(8,128)(2,1)S(1)}, bf16[192,4096]{1,0:T(8,128)(2,1)}, u32[]{:S(2)}, u32[]{:S(2)}) collective-permute-start(bf16[192,4096]{1,0:T(8,128)(2,1)S(1)} %bitcast.19), channel_id=1, source_target_pairs={{0,1},{1,0},{2,3},{3,2},{4,5},{5,4},{6,7},{7,6},{8,9},{9,8},{10,11... | collective-permute-start | bytes 4718600 | tf_op jit(solution)/shard_map/ppermute | solution.py:337
  16.5 30.1 %collective-permute-start.13 = (bf16[192,4096]{1,0:T(8,128)(2,1)S(1)}, bf16[192,4096]{1,0:T(8,128)(2,1)}, u32[]{:S(2)}, u32[]{:S(2)}) collective-permute-start(bf16[192,4096]{1,0:T(8,128)(2,1)S(1)} %bitcast.24), channel_id=1, source_target_pairs={{0,1},{1,0},{2,3},{3,2},{4,5},{5,4},{6,7},{7,6},{8,9},{9,8},{10,11... | collective-permute-start | bytes 4718600 | tf_op jit(solution)/shard_map/ppermute | solution.py:337
  17.0 38.9 %collective-permute-start.14 = (bf16[192,4096]{1,0:T(8,128)(2,1)}, bf16[192,4096]{1,0:T(8,128)(2,1)}, u32[]{:S(2)}, u32[]{:S(2)}) collective-permute-start(bf16[192,4096]{1,0:T(8,128)(2,1)} %bitcast.28), channel_id=1, source_target_pairs={{0,1},{1,0},{2,3},{3,2},{4,5},{5,4},{6,7},{7,6},{8,9},{9,8},{10,11... | collective-permute-start | bytes 4718600 | tf_op jit(solution)/shard_map/ppermute | solution.py:337
  41.5 10.4 %collective-permute-start.17 = (bf16[72,2048]{1,0:T(8,128)(2,1)S(1)}, bf16[72,2048]{1,0:T(8,128)(2,1)S(1)}, u32[]{:S(2)}, u32[]{:S(2)}) collective-permute-start(bf16[72,2048]{1,0:T(8,128)(2,1)S(1)} %get-tuple-element.80.refs_0_), channel_id=1, source_target_pairs={{0,2},{1,3},{2,4},{3,5},{4,6},{5,7},{6,0},{7,1},{8,10},{9,11},{10,... | collective-permute-start | bytes 884744 | tf_op jit(solution)/shard_map/ppermute | solution.py:273
  43.1 17.3 %copy-start.8 = (bf16[1,192,4096]{2,1,0:T(8,128)(2,1)S(1)}, bf16[1,192,4096]{2,1,0:T(8,128)(2,1)}, u32[]{:S(2)}) copy-start(bf16[1,192,4096]{2,1,0:T(8,128)(2,1)} %param.17) | copy-start | bytes 4718596
  43.1 9.9 %collective-permute-start.16 = (bf16[72,2048]{1,0:T(8,128)(2,1)S(1)}, bf16[72,2048]{1,0:T(8,128)(2,1)S(1)}, u32[]{:S(2)}, u32[]{:S(2)}) collective-permute-start(bf16[72,2048]{1,0:T(8,128)(2,1)S(1)} %get-tuple-element.81.refs_1_), channel_id=1, source_target_pairs={{0,6},{1,7},{2,0},{3,1},{4,2},{5,3},{6,4},{7,5},{8,14},{9,15},{10,... | collective-permute-start | bytes 884744 | tf_op jit(solution)/shard_map/ppermute | solution.py:273
  44.8 15.6 %collective-permute-start.15 = (bf16[72,2048]{1,0:T(8,128)(2,1)S(1)}, bf16[72,2048]{1,0:T(8,128)(2,1)S(1)}, u32[]{:S(2)}, u32[]{:S(2)}) collective-permute-start(bf16[72,2048]{1,0:T(8,128)(2,1)S(1)} %get-tuple-element.80.refs_0_), channel_id=1, source_target_pairs={{0,6},{1,7},{2,0},{3,1},{4,2},{5,3},{6,4},{7,5},{8,14},{9,15},{10,... | collective-permute-start | bytes 884744 | tf_op jit(solution)/shard_map/ppermute | solution.py:273
  46.6 13.8 %collective-permute-start.18 = (bf16[72,2048]{1,0:T(8,128)(2,1)S(1)}, bf16[72,2048]{1,0:T(8,128)(2,1)S(1)}, u32[]{:S(2)}, u32[]{:S(2)}) collective-permute-start(bf16[72,2048]{1,0:T(8,128)(2,1)S(1)} %get-tuple-element.81.refs_1_), channel_id=1, source_target_pairs={{0,2},{1,3},{2,4},{3,5},{4,6},{5,7},{6,0},{7,1},{8,10},{9,11},{10,... | collective-permute-start | bytes 884744 | tf_op jit(solution)/shard_map/ppermute | solution.py:273
  51.8 12.7 %collective-permute-start.19 = (bf16[72,2048]{1,0:T(8,128)(2,1)S(1)}, bf16[72,2048]{1,0:T(8,128)(2,1)S(1)}, u32[]{:S(2)}, u32[]{:S(2)}) collective-permute-start(bf16[72,2048]{1,0:T(8,128)(2,1)S(1)} %collective-permute-done.17.refs_2_), channel_id=1, source_target_pairs={{0,2},{1,3},{2,4},{3,5},{4,6},{5,7},{6,0},{7,1},{8,10},{9,11},{10,... | collective-permute-start | bytes 884744 | tf_op jit(solution)/shard_map/ppermute | solution.py:273
  53.1 11.4 %collective-permute-start.20 = (bf16[72,2048]{1,0:T(8,128)(2,1)S(1)}, bf16[72,2048]{1,0:T(8,128)(2,1)S(1)}, u32[]{:S(2)}, u32[]{:S(2)}) collective-permute-start(bf16[72,2048]{1,0:T(8,128)(2,1)S(1)} %collective-permute-done.16.refs_1_), channel_id=1, source_target_pairs={{0,6},{1,7},{2,0},{3,1},{4,2},{5,3},{6,4},{7,5},{8,14},{9,15},{10,... | collective-permute-start | bytes 884744 | tf_op jit(solution)/shard_map/ppermute | solution.py:273
  64.2 9.5 %collective-permute-start.22 = (bf16[72,2048]{1,0:T(8,128)(2,1)S(1)}, bf16[72,2048]{1,0:T(8,128)(2,1)S(1)}, u32[]{:S(2)}, u32[]{:S(2)}) collective-permute-start(bf16[72,2048]{1,0:T(8,128)(2,1)S(1)} %get-tuple-element.89), channel_id=1, source_target_pairs={{0,2},{1,3},{2,4},{3,5},{4,6},{5,7},{6,0},{7,1},{8,10},{9,11},{10,... | collective-permute-start | bytes 884744 | tf_op jit(solution)/shard_map/ppermute | solution.py:273
  68.2 9.7 %collective-permute-start.21 = (bf16[72,2048]{1,0:T(8,128)(2,1)S(1)}, bf16[72,2048]{1,0:T(8,128)(2,1)S(1)}, u32[]{:S(2)}, u32[]{:S(2)}) collective-permute-start(bf16[72,2048]{1,0:T(8,128)(2,1)S(1)} %get-tuple-element.92), channel_id=1, source_target_pairs={{0,2},{1,3},{2,4},{3,5},{4,6},{5,7},{6,0},{7,1},{8,10},{9,11},{10,... | collective-permute-start | bytes 884744 | tf_op jit(solution)/shard_map/ppermute | solution.py:273
  69.4 8.9 %collective-permute-start.25 = (bf16[72,2048]{1,0:T(8,128)(2,1)S(1)}, bf16[72,2048]{1,0:T(8,128)(2,1)S(1)}, u32[]{:S(2)}, u32[]{:S(2)}) collective-permute-start(bf16[72,2048]{1,0:T(8,128)(2,1)S(1)} %get-tuple-element.96), channel_id=1, source_target_pairs={{0,6},{1,7},{2,0},{3,1},{4,2},{5,3},{6,4},{7,5},{8,14},{9,15},{10,... | collective-permute-start | bytes 884744 | tf_op jit(solution)/shard_map/ppermute | solution.py:273
  71.5 10.9 %collective-permute-start.24 = (bf16[72,2048]{1,0:T(8,128)(2,1)S(1)}, bf16[72,2048]{1,0:T(8,128)(2,1)S(1)}, u32[]{:S(2)}, u32[]{:S(2)}) collective-permute-start(bf16[72,2048]{1,0:T(8,128)(2,1)S(1)} %get-tuple-element.95), channel_id=1, source_target_pairs={{0,6},{1,7},{2,0},{3,1},{4,2},{5,3},{6,4},{7,5},{8,14},{9,15},{10,... | collective-permute-start | bytes 884744 | tf_op jit(solution)/shard_map/ppermute | solution.py:273
  77.9 8.0 %collective-permute-start.23 = (bf16[72,2048]{1,0:T(8,128)(2,1)S(1)}, bf16[72,2048]{1,0:T(8,128)(2,1)S(1)}, u32[]{:S(2)}, u32[]{:S(2)}) collective-permute-start(bf16[72,2048]{1,0:T(8,128)(2,1)S(1)} %add_convert_fusion.3), channel_id=1, source_target_pairs={{0,2},{1,3},{2,4},{3,5},{4,6},{5,7},{6,0},{7,1},{8,10},{9,11},{10,... | collective-permute-start | bytes 884744 | tf_op jit(solution)/shard_map/ppermute | solution.py:273
  82.5 6.8 %collective-permute-start.26 = (bf16[72,2048]{1,0:T(8,128)(2,1)S(1)}, bf16[72,2048]{1,0:T(8,128)(2,1)S(1)}, u32[]{:S(2)}, u32[]{:S(2)}) collective-permute-start(bf16[72,2048]{1,0:T(8,128)(2,1)S(1)} %add_convert_fusion.2), channel_id=1, source_target_pairs={{0,6},{1,7},{2,0},{3,1},{4,2},{5,3},{6,4},{7,5},{8,14},{9,15},{10,... | collective-permute-start | bytes 884744 | tf_op jit(solution)/shard_map/ppermute | solution.py:273
  90.3 26.2 %copy-start = (bf16[256,4096]{1,0:T(8,128)(2,1)S(1)}, bf16[256,4096]{1,0:T(8,128)(2,1)}, u32[]{:S(2)}) copy-start(bf16[256,4096]{1,0:T(8,128)(2,1)} %tokens_ref.3) | copy-start | bytes 6291460
  90.6 25.9 %copy-start.1 = (f32[256,32]{0,1:T(8,128)S(1)}, f32[256,32]{0,1:T(8,128)}, u32[]{:S(2)}) copy-start(f32[256,32]{0,1:T(8,128)} %param.11) | copy-start | bytes 98308
  90.6 25.9 %copy-start.2 = (f32[32,384]{1,0:T(8,128)S(1)}, f32[32,384]{1,0:T(8,128)}, u32[]{:S(2)}) copy-start(f32[32,384]{1,0:T(8,128)} %gates_ref.1) | copy-start | bytes 147460
  90.6 25.9 %copy-start.3 = (s32[256]{0:T(256)S(1)}, s32[256]{0:T(256)}, u32[]{:S(2)}) copy-start(s32[256]{0:T(256)} %param.14) | copy-start | bytes 3076

commit v4 on v3

v4 whole, which is shorter than its diff:
```python
import functools

import jax
import jax.numpy as jnp
from jax import lax
from jax.experimental import pallas as pl
from jax.experimental.pallas import tpu as pltpu
from jax.sharding import PartitionSpec as P

BLOCK = 128
MOST = 3
PIECE = 512
BF16 = jnp.bfloat16
F32 = jnp.float32
I32 = jnp.int32
MIB = 1024 * 1024


def mul(a, b):
    return jnp.dot(a, b, preferred_element_type=F32)


def mul_t(a, b):
    return lax.dot_general(a, b, (((1,), (1,)), ((), ())), preferred_element_type=F32)


def iota(shape, dim):
    return lax.broadcasted_iota(I32, shape, dim)


def third(q):
    return lax.shift_right_logical(q * 11, 5)


def slots_of(index, base, tok_rows, gates=None):
    cap = index.shape[1]
    local = index - base
    mine = (local >= 0) & (local < tok_rows)
    upper = (iota((cap, cap), 0) <= iota((cap, cap), 1)).astype(F32).astype(BF16)
    rank = mul(mine.astype(F32).astype(BF16), upper)
    hot = []
    for s in range(MOST):
        hit = mine & (rank == float(s + 1))
        token = jnp.sum(jnp.where(hit, local + 1, 0), axis=1, keepdims=True) - 1
        here = iota((index.shape[0], tok_rows), 1) == token
        value = 1.0
        if gates is not None:
            value = jnp.sum(jnp.where(hit, gates, 0.0), axis=1, keepdims=True)
        hot.append(jnp.where(here, value, 0.0))
    return jnp.concatenate(hot, axis=0)


def scale_columns(rest):
    parts = []
    for _ in range(3):
        part = rest.astype(BF16).astype(F32)
        parts.append(part)
        rest = rest - part
    parts.append(jnp.zeros((BLOCK - 3 * rest.shape[0], rest.shape[1]), F32))
    return jnp.transpose(jnp.concatenate(parts, axis=0)).astype(BF16)


def scaled_piece(tokens, column, first, blocks):
    shape = (BLOCK, tokens.shape[1])
    lane = iota(shape, 0)
    third_of = (lane >= blocks).astype(I32) + (lane >= 2 * blocks).astype(I32)
    block = first + lax.shift_right_logical(iota(shape, 1), BLOCK.bit_length() - 1)
    spread = (lane - third_of * blocks == block) & (lane < 3 * blocks)
    scale = mul(column, jnp.where(spread, 1.0, 0.0).astype(BF16))
    return (tokens.astype(F32) * scale).astype(BF16)


def put_piece(wide_ref, piece, experts, value):
    per = wide_ref.shape[1] // experts
    for s in range(MOST):
        at = pl.ds(piece * MOST + s, experts, stride=per)
        for q in range(PIECE // BLOCK):
            wide_ref[q, at, :] = value[
                s * experts : (s + 1) * experts, q * BLOCK : (q + 1) * BLOCK
            ]


def get_piece(wide_ref, piece, experts):
    per = wide_ref.shape[1] // experts
    lanes = []
    for q in range(PIECE // BLOCK):
        lanes.append(
            jnp.concatenate(
                [
                    wide_ref[q, pl.ds(piece * MOST + s, experts, stride=per), :]
                    for s in range(MOST)
                ],
                axis=0,
            )
        )
    return jnp.concatenate(lanes, axis=1).astype(BF16)


def narrow_raw(wide_ref, out_ref):
    for q in range(PIECE // BLOCK):
        out_ref[:, q * BLOCK : (q + 1) * BLOCK] = wide_ref[q].astype(BF16)


def widen_raw(raw_ref, wide_ref):
    for q in range(PIECE // BLOCK):
        wide_ref[q] = raw_ref[:, q * BLOCK : (q + 1) * BLOCK].astype(F32)


def first_token(tok_rows):
    rank = lax.axis_index("wide") * lax.axis_size("narrow") + lax.axis_index("narrow")
    return rank * tok_rows


def most_rows(index, tok_rows, n_narrow):
    narrow = lax.shift_right_logical(index, tok_rows.bit_length() - 1) & (n_narrow - 1)
    most = jnp.zeros((index.shape[0], 1), F32)
    for n in range(n_narrow):
        held = jnp.sum(jnp.where(narrow == n, 1.0, 0.0), axis=1, keepdims=True)
        most = jnp.maximum(most, held)
    return jnp.max(most, axis=0, keepdims=True).astype(I32)


def dispatch_kernel(index_ref, scales_ref, tokens_ref, out_ref, most_ref, held_ref, raw_ref, sems):
    experts = index_ref.shape[0]
    chunks, tok_rows, chunk = held_ref.shape
    copies = []
    for k in range(chunks):
        part = tokens_ref.at[:, pl.ds(k * chunk, chunk)]
        copies.append(pltpu.make_async_copy(part, held_ref.at[k], sems.at[k]))
        copies[k].start()
    hot = slots_of(index_ref[...], first_token(tok_rows), tok_rows).astype(BF16)
    column = scale_columns(scales_ref[...])
    blocks = scales_ref.shape[0]
    most_ref[...] = most_rows(index_ref[...], tok_rows, lax.axis_size("narrow"))
    for k in range(chunks):
        copies[k].wait()
        picked = mul(hot, scaled_piece(held_ref[k], column, k * (chunk // BLOCK), blocks))
        for j in range(chunk // PIECE):
            piece = picked[:, j * PIECE : (j + 1) * PIECE]
            put_piece(raw_ref, k * (chunk // PIECE) + j, experts, piece)
    narrow_raw(raw_ref, out_ref)


def prepare_kernel(index_ref, gates_ref, counts_ref, scales_ref, tokens_ref, rows_ref, weight_ref):
    tok_rows, width = tokens_ref.shape
    weight = slots_of(index_ref[...], first_token(tok_rows), tok_rows, gates_ref[...])
    weight = weight / jnp.maximum(counts_ref[...], 1).astype(F32)
    high = weight.astype(BF16).astype(F32)
    both = jnp.concatenate([high, weight - high], axis=0)
    weight_ref[...] = jnp.transpose(both).astype(BF16)
    column = scale_columns(scales_ref[...])
    blocks = scales_ref.shape[0]
    for k in range(width // PIECE):
        cols = slice(k * PIECE, (k + 1) * PIECE)
        first = k * (PIECE // BLOCK)
        rows_ref[:, cols] = scaled_piece(tokens_ref[:, cols], column, first, blocks)


def row_places(index_ref, tok_rows, first_row, rows):
    wide, cap = index_ref.shape
    n_narrow = lax.axis_size("narrow")
    mine = index_ref[pl.ds(lax.axis_index("wide"), 1), :]
    first = (iota((wide, cap), 0) * n_narrow + lax.axis_index("narrow")) * tok_rows
    inside = jnp.where((mine >= first) & (mine < first + tok_rows), 1.0, 0.0).astype(BF16)
    counts = mul_t(jnp.ones((8, cap), BF16), inside).astype(BF16)
    n = iota((wide, MOST * wide), 1)
    slot = (n >= wide).astype(I32) + (n >= 2 * wide).astype(I32)
    of, at = n - slot * wide, iota((wide, MOST * wide), 0)
    count = mul(counts, jnp.where(at == of, 1.0, 0.0).astype(BF16))[0:1]
    before = mul(counts, jnp.where(at < of, 1.0, 0.0).astype(BF16))[0:1]
    slot = slot[0:1].astype(F32)
    place = jnp.where(slot < count, before + slot, -1.0)
    hot = (iota((rows, MOST * wide), 0) + first_row).astype(F32) == place
    return jnp.where(hot, 1.0, 0.0).astype(BF16)


def unpack_kernel(tok_rows, first_row, index_ref, raw_ref, *refs):
    out_refs, wide_ref = refs[:-1], refs[-1]
    rows, half = out_refs[0].shape
    wide = index_ref.shape[0]
    widen_raw(raw_ref, wide_ref)
    places = row_places(index_ref, tok_rows, first_row, rows)
    for j in range(2 * half // PIECE):
        at = j * PIECE % half
        value = mul(places, get_piece(wide_ref, j, wide)).astype(BF16)
        out_refs[j * PIECE // half][:, at : at + PIECE] = value


def expert_kernel(blocks, hold, *refs):
    xs, weights, outs = refs[: 2 * blocks], refs[2 * blocks : 2 * blocks + 6], refs[2 * blocks + 6 :]
    if hold:
        away, weights, sems = weights, outs[2 * blocks : -1], outs[-1]
        copies = [pltpu.make_async_copy(away[k], weights[k], sems.at[k]) for k in range(6)]
        for copy in copies:
            copy.start()
    left = jnp.concatenate([x[...] for x in xs[0::2]], axis=0)
    right = jnp.concatenate([x[...] for x in xs[1::2]], axis=0)
    rows, half = outs[0].shape
    hidden = []
    for k in (0, 2):
        gate_w, up_w = weights[k : k + 2]
        if hold:
            copies[k].wait()
            copies[k + 1].wait()
        v = mul_t(gate_w[:, :half], left) + mul_t(gate_w[:, half:], right)
        u = mul_t(up_w[:, :half], left) + mul_t(up_w[:, half:], right)
        hidden.append(jnp.transpose(v / (1.0 + jnp.exp(-v)) * u).astype(BF16))
    if hold:
        copies[4].wait()
        copies[5].wait()
    for c in range(2 * half // PIECE):
        cols = slice(c * PIECE, (c + 1) * PIECE)
        part = mul(hidden[0], weights[4][:, cols]) + mul(hidden[1], weights[5][:, cols])
        at = c * PIECE % half
        for b in range(blocks):
            out = outs[2 * b + c * PIECE // half]
            out[:, at : at + PIECE] = part[b * rows : (b + 1) * rows].astype(out.dtype)


def expert(xs, weights, out_types, hold=False):
    rows, half = xs[0][0].shape
    blocks = len(xs)
    args = [x for pair in xs for x in pair] + list(weights)
    vmem = pl.BlockSpec(memory_space=pltpu.VMEM)
    out_shape = [jax.ShapeDtypeStruct((rows, half), t) for t in out_types]
    scratch = []
    if hold:
        out_shape += [jax.ShapeDtypeStruct(w.shape, BF16) for w in weights]
        scratch = [pltpu.SemaphoreType.DMA((6,))]
    return pl.pallas_call(
        functools.partial(expert_kernel, blocks, hold),
        in_specs=[vmem] * (2 * blocks) + [pl.BlockSpec(memory_space=pl.ANY) if hold else vmem] * 6,
        out_specs=[vmem] * len(out_shape),
        out_shape=out_shape,
        scratch_shapes=scratch,
        compiler_params=pltpu.CompilerParams(vmem_limit_bytes=30 * MIB),
        cost_estimate=pl.CostEstimate(flops=1, bytes_accessed=1, transcendentals=0),
    )(*args)


def pack_kernel(tok_rows, index_ref, *refs):
    parts, late, out_ref, raw_ref = refs[:6], refs[6:8], refs[8], refs[9]
    rows, half = parts[0].shape
    wide = index_ref.shape[0]
    places = row_places(index_ref, tok_rows, 0, rows + late[0].shape[0])
    places = jnp.transpose(places.astype(F32)).astype(BF16)
    for j in range(2 * half // PIECE):
        side, at = j * PIECE // half, j * PIECE % half
        cols = slice(at, at + PIECE)
        summed = sum(p[:, cols].astype(F32) for p in parts[side::2])
        summed = jnp.concatenate([summed, late[side][:, cols].astype(F32)], axis=0)
        put_piece(raw_ref, j, wide, mul(places, summed.astype(BF16)))
    narrow_raw(raw_ref, out_ref)


def combine_kernel(weight_ref, raw_ref, rows_ref, out_ref, held_ref, wide_ref, sems):
    chunks, tok_rows, chunk = held_ref.shape
    experts = weight_ref.shape[1] // (2 * MOST)
    widen_raw(raw_ref, wide_ref)
    weight = weight_ref[...]
    copies = []
    for k in range(chunks):
        for j in range(chunk // PIECE):
            got = get_piece(wide_ref, k * (chunk // PIECE) + j, experts)
            branch = mul(weight, jnp.concatenate([got, got], axis=0))
            at = k * chunk + j * PIECE
            rows = rows_ref[:, at : at + PIECE].astype(F32)
            held_ref[k, :, j * PIECE : (j + 1) * PIECE] = (rows + branch).astype(BF16)
        part = out_ref.at[:, pl.ds(k * chunk, chunk)]
        copies.append(pltpu.make_async_copy(held_ref.at[k], part, sems.at[k]))
        copies[k].start()
    for copy in copies:
        copy.wait()


def along_y(x, step):
    n = lax.axis_size("narrow")
    return lax.ppermute(x, "narrow", [(i, (i + 2 * step) % n) for i in range(n)])


def around_y(first_row, rows, tok_rows, arrived, pick_index, own, sibling):
    total = arrived.shape[0]
    width = own[2].shape[1]
    vmem = pl.BlockSpec(memory_space=pltpu.VMEM)
    raw_f32 = pltpu.VMEM((PIECE // BLOCK, total, BLOCK), F32)
    half_shape = jax.ShapeDtypeStruct((rows, width // 2), BF16)
    x0 = pl.pallas_call(
        functools.partial(unpack_kernel, tok_rows, first_row),
        in_specs=[vmem] * 2,
        out_specs=[vmem, vmem],
        out_shape=[half_shape, half_shape],
        scratch_shapes=[raw_f32],
        compiler_params=pltpu.CompilerParams(vmem_limit_bytes=24 * MIB),
    )(pick_index, arrived)

    xm, xp = [along_y(x0[0], 1), None], [None, along_y(x0[1], -1)]
    xm[1] = along_y(x0[1], 1)
    xp[0] = along_y(x0[0], -1)
    x2 = (along_y(xm[0], 1), along_y(xp[1], -1))

    weights = (own[0], own[1], sibling[0], sibling[1], own[2], sibling[2])
    *p0, w0, w1, w2, w3, w4, w5 = expert([x0], weights, (F32, F32), hold=True)
    weights = (w0, w1, w2, w3, w4, w5)
    xp[0], xp[1], xm[0], xm[1] = lax.optimization_barrier((*xp, *xm, p0[0]))[:4]
    pp_a, pp_b, pm_a, pm_b = expert([xp, xm], weights, (F32, BF16, BF16, F32))
    x2 = lax.optimization_barrier((*x2, pp_b))[:2]
    p2 = expert([x2], weights, (BF16, BF16))
    got_mb = along_y(pp_b, 1)
    got_pa = along_y(pm_a, -1)
    from_m = along_y(p2[0], 1)
    from_p = along_y(p2[1], -1)
    from_m, got_mb, got_pa = lax.optimization_barrier((from_m, got_mb, got_pa))
    got_ma = along_y((pp_a + from_m.astype(F32)).astype(BF16), 1)
    got_pb = along_y((pm_b + from_p.astype(F32)).astype(BF16), -1)
    return p0[0], p0[1], got_ma, got_mb, got_pa, got_pb


def local(
    tokens, block_scales, pick_index, pick_gates, pick_counts, gate_weight, up_weight, down_weight
):
    tok_rows, width = tokens.shape
    n_wide = lax.axis_size("wide")
    n_narrow = lax.axis_size("narrow")
    other_core = [(i, i ^ 1) for i in range(n_narrow)]
    per = MOST * (width // PIECE)
    total = n_wide * per
    scales = block_scales.T
    chunk = 2 * PIECE
    chunks = width // chunk
    vmem = pl.BlockSpec(memory_space=pltpu.VMEM)
    anywhere = pl.BlockSpec(memory_space=pl.ANY)

    own = (gate_weight[0].T, up_weight[0].T, down_weight[0])
    sibling = tuple(lax.ppermute(v, "narrow", other_core) for v in own)

    raw_shape = jax.ShapeDtypeStruct((total, PIECE), BF16)
    raw_f32 = pltpu.VMEM((PIECE // BLOCK, total, BLOCK), F32)
    held = pltpu.VMEM((chunks, tok_rows, chunk), BF16)
    sems = pltpu.SemaphoreType.DMA((chunks,))
    outgoing, most = pl.pallas_call(
        dispatch_kernel,
        in_specs=[vmem, vmem, anywhere],
        out_specs=[vmem, vmem],
        out_shape=[raw_shape, jax.ShapeDtypeStruct((1, 1), I32)],
        scratch_shapes=[held, raw_f32, sems],
        compiler_params=pltpu.CompilerParams(vmem_limit_bytes=56 * MIB),
    )(pick_index, scales, tokens)

    def exchange(raw):
        raw = raw.reshape(n_wide, per, PIECE)
        raw = lax.all_to_all(raw, "wide", split_axis=0, concat_axis=0, tiled=True)
        return raw.reshape(total, PIECE)

    slots = MOST * n_wide
    rows_out, weight = pl.pallas_call(
        prepare_kernel,
        in_specs=[vmem] * 5,
        out_specs=[vmem] * 2,
        out_shape=[
            jax.ShapeDtypeStruct((tok_rows, width), BF16),
            jax.ShapeDtypeStruct((tok_rows, 2 * slots), BF16),
        ],
        compiler_params=pltpu.CompilerParams(vmem_limit_bytes=24 * MIB),
    )(pick_index, pick_gates, pick_counts.reshape(1, tok_rows), scales, tokens)

    arrived = exchange(outgoing)
    arrived, weight = lax.optimization_barrier((arrived, weight))
    rows = slots * 3 // 4
    parts = around_y(0, rows, tok_rows, arrived, pick_index, own, sibling)

    def second(arrived):
        late = around_y(rows, slots - rows, tok_rows, arrived, pick_index, own, sibling)
        return [sum(p.astype(F32) for p in late[side::2]).astype(BF16) for side in (0, 1)]

    def none(arrived):
        return [jnp.zeros((slots - rows, width // 2), BF16)] * 2

    arrived, *parts = lax.optimization_barrier((arrived, *parts))
    late = lax.cond(most[0, 0] > rows, second, none, arrived)
    packed = pl.pallas_call(
        functools.partial(pack_kernel, tok_rows),
        in_specs=[vmem] * 9,
        out_specs=vmem,
        out_shape=raw_shape,
        scratch_shapes=[raw_f32],
        compiler_params=pltpu.CompilerParams(vmem_limit_bytes=32 * MIB),
    )(pick_index, *parts, *late)
    returned = exchange(packed)
    return pl.pallas_call(
        combine_kernel,
        in_specs=[vmem] * 3,
        out_specs=anywhere,
        out_shape=jax.ShapeDtypeStruct((tok_rows, width), BF16),
        scratch_shapes=[held, raw_f32, sems],
        compiler_params=pltpu.CompilerParams(vmem_limit_bytes=24 * MIB),
    )(weight, returned, rows_out)


def solution(mesh):
    return jax.shard_map(
        local,
        mesh=mesh,
        in_specs=(
            P(("wide", "narrow"), None),
            P(("wide", "narrow"), None),
            P(),
            P(),
            P(("wide", "narrow")),
            P("wide", None, "narrow"),
            P("wide", None, "narrow"),
            P("wide", "narrow", None),
        ),
        out_specs=P(("wide", "narrow"), None),
        check_vma=False,
    )
```

time: 121 us -> 112 us (0.926)
  Pallas kernels: 23.2 us -> 18.8 us
  blocking collectives: 25.8 us -> 21.7 us
  waiting for transfers between devices: 39.8 us -> 36.4 us
  starting transfers between devices: 29.8 us -> 31.3 us
  local copies, waits for them, and re-layouts: 0.04 us -> 1.38 us
    all_to_all x1, blocking collectives: 25.8 us -> 21.7 us  [exchange(): raw = lax.all_to_all(raw, 'wide', split_axis=0, concat_axis=0, tiled=True)]
    pallas_call x6 -> x7, Pallas kernels: 21.4 us -> 18.1 us  [the longest x3 9.76 us: expert(): pl.pallas_call(functools.partial(expert_kernel, blocks, hold), in_specs=[...]
    all_to_all x1, waiting for transfers between devices: 22.5 us -> 20.4 us  [exchange(): raw = lax.all_to_all(raw, 'wide', split_axis=0, concat_axis=0, tiled=True)]
    ppermute x12, starting transfers between devices: 17.9 us -> 19.5 us  [along_y(): lax.ppermute(x, 'narrow', [(i, (i + 2 * step) % n) for i in range(n)])]
    unnamed x16 -> x20, local copies, waits for them, and re-layouts: 0.04 us -> 1.36 us
    ppermute x12, waiting for transfers between devices: 17.3 us -> 16.1 us  [along_y(): lax.ppermute(x, 'narrow', [(i, (i + 2 * step) % n) for i in range(n)])]
  transfers between devices with their start and end apart: 16 -> 16, of which waited for: 7 -> 5; matrix products, arithmetic and copies ran while one was open for 0% -> 0% of each run, Pallas kernels for 11% -> 10%
where the time goes in v4:
time: 112 us; the launch traced here: 111 us
  waiting for transfers between devices  36.4 us (32%)
  starting transfers between devices  31.3 us (28%)
  blocking collectives  21.7 us (19%)
  Pallas kernels  18.8 us (17%)
  local copies, waits for them, and re-layouts  1.38 us (1%)
    all_to_all x1, blocking collectives, exchange(): raw = lax.all_to_all(raw, 'wide', split_axis=0, concat_axis=0, tiled=True)  21.7 us
    all_to_all x1, waiting for transfers between devices, exchange(): raw = lax.all_to_all(raw, 'wide', split_axis=0, concat_axis=0, tiled=True)  20.4 us
    ppermute x12, starting transfers between devices, along_y(): lax.ppermute(x, 'narrow', [(i, (i + 2 * step) % n) for i in range(n)])  19.5 us
    ppermute x12, waiting for transfers between devices, along_y(): lax.ppermute(x, 'narrow', [(i, (i + 2 * step) % n) for i in range(n)])  16.1 us
    all_to_all x1, starting transfers between devices, exchange(): raw = lax.all_to_all(raw, 'wide', split_axis=0, concat_axis=0, tiled=True)  11.2 us
    pallas_call x3, Pallas kernels, expert(): pl.pallas_call(functools.partial(expert_kernel, blocks, hold), in_specs=[...  9.76 us
    pallas_call x1, Pallas kernels, local(): pl.pallas_call(dispatch_kernel, in_specs=[vmem, vmem, anywhere], out_spec...  4.86 us
  transfers between devices with their start and end apart: 16, of which 5 were waited for; matrix products, arithmetic and copies ran while one was open for 0% of the time, Pallas kernels for 10%

profile of v4, /device:TPU:32, one launch (start us, length us, event | category | flops | bytes accessed | tf_op | source)
XLA Modules:
  0.0 110.9 jit_solution(9934500172259281455)
XLA Ops:
  0.0 0.0 copy-start
  0.0 0.0 copy-start.3
  0.0 0.0 copy-start.4
  0.0 0.0 copy-start.5
  0.0 0.0 copy-start.9
  0.0 4.9 %shard_map.82 = (bf16[768,512]{1,0:T(8,128)(2,1)}, s32[1,1]{1,0:T(1,128)}) custom-call(s32[32,384]{1,0:T(8,128)} %index_ref.7, f32[32,256]{1,0:T(8,128)} %bitcast.16, bf16[256,4096]{1,0:T(8,128)(2,1)} %tokens_ref.3), custom_call_target="tpu_custom_call" | custom-call | tf_op jit(solution)/shard_map/pallas_call | solution.py:340
  4.9 11.2 %all-to-all-start = ((bf16[32,24,512]{2,1,0:T(8,128)(2,1)}), bf16[32,24,512]{2,1,0:T(8,128)(2,1)S(1)}, u32[]{:S(2)}, u32[]{:S(2)}) async-start(bf16[32,24,512]{2,1,0:T(8,128)(2,1)} %bitcast.30), calls=%async_computation | async-start | bytes 1572864 | tf_op jit(solution)/shard_map/all_to_all | solution.py:351
  16.1 0.1 collective-permute-start.12
  16.2 0.5 collective-permute-start.13
  16.7 0.1 collective-permute-start.14
  16.8 0.0 copy-done
  16.8 0.0 copy-done.3
  16.8 0.0 copy-done.4
  16.8 0.0 copy-done.5
  16.8 0.0 copy-done.9
  16.8 0.8 shard_map.83
  17.6 0.0 copy-start.1
  17.6 1.3 %copy-done.1 = bf16[256,4096]{1,0:T(8,128)(2,1)} copy-done((bf16[256,4096]{1,0:T(8,128)(2,1)}, bf16[256,4096]{1,0:T(8,128)(2,1)S(1)}, u32[]{:S(2)}) %copy-start.1) | copy-done | bytes 2097176
  18.9 20.4 %all-to-all-done = bf16[32,24,512]{2,1,0:T(8,128)(2,1)S(1)} async-done(((bf16[32,24,512]{2,1,0:T(8,128)(2,1)}), bf16[32,24,512]{2,1,0:T(8,128)(2,1)S(1)}, u32[]{:S(2)}, u32[]{:S(2)}) %all-to-all-start) | async-done | bytes 786464 | tf_op jit(solution)/shard_map/all_to_all | solution.py:351
  39.3 0.7 shard_map.84
  39.9 1.7 %collective-permute-start.17 = (bf16[72,2048]{1,0:T(8,128)(2,1)S(1)}, bf16[72,2048]{1,0:T(8,128)(2,1)S(1)}, u32[]{:S(2)}, u32[]{:S(2)}) collective-permute-start(bf16[72,2048]{1,0:T(8,128)(2,1)S(1)} %get-tuple-element.98.refs_0_), channel_id=1, source_target_pairs={{0,2},{1,3},{2,4},{3,5},{4,6},{5,7},{6,0},{7,1},{8,10},{9,11},{10,... | collective-permute-start | bytes 884744 | tf_op jit(solution)/shard_map/ppermute | solution.py:278
  41.6 1.7 %collective-permute-start.16 = (bf16[72,2048]{1,0:T(8,128)(2,1)S(1)}, bf16[72,2048]{1,0:T(8,128)(2,1)S(1)}, u32[]{:S(2)}, u32[]{:S(2)}) collective-permute-start(bf16[72,2048]{1,0:T(8,128)(2,1)S(1)} %get-tuple-element.99.refs_1_), channel_id=1, source_target_pairs={{0,6},{1,7},{2,0},{3,1},{4,2},{5,3},{6,4},{7,5},{8,14},{9,15},{10,... | collective-permute-start | bytes 884744 | tf_op jit(solution)/shard_map/ppermute | solution.py:278
  43.3 0.0 collective-permute-done.12.refs_4_
  43.3 1.8 %collective-permute-start.15 = (bf16[72,2048]{1,0:T(8,128)(2,1)S(1)}, bf16[72,2048]{1,0:T(8,128)(2,1)S(1)}, u32[]{:S(2)}, u32[]{:S(2)}) collective-permute-start(bf16[72,2048]{1,0:T(8,128)(2,1)S(1)} %get-tuple-element.98.refs_0_), channel_id=1, source_target_pairs={{0,6},{1,7},{2,0},{3,1},{4,2},{5,3},{6,4},{7,5},{8,14},{9,15},{10,... | collective-permute-start | bytes 884744 | tf_op jit(solution)/shard_map/ppermute | solution.py:278
  45.1 0.0 collective-permute-done.13.refs_5_
  45.1 0.2 collective-permute-start.18
  45.3 5.0 %collective-permute-done.17.refs_2_ = bf16[72,2048]{1,0:T(8,128)(2,1)S(1)} collective-permute-done((bf16[72,2048]{1,0:T(8,128)(2,1)S(1)}, bf16[72,2048]{1,0:T(8,128)(2,1)S(1)}, u32[]{:S(2)}, u32[]{:S(2)}) %collective-permute-start.17) | collective-permute-done | bytes 294944 | tf_op jit(solution)/shard_map/ppermute | solution.py:278
  50.3 1.2 %collective-permute-start.19 = (bf16[72,2048]{1,0:T(8,128)(2,1)S(1)}, bf16[72,2048]{1,0:T(8,128)(2,1)S(1)}, u32[]{:S(2)}, u32[]{:S(2)}) collective-permute-start(bf16[72,2048]{1,0:T(8,128)(2,1)S(1)} %collective-permute-done.17.refs_2_), channel_id=1, source_target_pairs={{0,2},{1,3},{2,4},{3,5},{4,6},{5,7},{6,0},{7,1},{8,10},{9,11},{10,... | collective-permute-start | bytes 884744 | tf_op jit(solution)/shard_map/ppermute | solution.py:278
  51.6 0.0 collective-permute-done.16.refs_1_
  51.6 2.9 %collective-permute-start.20 = (bf16[72,2048]{1,0:T(8,128)(2,1)S(1)}, bf16[72,2048]{1,0:T(8,128)(2,1)S(1)}, u32[]{:S(2)}, u32[]{:S(2)}) collective-permute-start(bf16[72,2048]{1,0:T(8,128)(2,1)S(1)} %collective-permute-done.16.refs_1_), channel_id=1, source_target_pairs={{0,6},{1,7},{2,0},{3,1},{4,2},{5,3},{6,4},{7,5},{8,14},{9,15},{10,... | collective-permute-start | bytes 884744 | tf_op jit(solution)/shard_map/ppermute | solution.py:278
  54.4 0.0 collective-permute-done.14.refs_7_
  54.4 4.7 %shard_map.85 = (f32[72,2048]{1,0:T(8,128)S(1)}, f32[72,2048]{1,0:T(8,128)S(1)}, bf16[192,4096]{1,0:T(8,128)(2,1)S(1)}, bf16[192,4096]{1,0:T(8,128)(2,1)S(1)}, b...) custom-call(bf16[72,2048]{1,0:T(8,128)(2,1)S(1)} %get-tuple-element., ...), custom_call_target="tpu_custom_call" | custom-call | flops 1 | bytes 1 | tf_op jit(solution)/shard_map/pallas_call | solution.py:230
  59.1 0.0 collective-permute-done.15.refs_0_
  59.1 0.0 collective-permute-done.18.refs_3_
  59.1 2.6 %shard_map.86 = (f32[72,2048]{1,0:T(8,128)S(1)}, bf16[72,2048]{1,0:T(8,128)(2,1)S(1)}, bf16[72,2048]{1,0:T(8,128)(2,1)S(1)}, f32[72,2048]{1,0:T(8,128)S(1)}) custom-call(bf16[72,2048]{1,0:T(8,128)(2,1)S(1)} %collective-permute-done.15.refs_0_, bf16[72,2048]{1,0:T(8,128)(2,1)S(1)} %collective-permute-done.16.refs_1_, ...), custom_call_target="tpu_custom_call" | custom-call | flops 1 | bytes 1 | tf_op jit(solution)/shard_map/pallas_call | solution.py:230
  61.7 0.3 collective-permute-start.22
  62.0 3.1 %collective-permute-start.23 = (bf16[72,2048]{1,0:T(8,128)(2,1)S(1)}, bf16[72,2048]{1,0:T(8,128)(2,1)S(1)}, u32[]{:S(2)}, u32[]{:S(2)}) collective-permute-start(bf16[72,2048]{1,0:T(8,128)(2,1)S(1)} %get-tuple-element.117), channel_id=1, source_target_pairs={{0,6},{1,7},{2,0},{3,1},{4,2},{5,3},{6,4},{7,5},{8,14},{9,15},{10,... | collective-permute-start | bytes 884744 | tf_op jit(solution)/shard_map/ppermute | solution.py:278
  65.1 0.0 collective-permute-done.19.refs_0_
  65.1 0.0 collective-permute-done.20.refs_1_
  65.1 0.0 copy-start.7
  65.1 0.0 copy-start.8
  65.1 2.5 %shard_map.87 = (bf16[72,2048]{1,0:T(8,128)(2,1)S(1)}, bf16[72,2048]{1,0:T(8,128)(2,1)S(1)}) custom-call(bf16[72,2048]{1,0:T(8,128)(2,1)S(1)} %collective-permute-done.19.refs_0_, bf16[72,2048]{1,0:T(8,128)(2,1)S(1)} %collective-permute-done.20.refs_1_, bf16[192,4096]{1,0:T(8,128)(2,1)S(1)} %get-tuple-element.106.refs_4_.refs_2_, ...), custom_call_target="tpu_custom_call" | custom-call | flops 1 | bytes 1 | tf_op jit(solution)/shard_map/pallas_call | solution.py:230
  67.6 0.0 copy-start.6
  67.6 0.6 collective-permute-start.21
  68.2 2.7 %collective-permute-start.25 = (bf16[72,2048]{1,0:T(8,128)(2,1)S(1)}, bf16[72,2048]{1,0:T(8,128)(2,1)S(1)}, u32[]{:S(2)}, u32[]{:S(2)}) collective-permute-start(bf16[72,2048]{1,0:T(8,128)(2,1)S(1)} %get-tuple-element.122), channel_id=1, source_target_pairs={{0,6},{1,7},{2,0},{3,1},{4,2},{5,3},{6,4},{7,5},{8,14},{9,15},{10,... | collective-permute-start | bytes 884744 | tf_op jit(solution)/shard_map/ppermute | solution.py:278
  70.9 0.2 collective-permute-done.22.refs_3_
  71.1 0.0 collective-permute-done.23.refs_4_
  71.1 7.0 %collective-permute-done.21 = bf16[72,2048]{1,0:T(8,128)(2,1)S(1)} collective-permute-done((bf16[72,2048]{1,0:T(8,128)(2,1)S(1)}, bf16[72,2048]{1,0:T(8,128)(2,1)S(1)}, u32[]{:S(2)}, u32[]{:S(2)}) %collective-permute-start.21) | collective-permute-done | bytes 294944 | tf_op jit(solution)/shard_map/ppermute | solution.py:278
  78.0 0.1 add_convert_fusion.5
  78.1 0.1 collective-permute-start.24
  78.2 0.0 collective-permute-done.25
  78.2 0.1 add_convert_fusion.4
  78.3 3.3 %collective-permute-start.26 = (bf16[72,2048]{1,0:T(8,128)(2,1)S(1)}, bf16[72,2048]{1,0:T(8,128)(2,1)S(1)}, u32[]{:S(2)}, u32[]{:S(2)}) collective-permute-start(bf16[72,2048]{1,0:T(8,128)(2,1)S(1)} %add_convert_fusion.4), channel_id=1, source_target_pairs={{0,6},{1,7},{2,0},{3,1},{4,2},{5,3},{6,4},{7,5},{8,14},{9,15},{10,... | collective-permute-start | bytes 884744 | tf_op jit(solution)/shard_map/ppermute | solution.py:278
  82.2 3.9 %collective-permute-done.24.refs_2_ = bf16[72,2048]{1,0:T(8,128)(2,1)S(1)} collective-permute-done((bf16[72,2048]{1,0:T(8,128)(2,1)S(1)}, bf16[72,2048]{1,0:T(8,128)(2,1)S(1)}, u32[]{:S(2)}, u32[]{:S(2)}) %collective-permute-start.24) | collective-permute-done | bytes 294944 | tf_op jit(solution)/shard_map/ppermute | solution.py:278
  86.1 0.0 collective-permute-done.26.refs_5_
  86.1 0.0 copy-done.7
  86.1 0.0 copy-done.8
  86.1 0.0 copy-done.6
  86.2 0.0 copy-start.2
  86.2 1.0 shard_map.88
  87.2 21.7 %all_to_all.10 = bf16[32,24,512]{2,1,0:T(8,128)(2,1)S(1)} all-to-all(bf16[32,24,512]{2,1,0:T(8,128)(2,1)S(1)} %bitcast.15), channel_id=1, replica_groups=mesh['wide'=32,'narrow'=8] {'wide'}, dimensions={0} | all-to-all | bytes 1572864 | tf_op jit(solution)/shard_map/all_to_all | solution.py:351
  109.0 0.0 copy-done.2
  109.0 1.8 %shard_map.89 = bf16[256,4096]{1,0:T(8,128)(2,1)} custom-call(bf16[256,192]{1,0:T(8,128)(2,1)S(1)} %get-tuple-element.96.weight_ref, bf16[768,512]{1,0:T(8,128)(2,1)S(1)} %bitcast.14, bf16[256,4096]{1,0:T(8,128)(2,1)S(1)} %copy-done.2), custom_call_target="tpu_custom_call" | custom-call | tf_op jit(solution)/shard_map/pallas_call | solution.py:389
  (3 shorter events, 0.1 us)
Async XLA Ops:
  0.0 16.8 %copy-start = (bf16[256,4096]{1,0:T(8,128)(2,1)S(1)}, bf16[256,4096]{1,0:T(8,128)(2,1)}, u32[]{:S(2)}) copy-start(bf16[256,4096]{1,0:T(8,128)(2,1)} %tokens_ref.3) | copy-start | bytes 6291460
  0.0 16.8 %copy-start.3 = (f32[256,32]{0,1:T(8,128)S(1)}, f32[256,32]{0,1:T(8,128)}, u32[]{:S(2)}) copy-start(f32[256,32]{0,1:T(8,128)} %param.11) | copy-start | bytes 98308
  0.0 16.8 %copy-start.4 = (f32[32,384]{1,0:T(8,128)S(1)}, f32[32,384]{1,0:T(8,128)}, u32[]{:S(2)}) copy-start(f32[32,384]{1,0:T(8,128)} %gates_ref.1) | copy-start | bytes 147460
  0.0 16.8 %copy-start.5 = (s32[256]{0:T(256)S(1)}, s32[256]{0:T(256)}, u32[]{:S(2)}) copy-start(s32[256]{0:T(256)} %param.14) | copy-start | bytes 3076
  0.0 16.8 %copy-start.9 = (s32[32,384]{1,0:T(8,128)S(1)}, s32[32,384]{1,0:T(8,128)}, u32[]{:S(2)}) copy-start(s32[32,384]{1,0:T(8,128)} %index_ref.7) | copy-start | bytes 147460
  4.9 34.4 %all-to-all-start = ((bf16[32,24,512]{2,1,0:T(8,128)(2,1)}), bf16[32,24,512]{2,1,0:T(8,128)(2,1)S(1)}, u32[]{:S(2)}, u32[]{:S(2)}) async-start(bf16[32,24,512]{2,1,0:T(8,128)(2,1)} %bitcast.30), calls=%async_computation | async-start | bytes 1572864 | tf_op jit(solution)/shard_map/all_to_all | solution.py:351
  16.1 27.2 %collective-permute-start.12 = (bf16[192,4096]{1,0:T(8,128)(2,1)}, bf16[192,4096]{1,0:T(8,128)(2,1)}, u32[]{:S(2)}, u32[]{:S(2)}) collective-permute-start(bf16[192,4096]{1,0:T(8,128)(2,1)} %bitcast.21), channel_id=1, source_target_pairs={{0,1},{1,0},{2,3},{3,2},{4,5},{5,4},{6,7},{7,6},{8,9},{9,8},{10,11... | collective-permute-start | bytes 4718600 | tf_op jit(solution)/shard_map/ppermute | solution.py:334
  16.2 28.9 %collective-permute-start.13 = (bf16[192,4096]{1,0:T(8,128)(2,1)}, bf16[192,4096]{1,0:T(8,128)(2,1)}, u32[]{:S(2)}, u32[]{:S(2)}) collective-permute-start(bf16[192,4096]{1,0:T(8,128)(2,1)} %bitcast.24), channel_id=1, source_target_pairs={{0,1},{1,0},{2,3},{3,2},{4,5},{5,4},{6,7},{7,6},{8,9},{9,8},{10,11... | collective-permute-start | bytes 4718600 | tf_op jit(solution)/shard_map/ppermute | solution.py:334
  16.7 37.7 %collective-permute-start.14 = (bf16[192,4096]{1,0:T(8,128)(2,1)}, bf16[192,4096]{1,0:T(8,128)(2,1)}, u32[]{:S(2)}, u32[]{:S(2)}) collective-permute-start(bf16[192,4096]{1,0:T(8,128)(2,1)} %bitcast.27), channel_id=1, source_target_pairs={{0,1},{1,0},{2,3},{3,2},{4,5},{5,4},{6,7},{7,6},{8,9},{9,8},{10,11... | collective-permute-start | bytes 4718600 | tf_op jit(solution)/shard_map/ppermute | solution.py:334
  17.6 1.3 %copy-start.1 = (bf16[256,4096]{1,0:T(8,128)(2,1)}, bf16[256,4096]{1,0:T(8,128)(2,1)S(1)}, u32[]{:S(2)}) copy-start(bf16[256,4096]{1,0:T(8,128)(2,1)S(1)} %get-tuple-element.133.rows_ref) | copy-start | bytes 6291460
  39.9 10.4 %collective-permute-start.17 = (bf16[72,2048]{1,0:T(8,128)(2,1)S(1)}, bf16[72,2048]{1,0:T(8,128)(2,1)S(1)}, u32[]{:S(2)}, u32[]{:S(2)}) collective-permute-start(bf16[72,2048]{1,0:T(8,128)(2,1)S(1)} %get-tuple-element.98.refs_0_), channel_id=1, source_target_pairs={{0,2},{1,3},{2,4},{3,5},{4,6},{5,7},{6,0},{7,1},{8,10},{9,11},{10,... | collective-permute-start | bytes 884744 | tf_op jit(solution)/shard_map/ppermute | solution.py:278
  41.6 10.0 %collective-permute-start.16 = (bf16[72,2048]{1,0:T(8,128)(2,1)S(1)}, bf16[72,2048]{1,0:T(8,128)(2,1)S(1)}, u32[]{:S(2)}, u32[]{:S(2)}) collective-permute-start(bf16[72,2048]{1,0:T(8,128)(2,1)S(1)} %get-tuple-element.99.refs_1_), channel_id=1, source_target_pairs={{0,6},{1,7},{2,0},{3,1},{4,2},{5,3},{6,4},{7,5},{8,14},{9,15},{10,... | collective-permute-start | bytes 884744 | tf_op jit(solution)/shard_map/ppermute | solution.py:278
  43.3 15.8 %collective-permute-start.15 = (bf16[72,2048]{1,0:T(8,128)(2,1)S(1)}, bf16[72,2048]{1,0:T(8,128)(2,1)S(1)}, u32[]{:S(2)}, u32[]{:S(2)}) collective-permute-start(bf16[72,2048]{1,0:T(8,128)(2,1)S(1)} %get-tuple-element.98.refs_0_), channel_id=1, source_target_pairs={{0,6},{1,7},{2,0},{3,1},{4,2},{5,3},{6,4},{7,5},{8,14},{9,15},{10,... | collective-permute-start | bytes 884744 | tf_op jit(solution)/shard_map/ppermute | solution.py:278
  45.1 14.0 %collective-permute-start.18 = (bf16[72,2048]{1,0:T(8,128)(2,1)S(1)}, bf16[72,2048]{1,0:T(8,128)(2,1)S(1)}, u32[]{:S(2)}, u32[]{:S(2)}) collective-permute-start(bf16[72,2048]{1,0:T(8,128)(2,1)S(1)} %get-tuple-element.99.refs_1_), channel_id=1, source_target_pairs={{0,2},{1,3},{2,4},{3,5},{4,6},{5,7},{6,0},{7,1},{8,10},{9,11},{10,... | collective-permute-start | bytes 884744 | tf_op jit(solution)/shard_map/ppermute | solution.py:278
  50.3 14.7 %collective-permute-start.19 = (bf16[72,2048]{1,0:T(8,128)(2,1)S(1)}, bf16[72,2048]{1,0:T(8,128)(2,1)S(1)}, u32[]{:S(2)}, u32[]{:S(2)}) collective-permute-start(bf16[72,2048]{1,0:T(8,128)(2,1)S(1)} %collective-permute-done.17.refs_2_), channel_id=1, source_target_pairs={{0,2},{1,3},{2,4},{3,5},{4,6},{5,7},{6,0},{7,1},{8,10},{9,11},{10,... | collective-permute-start | bytes 884744 | tf_op jit(solution)/shard_map/ppermute | solution.py:278
  51.6 13.5 %collective-permute-start.20 = (bf16[72,2048]{1,0:T(8,128)(2,1)S(1)}, bf16[72,2048]{1,0:T(8,128)(2,1)S(1)}, u32[]{:S(2)}, u32[]{:S(2)}) collective-permute-start(bf16[72,2048]{1,0:T(8,128)(2,1)S(1)} %collective-permute-done.16.refs_1_), channel_id=1, source_target_pairs={{0,6},{1,7},{2,0},{3,1},{4,2},{5,3},{6,4},{7,5},{8,14},{9,15},{10,... | collective-permute-start | bytes 884744 | tf_op jit(solution)/shard_map/ppermute | solution.py:278
  61.7 9.3 %collective-permute-start.22 = (bf16[72,2048]{1,0:T(8,128)(2,1)S(1)}, bf16[72,2048]{1,0:T(8,128)(2,1)S(1)}, u32[]{:S(2)}, u32[]{:S(2)}) collective-permute-start(bf16[72,2048]{1,0:T(8,128)(2,1)S(1)} %get-tuple-element.113), channel_id=1, source_target_pairs={{0,2},{1,3},{2,4},{3,5},{4,6},{5,7},{6,0},{7,1},{8,10},{9,11},{10,... | collective-permute-start | bytes 884744 | tf_op jit(solution)/shard_map/ppermute | solution.py:278
  62.0 9.1 %collective-permute-start.23 = (bf16[72,2048]{1,0:T(8,128)(2,1)S(1)}, bf16[72,2048]{1,0:T(8,128)(2,1)S(1)}, u32[]{:S(2)}, u32[]{:S(2)}) collective-permute-start(bf16[72,2048]{1,0:T(8,128)(2,1)S(1)} %get-tuple-element.117), channel_id=1, source_target_pairs={{0,6},{1,7},{2,0},{3,1},{4,2},{5,3},{6,4},{7,5},{8,14},{9,15},{10,... | collective-permute-start | bytes 884744 | tf_op jit(solution)/shard_map/ppermute | solution.py:278
  65.1 21.0 %copy-start.7 = (bf16[1,4096,192]{1,2,0:T(8,128)(2,1)S(1)}, bf16[1,4096,192]{1,2,0:T(8,128)(2,1)}, u32[]{:S(2)}) copy-start(bf16[1,4096,192]{1,2,0:T(8,128)(2,1)} %param.16) | copy-start | bytes 4718596
  65.1 21.0 %copy-start.8 = (bf16[1,192,4096]{2,1,0:T(8,128)(2,1)S(1)}, bf16[1,192,4096]{2,1,0:T(8,128)(2,1)}, u32[]{:S(2)}) copy-start(bf16[1,192,4096]{2,1,0:T(8,128)(2,1)} %param.17) | copy-start | bytes 4718596
  67.6 18.6 %copy-start.6 = (bf16[1,4096,192]{1,2,0:T(8,128)(2,1)S(1)}, bf16[1,4096,192]{1,2,0:T(8,128)(2,1)}, u32[]{:S(2)}) copy-start(bf16[1,4096,192]{1,2,0:T(8,128)(2,1)} %param.15) | copy-start | bytes 4718596
  67.6 10.5 %collective-permute-start.21 = (bf16[72,2048]{1,0:T(8,128)(2,1)S(1)}, bf16[72,2048]{1,0:T(8,128)(2,1)S(1)}, u32[]{:S(2)}, u32[]{:S(2)}) collective-permute-start(bf16[72,2048]{1,0:T(8,128)(2,1)S(1)} %get-tuple-element.116), channel_id=1, source_target_pairs={{0,2},{1,3},{2,4},{3,5},{4,6},{5,7},{6,0},{7,1},{8,10},{9,11},{10,... | collective-permute-start | bytes 884744 | tf_op jit(solution)/shard_map/ppermute | solution.py:278
  68.2 10.0 %collective-permute-start.25 = (bf16[72,2048]{1,0:T(8,128)(2,1)S(1)}, bf16[72,2048]{1,0:T(8,128)(2,1)S(1)}, u32[]{:S(2)}, u32[]{:S(2)}) collective-permute-start(bf16[72,2048]{1,0:T(8,128)(2,1)S(1)} %get-tuple-element.122), channel_id=1, source_target_pairs={{0,6},{1,7},{2,0},{3,1},{4,2},{5,3},{6,4},{7,5},{8,14},{9,15},{10,... | collective-permute-start | bytes 884744 | tf_op jit(solution)/shard_map/ppermute | solution.py:278
  78.1 8.0 %collective-permute-start.24 = (bf16[72,2048]{1,0:T(8,128)(2,1)S(1)}, bf16[72,2048]{1,0:T(8,128)(2,1)S(1)}, u32[]{:S(2)}, u32[]{:S(2)}) collective-permute-start(bf16[72,2048]{1,0:T(8,128)(2,1)S(1)} %add_convert_fusion.5), channel_id=1, source_target_pairs={{0,2},{1,3},{2,4},{3,5},{4,6},{5,7},{6,0},{7,1},{8,10},{9,11},{10,... | collective-permute-start | bytes 884744 | tf_op jit(solution)/shard_map/ppermute | solution.py:278
  78.3 7.8 %collective-permute-start.26 = (bf16[72,2048]{1,0:T(8,128)(2,1)S(1)}, bf16[72,2048]{1,0:T(8,128)(2,1)S(1)}, u32[]{:S(2)}, u32[]{:S(2)}) collective-permute-start(bf16[72,2048]{1,0:T(8,128)(2,1)S(1)} %add_convert_fusion.4), channel_id=1, source_target_pairs={{0,6},{1,7},{2,0},{3,1},{4,2},{5,3},{6,4},{7,5},{8,14},{9,15},{10,... | collective-permute-start | bytes 884744 | tf_op jit(solution)/shard_map/ppermute | solution.py:278
  86.2 22.8 %copy-start.2 = (bf16[256,4096]{1,0:T(8,128)(2,1)S(1)}, bf16[256,4096]{1,0:T(8,128)(2,1)}, u32[]{:S(2)}) copy-start(bf16[256,4096]{1,0:T(8,128)(2,1)} %copy-done.1) | copy-start | bytes 6291460

commit v5 on v4

--- a/solution.py
+++ b/solution.py
@@ -120,14 +120,24 @@
     return jnp.max(most, axis=0, keepdims=True).astype(I32)
 
 
-def dispatch_kernel(index_ref, scales_ref, tokens_ref, out_ref, most_ref, held_ref, raw_ref, sems):
+def dispatch_kernel(
+    far_index, far_scales, tokens_ref, out_ref, most_ref, index_ref, scales_ref, held_ref, raw_ref, sems
+):
     experts = index_ref.shape[0]
     chunks, tok_rows, chunk = held_ref.shape
+    first = [
+        pltpu.make_async_copy(far_index, index_ref, sems.at[chunks]),
+        pltpu.make_async_copy(far_scales, scales_ref, sems.at[chunks + 1]),
+    ]
+    for copy in first:
+        copy.start()
     copies = []
     for k in range(chunks):
         part = tokens_ref.at[:, pl.ds(k * chunk, chunk)]
         copies.append(pltpu.make_async_copy(part, held_ref.at[k], sems.at[k]))
         copies[k].start()
+    for copy in first:
+        copy.wait()
     hot = slots_of(index_ref[...], first_token(tok_rows), tok_rows).astype(BF16)
     column = scale_columns(scales_ref[...])
     blocks = scales_ref.shape[0]
@@ -339,10 +349,16 @@
     sems = pltpu.SemaphoreType.DMA((chunks,))
     outgoing, most = pl.pallas_call(
         dispatch_kernel,
-        in_specs=[vmem, vmem, anywhere],
+        in_specs=[anywhere] * 3,
         out_specs=[vmem, vmem],
         out_shape=[raw_shape, jax.ShapeDtypeStruct((1, 1), I32)],
-        scratch_shapes=[held, raw_f32, sems],
+        scratch_shapes=[
+            pltpu.VMEM(pick_index.shape, I32),
+            pltpu.VMEM(scales.shape, F32),
+            held,
+            raw_f32,
+            pltpu.SemaphoreType.DMA((chunks + 2,)),
+        ],
         compiler_params=pltpu.CompilerParams(vmem_limit_bytes=56 * MIB),
     )(pick_index, scales, tokens)
 

time: 112 us -> 111 us (level)
  no operation moved by 1% of the time
where the time goes in v5:
time: 111 us; the launch traced here: 110 us
  waiting for transfers between devices  36.4 us (33%)
  starting transfers between devices  31.3 us (28%)
  blocking collectives  21.9 us (20%)
  Pallas kernels  18.1 us (16%)
  local copies, waits for them, and re-layouts  1.38 us (1%)
    all_to_all x1, blocking collectives, exchange(): raw = lax.all_to_all(raw, 'wide', split_axis=0, concat_axis=0, tiled=True)  21.9 us
    all_to_all x1, waiting for transfers between devices, exchange(): raw = lax.all_to_all(raw, 'wide', split_axis=0, concat_axis=0, tiled=True)  20.3 us
    ppermute x12, starting transfers between devices, along_y(): lax.ppermute(x, 'narrow', [(i, (i + 2 * step) % n) for i in range(n)])  19.5 us
    ppermute x12, waiting for transfers between devices, along_y(): lax.ppermute(x, 'narrow', [(i, (i + 2 * step) % n) for i in range(n)])  16 us
    all_to_all x1, starting transfers between devices, exchange(): raw = lax.all_to_all(raw, 'wide', split_axis=0, concat_axis=0, tiled=True)  11.2 us
    pallas_call x3, Pallas kernels, expert(): pl.pallas_call(functools.partial(expert_kernel, blocks, hold), in_specs=[...  9.75 us
    pallas_call x1, Pallas kernels, local(): pl.pallas_call(dispatch_kernel, in_specs=[anywhere] * 3, out_specs=[vmem,...  4.12 us
  transfers between devices with their start and end apart: 16, of which 5 were waited for; matrix products, arithmetic and copies ran while one was open for 0% of the time, Pallas kernels for 10%

profile of v5, /device:TPU:32, one launch (start us, length us, event | category | flops | bytes accessed | tf_op | source)
XLA Modules:
  0.0 110.2 jit_solution(5335112078212454971)
XLA Ops:
  0.0 0.0 copy-start
  0.0 0.0 copy-start.3
  0.0 0.0 copy-start.4
  0.0 0.0 copy-start.5
  0.0 0.0 copy-start.9
  0.0 4.1 %shard_map.82 = (bf16[768,512]{1,0:T(8,128)(2,1)}, s32[1,1]{1,0:T(1,128)}) custom-call(s32[32,384]{1,0:T(8,128)} %index_ref.5, f32[32,256]{1,0:T(8,128)} %bitcast.16, bf16[256,4096]{1,0:T(8,128)(2,1)} %tokens_ref.3), custom_call_target="tpu_custom_call" | custom-call | tf_op jit(solution)/shard_map/pallas_call | solution.py:350
  4.2 11.2 %all-to-all-start = ((bf16[32,24,512]{2,1,0:T(8,128)(2,1)}), bf16[32,24,512]{2,1,0:T(8,128)(2,1)S(1)}, u32[]{:S(2)}, u32[]{:S(2)}) async-start(bf16[32,24,512]{2,1,0:T(8,128)(2,1)} %bitcast.30), calls=%async_computation | async-start | bytes 1572864 | tf_op jit(solution)/shard_map/all_to_all | solution.py:367
  15.4 0.1 collective-permute-start.12
  15.5 0.5 collective-permute-start.13
  16.0 0.1 collective-permute-start.14
  16.1 0.0 copy-done
  16.1 0.0 copy-done.3
  16.1 0.0 copy-done.4
  16.1 0.0 copy-done.5
  16.1 0.0 copy-done.9
  16.1 0.8 shard_map.83
  16.9 0.0 copy-start.1
  16.9 1.3 %copy-done.1 = bf16[256,4096]{1,0:T(8,128)(2,1)} copy-done((bf16[256,4096]{1,0:T(8,128)(2,1)}, bf16[256,4096]{1,0:T(8,128)(2,1)S(1)}, u32[]{:S(2)}) %copy-start.1) | copy-done | bytes 2097176
  18.2 20.3 %all-to-all-done = bf16[32,24,512]{2,1,0:T(8,128)(2,1)S(1)} async-done(((bf16[32,24,512]{2,1,0:T(8,128)(2,1)}), bf16[32,24,512]{2,1,0:T(8,128)(2,1)S(1)}, u32[]{:S(2)}, u32[]{:S(2)}) %all-to-all-start) | async-done | bytes 786464 | tf_op jit(solution)/shard_map/all_to_all | solution.py:367
  38.5 0.7 shard_map.84
  39.2 1.7 %collective-permute-start.17 = (bf16[72,2048]{1,0:T(8,128)(2,1)S(1)}, bf16[72,2048]{1,0:T(8,128)(2,1)S(1)}, u32[]{:S(2)}, u32[]{:S(2)}) collective-permute-start(bf16[72,2048]{1,0:T(8,128)(2,1)S(1)} %get-tuple-element.98.refs_0_), channel_id=1, source_target_pairs={{0,2},{1,3},{2,4},{3,5},{4,6},{5,7},{6,0},{7,1},{8,10},{9,11},{10,... | collective-permute-start | bytes 884744 | tf_op jit(solution)/shard_map/ppermute | solution.py:288
  40.9 1.7 %collective-permute-start.16 = (bf16[72,2048]{1,0:T(8,128)(2,1)S(1)}, bf16[72,2048]{1,0:T(8,128)(2,1)S(1)}, u32[]{:S(2)}, u32[]{:S(2)}) collective-permute-start(bf16[72,2048]{1,0:T(8,128)(2,1)S(1)} %get-tuple-element.99.refs_1_), channel_id=1, source_target_pairs={{0,6},{1,7},{2,0},{3,1},{4,2},{5,3},{6,4},{7,5},{8,14},{9,15},{10,... | collective-permute-start | bytes 884744 | tf_op jit(solution)/shard_map/ppermute | solution.py:288
  42.5 0.0 collective-permute-done.12.refs_4_
  42.5 1.8 %collective-permute-start.15 = (bf16[72,2048]{1,0:T(8,128)(2,1)S(1)}, bf16[72,2048]{1,0:T(8,128)(2,1)S(1)}, u32[]{:S(2)}, u32[]{:S(2)}) collective-permute-start(bf16[72,2048]{1,0:T(8,128)(2,1)S(1)} %get-tuple-element.98.refs_0_), channel_id=1, source_target_pairs={{0,6},{1,7},{2,0},{3,1},{4,2},{5,3},{6,4},{7,5},{8,14},{9,15},{10,... | collective-permute-start | bytes 884744 | tf_op jit(solution)/shard_map/ppermute | solution.py:288
  44.3 0.0 collective-permute-done.13.refs_5_
  44.3 0.2 collective-permute-start.18
  44.6 5.0 %collective-permute-done.17.refs_2_ = bf16[72,2048]{1,0:T(8,128)(2,1)S(1)} collective-permute-done((bf16[72,2048]{1,0:T(8,128)(2,1)S(1)}, bf16[72,2048]{1,0:T(8,128)(2,1)S(1)}, u32[]{:S(2)}, u32[]{:S(2)}) %collective-permute-start.17) | collective-permute-done | bytes 294944 | tf_op jit(solution)/shard_map/ppermute | solution.py:288
  49.6 1.2 %collective-permute-start.19 = (bf16[72,2048]{1,0:T(8,128)(2,1)S(1)}, bf16[72,2048]{1,0:T(8,128)(2,1)S(1)}, u32[]{:S(2)}, u32[]{:S(2)}) collective-permute-start(bf16[72,2048]{1,0:T(8,128)(2,1)S(1)} %collective-permute-done.17.refs_2_), channel_id=1, source_target_pairs={{0,2},{1,3},{2,4},{3,5},{4,6},{5,7},{6,0},{7,1},{8,10},{9,11},{10,... | collective-permute-start | bytes 884744 | tf_op jit(solution)/shard_map/ppermute | solution.py:288
  50.8 0.0 collective-permute-done.16.refs_1_
  50.8 2.9 %collective-permute-start.20 = (bf16[72,2048]{1,0:T(8,128)(2,1)S(1)}, bf16[72,2048]{1,0:T(8,128)(2,1)S(1)}, u32[]{:S(2)}, u32[]{:S(2)}) collective-permute-start(bf16[72,2048]{1,0:T(8,128)(2,1)S(1)} %collective-permute-done.16.refs_1_), channel_id=1, source_target_pairs={{0,6},{1,7},{2,0},{3,1},{4,2},{5,3},{6,4},{7,5},{8,14},{9,15},{10,... | collective-permute-start | bytes 884744 | tf_op jit(solution)/shard_map/ppermute | solution.py:288
  53.7 0.0 collective-permute-done.14.refs_7_
  53.7 4.7 %shard_map.85 = (f32[72,2048]{1,0:T(8,128)S(1)}, f32[72,2048]{1,0:T(8,128)S(1)}, bf16[192,4096]{1,0:T(8,128)(2,1)S(1)}, bf16[192,4096]{1,0:T(8,128)(2,1)S(1)}, b...) custom-call(bf16[72,2048]{1,0:T(8,128)(2,1)S(1)} %get-tuple-element., ...), custom_call_target="tpu_custom_call" | custom-call | flops 1 | bytes 1 | tf_op jit(solution)/shard_map/pallas_call | solution.py:240
  58.4 0.0 collective-permute-done.15.refs_0_
  58.4 0.0 collective-permute-done.18.refs_3_
  58.4 2.6 %shard_map.86 = (f32[72,2048]{1,0:T(8,128)S(1)}, bf16[72,2048]{1,0:T(8,128)(2,1)S(1)}, bf16[72,2048]{1,0:T(8,128)(2,1)S(1)}, f32[72,2048]{1,0:T(8,128)S(1)}) custom-call(bf16[72,2048]{1,0:T(8,128)(2,1)S(1)} %collective-permute-done.15.refs_0_, bf16[72,2048]{1,0:T(8,128)(2,1)S(1)} %collective-permute-done.16.refs_1_, ...), custom_call_target="tpu_custom_call" | custom-call | flops 1 | bytes 1 | tf_op jit(solution)/shard_map/pallas_call | solution.py:240
  61.0 0.3 collective-permute-start.22
  61.3 3.0 %collective-permute-start.23 = (bf16[72,2048]{1,0:T(8,128)(2,1)S(1)}, bf16[72,2048]{1,0:T(8,128)(2,1)S(1)}, u32[]{:S(2)}, u32[]{:S(2)}) collective-permute-start(bf16[72,2048]{1,0:T(8,128)(2,1)S(1)} %get-tuple-element.117), channel_id=1, source_target_pairs={{0,6},{1,7},{2,0},{3,1},{4,2},{5,3},{6,4},{7,5},{8,14},{9,15},{10,... | collective-permute-start | bytes 884744 | tf_op jit(solution)/shard_map/ppermute | solution.py:288
  64.3 0.0 collective-permute-done.19.refs_0_
  64.3 0.0 collective-permute-done.20.refs_1_
  64.3 0.0 copy-start.7
  64.3 0.0 copy-start.8
  64.3 2.5 %shard_map.87 = (bf16[72,2048]{1,0:T(8,128)(2,1)S(1)}, bf16[72,2048]{1,0:T(8,128)(2,1)S(1)}) custom-call(bf16[72,2048]{1,0:T(8,128)(2,1)S(1)} %collective-permute-done.19.refs_0_, bf16[72,2048]{1,0:T(8,128)(2,1)S(1)} %collective-permute-done.20.refs_1_, bf16[192,4096]{1,0:T(8,128)(2,1)S(1)} %get-tuple-element.106.refs_4_.refs_2_, ...), custom_call_target="tpu_custom_call" | custom-call | flops 1 | bytes 1 | tf_op jit(solution)/shard_map/pallas_call | solution.py:240
  66.8 0.0 copy-start.6
  66.8 0.6 collective-permute-start.21
  67.4 2.7 %collective-permute-start.25 = (bf16[72,2048]{1,0:T(8,128)(2,1)S(1)}, bf16[72,2048]{1,0:T(8,128)(2,1)S(1)}, u32[]{:S(2)}, u32[]{:S(2)}) collective-permute-start(bf16[72,2048]{1,0:T(8,128)(2,1)S(1)} %get-tuple-element.122), channel_id=1, source_target_pairs={{0,6},{1,7},{2,0},{3,1},{4,2},{5,3},{6,4},{7,5},{8,14},{9,15},{10,... | collective-permute-start | bytes 884744 | tf_op jit(solution)/shard_map/ppermute | solution.py:288
  70.1 0.2 collective-permute-done.22.refs_3_
  70.3 0.0 collective-permute-done.23.refs_4_
  70.3 6.9 %collective-permute-done.21 = bf16[72,2048]{1,0:T(8,128)(2,1)S(1)} collective-permute-done((bf16[72,2048]{1,0:T(8,128)(2,1)S(1)}, bf16[72,2048]{1,0:T(8,128)(2,1)S(1)}, u32[]{:S(2)}, u32[]{:S(2)}) %collective-permute-start.21) | collective-permute-done | bytes 294944 | tf_op jit(solution)/shard_map/ppermute | solution.py:288
  77.2 0.1 add_convert_fusion.5
  77.3 0.1 collective-permute-start.24
  77.4 0.0 collective-permute-done.25
  77.4 0.1 add_convert_fusion.4
  77.5 3.3 %collective-permute-start.26 = (bf16[72,2048]{1,0:T(8,128)(2,1)S(1)}, bf16[72,2048]{1,0:T(8,128)(2,1)S(1)}, u32[]{:S(2)}, u32[]{:S(2)}) collective-permute-start(bf16[72,2048]{1,0:T(8,128)(2,1)S(1)} %add_convert_fusion.4), channel_id=1, source_target_pairs={{0,6},{1,7},{2,0},{3,1},{4,2},{5,3},{6,4},{7,5},{8,14},{9,15},{10,... | collective-permute-start | bytes 884744 | tf_op jit(solution)/shard_map/ppermute | solution.py:288
  81.4 3.9 %collective-permute-done.24.refs_2_ = bf16[72,2048]{1,0:T(8,128)(2,1)S(1)} collective-permute-done((bf16[72,2048]{1,0:T(8,128)(2,1)S(1)}, bf16[72,2048]{1,0:T(8,128)(2,1)S(1)}, u32[]{:S(2)}, u32[]{:S(2)}) %collective-permute-start.24) | collective-permute-done | bytes 294944 | tf_op jit(solution)/shard_map/ppermute | solution.py:288
  85.3 0.0 collective-permute-done.26.refs_5_
  85.3 0.0 copy-done.7
  85.3 0.0 copy-done.8
  85.3 0.0 copy-done.6
  85.4 0.0 copy-start.2
  85.4 1.0 shard_map.88
  86.4 21.9 %all_to_all.10 = bf16[32,24,512]{2,1,0:T(8,128)(2,1)S(1)} all-to-all(bf16[32,24,512]{2,1,0:T(8,128)(2,1)S(1)} %bitcast.15), channel_id=1, replica_groups=mesh['wide'=32,'narrow'=8] {'wide'}, dimensions={0} | all-to-all | bytes 1572864 | tf_op jit(solution)/shard_map/all_to_all | solution.py:367
  108.3 0.0 copy-done.2
  108.3 1.8 %shard_map.89 = bf16[256,4096]{1,0:T(8,128)(2,1)} custom-call(bf16[256,192]{1,0:T(8,128)(2,1)S(1)} %get-tuple-element.96.weight_ref, bf16[768,512]{1,0:T(8,128)(2,1)S(1)} %bitcast.14, bf16[256,4096]{1,0:T(8,128)(2,1)S(1)} %copy-done.2), custom_call_target="tpu_custom_call" | custom-call | tf_op jit(solution)/shard_map/pallas_call | solution.py:405
  (3 shorter events, 0.1 us)
Async XLA Ops:
  0.0 16.1 %copy-start = (bf16[256,4096]{1,0:T(8,128)(2,1)S(1)}, bf16[256,4096]{1,0:T(8,128)(2,1)}, u32[]{:S(2)}) copy-start(bf16[256,4096]{1,0:T(8,128)(2,1)} %tokens_ref.3) | copy-start | bytes 6291460
  0.0 16.1 %copy-start.3 = (f32[256,32]{0,1:T(8,128)S(1)}, f32[256,32]{0,1:T(8,128)}, u32[]{:S(2)}) copy-start(f32[256,32]{0,1:T(8,128)} %param.11) | copy-start | bytes 98308
  0.0 16.1 %copy-start.4 = (f32[32,384]{1,0:T(8,128)S(1)}, f32[32,384]{1,0:T(8,128)}, u32[]{:S(2)}) copy-start(f32[32,384]{1,0:T(8,128)} %gates_ref.1) | copy-start | bytes 147460
  0.0 16.1 %copy-start.5 = (s32[256]{0:T(256)S(1)}, s32[256]{0:T(256)}, u32[]{:S(2)}) copy-start(s32[256]{0:T(256)} %param.14) | copy-start | bytes 3076
  0.0 16.1 %copy-start.9 = (s32[32,384]{1,0:T(8,128)S(1)}, s32[32,384]{1,0:T(8,128)}, u32[]{:S(2)}) copy-start(s32[32,384]{1,0:T(8,128)} %index_ref.5) | copy-start | bytes 147460
  4.2 34.4 %all-to-all-start = ((bf16[32,24,512]{2,1,0:T(8,128)(2,1)}), bf16[32,24,512]{2,1,0:T(8,128)(2,1)S(1)}, u32[]{:S(2)}, u32[]{:S(2)}) async-start(bf16[32,24,512]{2,1,0:T(8,128)(2,1)} %bitcast.30), calls=%async_computation | async-start | bytes 1572864 | tf_op jit(solution)/shard_map/all_to_all | solution.py:367
  15.4 27.2 %collective-permute-start.12 = (bf16[192,4096]{1,0:T(8,128)(2,1)}, bf16[192,4096]{1,0:T(8,128)(2,1)}, u32[]{:S(2)}, u32[]{:S(2)}) collective-permute-start(bf16[192,4096]{1,0:T(8,128)(2,1)} %bitcast.21), channel_id=1, source_target_pairs={{0,1},{1,0},{2,3},{3,2},{4,5},{5,4},{6,7},{7,6},{8,9},{9,8},{10,11... | collective-permute-start | bytes 4718600 | tf_op jit(solution)/shard_map/ppermute | solution.py:344
  15.5 28.9 %collective-permute-start.13 = (bf16[192,4096]{1,0:T(8,128)(2,1)}, bf16[192,4096]{1,0:T(8,128)(2,1)}, u32[]{:S(2)}, u32[]{:S(2)}) collective-permute-start(bf16[192,4096]{1,0:T(8,128)(2,1)} %bitcast.24), channel_id=1, source_target_pairs={{0,1},{1,0},{2,3},{3,2},{4,5},{5,4},{6,7},{7,6},{8,9},{9,8},{10,11... | collective-permute-start | bytes 4718600 | tf_op jit(solution)/shard_map/ppermute | solution.py:344
  16.0 37.7 %collective-permute-start.14 = (bf16[192,4096]{1,0:T(8,128)(2,1)}, bf16[192,4096]{1,0:T(8,128)(2,1)}, u32[]{:S(2)}, u32[]{:S(2)}) collective-permute-start(bf16[192,4096]{1,0:T(8,128)(2,1)} %bitcast.27), channel_id=1, source_target_pairs={{0,1},{1,0},{2,3},{3,2},{4,5},{5,4},{6,7},{7,6},{8,9},{9,8},{10,11... | collective-permute-start | bytes 4718600 | tf_op jit(solution)/shard_map/ppermute | solution.py:344
  16.9 1.3 %copy-start.1 = (bf16[256,4096]{1,0:T(8,128)(2,1)}, bf16[256,4096]{1,0:T(8,128)(2,1)S(1)}, u32[]{:S(2)}) copy-start(bf16[256,4096]{1,0:T(8,128)(2,1)S(1)} %get-tuple-element.133.rows_ref) | copy-start | bytes 6291460
  39.2 10.4 %collective-permute-start.17 = (bf16[72,2048]{1,0:T(8,128)(2,1)S(1)}, bf16[72,2048]{1,0:T(8,128)(2,1)S(1)}, u32[]{:S(2)}, u32[]{:S(2)}) collective-permute-start(bf16[72,2048]{1,0:T(8,128)(2,1)S(1)} %get-tuple-element.98.refs_0_), channel_id=1, source_target_pairs={{0,2},{1,3},{2,4},{3,5},{4,6},{5,7},{6,0},{7,1},{8,10},{9,11},{10,... | collective-permute-start | bytes 884744 | tf_op jit(solution)/shard_map/ppermute | solution.py:288
  40.9 9.9 %collective-permute-start.16 = (bf16[72,2048]{1,0:T(8,128)(2,1)S(1)}, bf16[72,2048]{1,0:T(8,128)(2,1)S(1)}, u32[]{:S(2)}, u32[]{:S(2)}) collective-permute-start(bf16[72,2048]{1,0:T(8,128)(2,1)S(1)} %get-tuple-element.99.refs_1_), channel_id=1, source_target_pairs={{0,6},{1,7},{2,0},{3,1},{4,2},{5,3},{6,4},{7,5},{8,14},{9,15},{10,... | collective-permute-start | bytes 884744 | tf_op jit(solution)/shard_map/ppermute | solution.py:288
  42.5 15.8 %collective-permute-start.15 = (bf16[72,2048]{1,0:T(8,128)(2,1)S(1)}, bf16[72,2048]{1,0:T(8,128)(2,1)S(1)}, u32[]{:S(2)}, u32[]{:S(2)}) collective-permute-start(bf16[72,2048]{1,0:T(8,128)(2,1)S(1)} %get-tuple-element.98.refs_0_), channel_id=1, source_target_pairs={{0,6},{1,7},{2,0},{3,1},{4,2},{5,3},{6,4},{7,5},{8,14},{9,15},{10,... | collective-permute-start | bytes 884744 | tf_op jit(solution)/shard_map/ppermute | solution.py:288
  44.3 14.0 %collective-permute-start.18 = (bf16[72,2048]{1,0:T(8,128)(2,1)S(1)}, bf16[72,2048]{1,0:T(8,128)(2,1)S(1)}, u32[]{:S(2)}, u32[]{:S(2)}) collective-permute-start(bf16[72,2048]{1,0:T(8,128)(2,1)S(1)} %get-tuple-element.99.refs_1_), channel_id=1, source_target_pairs={{0,2},{1,3},{2,4},{3,5},{4,6},{5,7},{6,0},{7,1},{8,10},{9,11},{10,... | collective-permute-start | bytes 884744 | tf_op jit(solution)/shard_map/ppermute | solution.py:288
  49.6 14.7 %collective-permute-start.19 = (bf16[72,2048]{1,0:T(8,128)(2,1)S(1)}, bf16[72,2048]{1,0:T(8,128)(2,1)S(1)}, u32[]{:S(2)}, u32[]{:S(2)}) collective-permute-start(bf16[72,2048]{1,0:T(8,128)(2,1)S(1)} %collective-permute-done.17.refs_2_), channel_id=1, source_target_pairs={{0,2},{1,3},{2,4},{3,5},{4,6},{5,7},{6,0},{7,1},{8,10},{9,11},{10,... | collective-permute-start | bytes 884744 | tf_op jit(solution)/shard_map/ppermute | solution.py:288
  50.8 13.5 %collective-permute-start.20 = (bf16[72,2048]{1,0:T(8,128)(2,1)S(1)}, bf16[72,2048]{1,0:T(8,128)(2,1)S(1)}, u32[]{:S(2)}, u32[]{:S(2)}) collective-permute-start(bf16[72,2048]{1,0:T(8,128)(2,1)S(1)} %collective-permute-done.16.refs_1_), channel_id=1, source_target_pairs={{0,6},{1,7},{2,0},{3,1},{4,2},{5,3},{6,4},{7,5},{8,14},{9,15},{10,... | collective-permute-start | bytes 884744 | tf_op jit(solution)/shard_map/ppermute | solution.py:288
  61.0 9.3 %collective-permute-start.22 = (bf16[72,2048]{1,0:T(8,128)(2,1)S(1)}, bf16[72,2048]{1,0:T(8,128)(2,1)S(1)}, u32[]{:S(2)}, u32[]{:S(2)}) collective-permute-start(bf16[72,2048]{1,0:T(8,128)(2,1)S(1)} %get-tuple-element.113), channel_id=1, source_target_pairs={{0,2},{1,3},{2,4},{3,5},{4,6},{5,7},{6,0},{7,1},{8,10},{9,11},{10,... | collective-permute-start | bytes 884744 | tf_op jit(solution)/shard_map/ppermute | solution.py:288
  61.3 9.1 %collective-permute-start.23 = (bf16[72,2048]{1,0:T(8,128)(2,1)S(1)}, bf16[72,2048]{1,0:T(8,128)(2,1)S(1)}, u32[]{:S(2)}, u32[]{:S(2)}) collective-permute-start(bf16[72,2048]{1,0:T(8,128)(2,1)S(1)} %get-tuple-element.117), channel_id=1, source_target_pairs={{0,6},{1,7},{2,0},{3,1},{4,2},{5,3},{6,4},{7,5},{8,14},{9,15},{10,... | collective-permute-start | bytes 884744 | tf_op jit(solution)/shard_map/ppermute | solution.py:288
  64.3 21.0 %copy-start.7 = (bf16[1,4096,192]{1,2,0:T(8,128)(2,1)S(1)}, bf16[1,4096,192]{1,2,0:T(8,128)(2,1)}, u32[]{:S(2)}) copy-start(bf16[1,4096,192]{1,2,0:T(8,128)(2,1)} %param.16) | copy-start | bytes 4718596
  64.3 21.0 %copy-start.8 = (bf16[1,192,4096]{2,1,0:T(8,128)(2,1)S(1)}, bf16[1,192,4096]{2,1,0:T(8,128)(2,1)}, u32[]{:S(2)}) copy-start(bf16[1,192,4096]{2,1,0:T(8,128)(2,1)} %param.17) | copy-start | bytes 4718596
  66.8 18.5 %copy-start.6 = (bf16[1,4096,192]{1,2,0:T(8,128)(2,1)S(1)}, bf16[1,4096,192]{1,2,0:T(8,128)(2,1)}, u32[]{:S(2)}) copy-start(bf16[1,4096,192]{1,2,0:T(8,128)(2,1)} %param.15) | copy-start | bytes 4718596
  66.8 10.4 %collective-permute-start.21 = (bf16[72,2048]{1,0:T(8,128)(2,1)S(1)}, bf16[72,2048]{1,0:T(8,128)(2,1)S(1)}, u32[]{:S(2)}, u32[]{:S(2)}) collective-permute-start(bf16[72,2048]{1,0:T(8,128)(2,1)S(1)} %get-tuple-element.116), channel_id=1, source_target_pairs={{0,2},{1,3},{2,4},{3,5},{4,6},{5,7},{6,0},{7,1},{8,10},{9,11},{10,... | collective-permute-start | bytes 884744 | tf_op jit(solution)/shard_map/ppermute | solution.py:288
  67.4 10.0 %collective-permute-start.25 = (bf16[72,2048]{1,0:T(8,128)(2,1)S(1)}, bf16[72,2048]{1,0:T(8,128)(2,1)S(1)}, u32[]{:S(2)}, u32[]{:S(2)}) collective-permute-start(bf16[72,2048]{1,0:T(8,128)(2,1)S(1)} %get-tuple-element.122), channel_id=1, source_target_pairs={{0,6},{1,7},{2,0},{3,1},{4,2},{5,3},{6,4},{7,5},{8,14},{9,15},{10,... | collective-permute-start | bytes 884744 | tf_op jit(solution)/shard_map/ppermute | solution.py:288
  77.3 8.0 %collective-permute-start.24 = (bf16[72,2048]{1,0:T(8,128)(2,1)S(1)}, bf16[72,2048]{1,0:T(8,128)(2,1)S(1)}, u32[]{:S(2)}, u32[]{:S(2)}) collective-permute-start(bf16[72,2048]{1,0:T(8,128)(2,1)S(1)} %add_convert_fusion.5), channel_id=1, source_target_pairs={{0,2},{1,3},{2,4},{3,5},{4,6},{5,7},{6,0},{7,1},{8,10},{9,11},{10,... | collective-permute-start | bytes 884744 | tf_op jit(solution)/shard_map/ppermute | solution.py:288
  77.5 7.8 %collective-permute-start.26 = (bf16[72,2048]{1,0:T(8,128)(2,1)S(1)}, bf16[72,2048]{1,0:T(8,128)(2,1)S(1)}, u32[]{:S(2)}, u32[]{:S(2)}) collective-permute-start(bf16[72,2048]{1,0:T(8,128)(2,1)S(1)} %add_convert_fusion.4), channel_id=1, source_target_pairs={{0,6},{1,7},{2,0},{3,1},{4,2},{5,3},{6,4},{7,5},{8,14},{9,15},{10,... | collective-permute-start | bytes 884744 | tf_op jit(solution)/shard_map/ppermute | solution.py:288
  85.4 22.9 %copy-start.2 = (bf16[256,4096]{1,0:T(8,128)(2,1)S(1)}, bf16[256,4096]{1,0:T(8,128)(2,1)}, u32[]{:S(2)}) copy-start(bf16[256,4096]{1,0:T(8,128)(2,1)} %copy-done.1) | copy-start | bytes 6291460

commit v6 on v5

--- a/solution.py
+++ b/solution.py
@@ -97,13 +97,15 @@
 
 
 def narrow_raw(wide_ref, out_ref):
+    total = out_ref.shape[0]
     for q in range(PIECE // BLOCK):
-        out_ref[:, q * BLOCK : (q + 1) * BLOCK] = wide_ref[q].astype(BF16)
+        out_ref[:, q * BLOCK : (q + 1) * BLOCK] = wide_ref[q, :total, :].astype(BF16)
 
 
 def widen_raw(raw_ref, wide_ref):
     for q in range(PIECE // BLOCK):
-        wide_ref[q] = raw_ref[:, q * BLOCK : (q + 1) * BLOCK].astype(F32)
+        part = raw_ref[:, q * BLOCK : (q + 1) * BLOCK].astype(F32)
+        wide_ref[q, : raw_ref.shape[0], :] = part
 
 
 def first_token(tok_rows):
@@ -292,7 +294,7 @@
     total = arrived.shape[0]
     width = own[2].shape[1]
     vmem = pl.BlockSpec(memory_space=pltpu.VMEM)
-    raw_f32 = pltpu.VMEM((PIECE // BLOCK, total, BLOCK), F32)
+    raw_f32 = pltpu.VMEM((PIECE // BLOCK, total + total // pick_index.shape[0], BLOCK), F32)
     half_shape = jax.ShapeDtypeStruct((rows, width // 2), BF16)
     x0 = pl.pallas_call(
         functools.partial(unpack_kernel, tok_rows, first_row),
@@ -344,7 +346,7 @@
     sibling = tuple(lax.ppermute(v, "narrow", other_core) for v in own)
 
     raw_shape = jax.ShapeDtypeStruct((total, PIECE), BF16)
-    raw_f32 = pltpu.VMEM((PIECE // BLOCK, total, BLOCK), F32)
+    raw_f32 = pltpu.VMEM((PIECE // BLOCK, total + per, BLOCK), F32)
     held = pltpu.VMEM((chunks, tok_rows, chunk), BF16)
     sems = pltpu.SemaphoreType.DMA((chunks,))
     outgoing, most = pl.pallas_call(

time: 111 us -> 111 us (level)
  no operation moved by 1% of the time
where the time goes in v6:
time: 111 us; the launch traced here: 110 us
  waiting for transfers between devices  36.4 us (33%)
  starting transfers between devices  31.3 us (28%)
  blocking collectives  21.7 us (20%)
  Pallas kernels  18.1 us (16%)
  local copies, waits for them, and re-layouts  1.38 us (1%)
    all_to_all x1, blocking collectives, exchange(): raw = lax.all_to_all(raw, 'wide', split_axis=0, concat_axis=0, tiled=True)  21.7 us
    all_to_all x1, waiting for transfers between devices, exchange(): raw = lax.all_to_all(raw, 'wide', split_axis=0, concat_axis=0, tiled=True)  20.3 us
    ppermute x12, starting transfers between devices, along_y(): lax.ppermute(x, 'narrow', [(i, (i + 2 * step) % n) for i in range(n)])  19.5 us
    ppermute x12, waiting for transfers between devices, along_y(): lax.ppermute(x, 'narrow', [(i, (i + 2 * step) % n) for i in range(n)])  16.1 us
    all_to_all x1, starting transfers between devices, exchange(): raw = lax.all_to_all(raw, 'wide', split_axis=0, concat_axis=0, tiled=True)  11.2 us
    pallas_call x3, Pallas kernels, expert(): pl.pallas_call(functools.partial(expert_kernel, blocks, hold), in_specs=[...  9.75 us
    pallas_call x1, Pallas kernels, local(): pl.pallas_call(dispatch_kernel, in_specs=[anywhere] * 3, out_specs=[vmem,...  4.13 us
  transfers between devices with their start and end apart: 16, of which 5 were waited for; matrix products, arithmetic and copies ran while one was open for 0% of the time, Pallas kernels for 10%

profile of v6, /device:TPU:32, one launch (start us, length us, event | category | flops | bytes accessed | tf_op | source)
XLA Modules:
  0.0 110.1 jit_solution(12961556505440512635)
XLA Ops:
  0.0 0.0 copy-start
  0.0 0.0 copy-start.3
  0.0 0.0 copy-start.4
  0.0 0.0 copy-start.5
  0.0 0.0 copy-start.9
  0.0 4.1 %shard_map.82 = (bf16[768,512]{1,0:T(8,128)(2,1)}, s32[1,1]{1,0:T(1,128)}) custom-call(s32[32,384]{1,0:T(8,128)} %index_ref.5, f32[32,256]{1,0:T(8,128)} %bitcast.16, bf16[256,4096]{1,0:T(8,128)(2,1)} %tokens_ref.3), custom_call_target="tpu_custom_call" | custom-call | tf_op jit(solution)/shard_map/pallas_call | solution.py:352
  4.2 11.2 %all-to-all-start = ((bf16[32,24,512]{2,1,0:T(8,128)(2,1)}), bf16[32,24,512]{2,1,0:T(8,128)(2,1)S(1)}, u32[]{:S(2)}, u32[]{:S(2)}) async-start(bf16[32,24,512]{2,1,0:T(8,128)(2,1)} %bitcast.30), calls=%async_computation | async-start | bytes 1572864 | tf_op jit(solution)/shard_map/all_to_all | solution.py:369
  15.4 0.1 collective-permute-start.12
  15.5 0.5 collective-permute-start.13
  16.0 0.1 collective-permute-start.14
  16.1 0.0 copy-done
  16.1 0.0 copy-done.3
  16.1 0.0 copy-done.4
  16.1 0.0 copy-done.5
  16.1 0.0 copy-done.9
  16.1 0.8 shard_map.83
  16.9 0.0 copy-start.1
  16.9 1.3 %copy-done.1 = bf16[256,4096]{1,0:T(8,128)(2,1)} copy-done((bf16[256,4096]{1,0:T(8,128)(2,1)}, bf16[256,4096]{1,0:T(8,128)(2,1)S(1)}, u32[]{:S(2)}) %copy-start.1) | copy-done | bytes 2097176
  18.2 20.3 %all-to-all-done = bf16[32,24,512]{2,1,0:T(8,128)(2,1)S(1)} async-done(((bf16[32,24,512]{2,1,0:T(8,128)(2,1)}), bf16[32,24,512]{2,1,0:T(8,128)(2,1)S(1)}, u32[]{:S(2)}, u32[]{:S(2)}) %all-to-all-start) | async-done | bytes 786464 | tf_op jit(solution)/shard_map/all_to_all | solution.py:369
  38.5 0.7 shard_map.84
  39.2 1.7 %collective-permute-start.17 = (bf16[72,2048]{1,0:T(8,128)(2,1)S(1)}, bf16[72,2048]{1,0:T(8,128)(2,1)S(1)}, u32[]{:S(2)}, u32[]{:S(2)}) collective-permute-start(bf16[72,2048]{1,0:T(8,128)(2,1)S(1)} %get-tuple-element.98.refs_0_), channel_id=1, source_target_pairs={{0,2},{1,3},{2,4},{3,5},{4,6},{5,7},{6,0},{7,1},{8,10},{9,11},{10,... | collective-permute-start | bytes 884744 | tf_op jit(solution)/shard_map/ppermute | solution.py:290
  40.9 1.7 %collective-permute-start.16 = (bf16[72,2048]{1,0:T(8,128)(2,1)S(1)}, bf16[72,2048]{1,0:T(8,128)(2,1)S(1)}, u32[]{:S(2)}, u32[]{:S(2)}) collective-permute-start(bf16[72,2048]{1,0:T(8,128)(2,1)S(1)} %get-tuple-element.99.refs_1_), channel_id=1, source_target_pairs={{0,6},{1,7},{2,0},{3,1},{4,2},{5,3},{6,4},{7,5},{8,14},{9,15},{10,... | collective-permute-start | bytes 884744 | tf_op jit(solution)/shard_map/ppermute | solution.py:290
  42.5 0.0 collective-permute-done.12.refs_4_
  42.5 1.8 %collective-permute-start.15 = (bf16[72,2048]{1,0:T(8,128)(2,1)S(1)}, bf16[72,2048]{1,0:T(8,128)(2,1)S(1)}, u32[]{:S(2)}, u32[]{:S(2)}) collective-permute-start(bf16[72,2048]{1,0:T(8,128)(2,1)S(1)} %get-tuple-element.98.refs_0_), channel_id=1, source_target_pairs={{0,6},{1,7},{2,0},{3,1},{4,2},{5,3},{6,4},{7,5},{8,14},{9,15},{10,... | collective-permute-start | bytes 884744 | tf_op jit(solution)/shard_map/ppermute | solution.py:290
  44.3 0.0 collective-permute-done.13.refs_5_
  44.3 0.2 collective-permute-start.18
  44.6 5.0 %collective-permute-done.17.refs_2_ = bf16[72,2048]{1,0:T(8,128)(2,1)S(1)} collective-permute-done((bf16[72,2048]{1,0:T(8,128)(2,1)S(1)}, bf16[72,2048]{1,0:T(8,128)(2,1)S(1)}, u32[]{:S(2)}, u32[]{:S(2)}) %collective-permute-start.17) | collective-permute-done | bytes 294944 | tf_op jit(solution)/shard_map/ppermute | solution.py:290
  49.6 1.2 %collective-permute-start.19 = (bf16[72,2048]{1,0:T(8,128)(2,1)S(1)}, bf16[72,2048]{1,0:T(8,128)(2,1)S(1)}, u32[]{:S(2)}, u32[]{:S(2)}) collective-permute-start(bf16[72,2048]{1,0:T(8,128)(2,1)S(1)} %collective-permute-done.17.refs_2_), channel_id=1, source_target_pairs={{0,2},{1,3},{2,4},{3,5},{4,6},{5,7},{6,0},{7,1},{8,10},{9,11},{10,... | collective-permute-start | bytes 884744 | tf_op jit(solution)/shard_map/ppermute | solution.py:290
  50.8 0.0 collective-permute-done.16.refs_1_
  50.8 2.9 %collective-permute-start.20 = (bf16[72,2048]{1,0:T(8,128)(2,1)S(1)}, bf16[72,2048]{1,0:T(8,128)(2,1)S(1)}, u32[]{:S(2)}, u32[]{:S(2)}) collective-permute-start(bf16[72,2048]{1,0:T(8,128)(2,1)S(1)} %collective-permute-done.16.refs_1_), channel_id=1, source_target_pairs={{0,6},{1,7},{2,0},{3,1},{4,2},{5,3},{6,4},{7,5},{8,14},{9,15},{10,... | collective-permute-start | bytes 884744 | tf_op jit(solution)/shard_map/ppermute | solution.py:290
  53.7 0.0 collective-permute-done.14.refs_7_
  53.7 4.7 %shard_map.85 = (f32[72,2048]{1,0:T(8,128)S(1)}, f32[72,2048]{1,0:T(8,128)S(1)}, bf16[192,4096]{1,0:T(8,128)(2,1)S(1)}, bf16[192,4096]{1,0:T(8,128)(2,1)S(1)}, b...) custom-call(bf16[72,2048]{1,0:T(8,128)(2,1)S(1)} %get-tuple-element., ...), custom_call_target="tpu_custom_call" | custom-call | flops 1 | bytes 1 | tf_op jit(solution)/shard_map/pallas_call | solution.py:242
  58.4 0.0 collective-permute-done.15.refs_0_
  58.4 0.0 collective-permute-done.18.refs_3_
  58.4 2.6 %shard_map.86 = (f32[72,2048]{1,0:T(8,128)S(1)}, bf16[72,2048]{1,0:T(8,128)(2,1)S(1)}, bf16[72,2048]{1,0:T(8,128)(2,1)S(1)}, f32[72,2048]{1,0:T(8,128)S(1)}) custom-call(bf16[72,2048]{1,0:T(8,128)(2,1)S(1)} %collective-permute-done.15.refs_0_, bf16[72,2048]{1,0:T(8,128)(2,1)S(1)} %collective-permute-done.16.refs_1_, ...), custom_call_target="tpu_custom_call" | custom-call | flops 1 | bytes 1 | tf_op jit(solution)/shard_map/pallas_call | solution.py:242
  61.0 0.3 collective-permute-start.22
  61.3 3.1 %collective-permute-start.23 = (bf16[72,2048]{1,0:T(8,128)(2,1)S(1)}, bf16[72,2048]{1,0:T(8,128)(2,1)S(1)}, u32[]{:S(2)}, u32[]{:S(2)}) collective-permute-start(bf16[72,2048]{1,0:T(8,128)(2,1)S(1)} %get-tuple-element.117), channel_id=1, source_target_pairs={{0,6},{1,7},{2,0},{3,1},{4,2},{5,3},{6,4},{7,5},{8,14},{9,15},{10,... | collective-permute-start | bytes 884744 | tf_op jit(solution)/shard_map/ppermute | solution.py:290
  64.3 0.0 collective-permute-done.19.refs_0_
  64.3 0.0 collective-permute-done.20.refs_1_
  64.3 0.0 copy-start.7
  64.3 0.0 copy-start.8
  64.4 2.5 %shard_map.87 = (bf16[72,2048]{1,0:T(8,128)(2,1)S(1)}, bf16[72,2048]{1,0:T(8,128)(2,1)S(1)}) custom-call(bf16[72,2048]{1,0:T(8,128)(2,1)S(1)} %collective-permute-done.19.refs_0_, bf16[72,2048]{1,0:T(8,128)(2,1)S(1)} %collective-permute-done.20.refs_1_, bf16[192,4096]{1,0:T(8,128)(2,1)S(1)} %get-tuple-element.106.refs_4_.refs_2_, ...), custom_call_target="tpu_custom_call" | custom-call | flops 1 | bytes 1 | tf_op jit(solution)/shard_map/pallas_call | solution.py:242
  66.8 0.0 copy-start.6
  66.8 0.6 collective-permute-start.21
  67.4 2.7 %collective-permute-start.25 = (bf16[72,2048]{1,0:T(8,128)(2,1)S(1)}, bf16[72,2048]{1,0:T(8,128)(2,1)S(1)}, u32[]{:S(2)}, u32[]{:S(2)}) collective-permute-start(bf16[72,2048]{1,0:T(8,128)(2,1)S(1)} %get-tuple-element.122), channel_id=1, source_target_pairs={{0,6},{1,7},{2,0},{3,1},{4,2},{5,3},{6,4},{7,5},{8,14},{9,15},{10,... | collective-permute-start | bytes 884744 | tf_op jit(solution)/shard_map/ppermute | solution.py:290
  70.2 0.2 collective-permute-done.22.refs_3_
  70.3 0.0 collective-permute-done.23.refs_4_
  70.3 7.0 %collective-permute-done.21 = bf16[72,2048]{1,0:T(8,128)(2,1)S(1)} collective-permute-done((bf16[72,2048]{1,0:T(8,128)(2,1)S(1)}, bf16[72,2048]{1,0:T(8,128)(2,1)S(1)}, u32[]{:S(2)}, u32[]{:S(2)}) %collective-permute-start.21) | collective-permute-done | bytes 294944 | tf_op jit(solution)/shard_map/ppermute | solution.py:290
  77.3 0.1 add_convert_fusion.5
  77.4 0.1 collective-permute-start.24
  77.5 0.0 collective-permute-done.25
  77.5 0.1 add_convert_fusion.4
  77.5 3.3 %collective-permute-start.26 = (bf16[72,2048]{1,0:T(8,128)(2,1)S(1)}, bf16[72,2048]{1,0:T(8,128)(2,1)S(1)}, u32[]{:S(2)}, u32[]{:S(2)}) collective-permute-start(bf16[72,2048]{1,0:T(8,128)(2,1)S(1)} %add_convert_fusion.4), channel_id=1, source_target_pairs={{0,6},{1,7},{2,0},{3,1},{4,2},{5,3},{6,4},{7,5},{8,14},{9,15},{10,... | collective-permute-start | bytes 884744 | tf_op jit(solution)/shard_map/ppermute | solution.py:290
  81.5 3.9 %collective-permute-done.24.refs_2_ = bf16[72,2048]{1,0:T(8,128)(2,1)S(1)} collective-permute-done((bf16[72,2048]{1,0:T(8,128)(2,1)S(1)}, bf16[72,2048]{1,0:T(8,128)(2,1)S(1)}, u32[]{:S(2)}, u32[]{:S(2)}) %collective-permute-start.24) | collective-permute-done | bytes 294944 | tf_op jit(solution)/shard_map/ppermute | solution.py:290
  85.4 0.0 collective-permute-done.26.refs_5_
  85.4 0.0 copy-done.7
  85.4 0.0 copy-done.8
  85.4 0.0 copy-done.6
  85.4 0.0 copy-start.2
  85.5 1.0 shard_map.88
  86.5 21.7 %all_to_all.10 = bf16[32,24,512]{2,1,0:T(8,128)(2,1)S(1)} all-to-all(bf16[32,24,512]{2,1,0:T(8,128)(2,1)S(1)} %bitcast.15), channel_id=1, replica_groups=mesh['wide'=32,'narrow'=8] {'wide'}, dimensions={0} | all-to-all | bytes 1572864 | tf_op jit(solution)/shard_map/all_to_all | solution.py:369
  108.2 0.0 copy-done.2
  108.2 1.8 %shard_map.89 = bf16[256,4096]{1,0:T(8,128)(2,1)} custom-call(bf16[256,192]{1,0:T(8,128)(2,1)S(1)} %get-tuple-element.96.weight_ref, bf16[768,512]{1,0:T(8,128)(2,1)S(1)} %bitcast.14, bf16[256,4096]{1,0:T(8,128)(2,1)S(1)} %copy-done.2), custom_call_target="tpu_custom_call" | custom-call | tf_op jit(solution)/shard_map/pallas_call | solution.py:407
  (3 shorter events, 0.1 us)
Async XLA Ops:
  0.0 16.1 %copy-start = (bf16[256,4096]{1,0:T(8,128)(2,1)S(1)}, bf16[256,4096]{1,0:T(8,128)(2,1)}, u32[]{:S(2)}) copy-start(bf16[256,4096]{1,0:T(8,128)(2,1)} %tokens_ref.3) | copy-start | bytes 6291460
  0.0 16.1 %copy-start.3 = (f32[256,32]{0,1:T(8,128)S(1)}, f32[256,32]{0,1:T(8,128)}, u32[]{:S(2)}) copy-start(f32[256,32]{0,1:T(8,128)} %param.11) | copy-start | bytes 98308
  0.0 16.1 %copy-start.4 = (f32[32,384]{1,0:T(8,128)S(1)}, f32[32,384]{1,0:T(8,128)}, u32[]{:S(2)}) copy-start(f32[32,384]{1,0:T(8,128)} %gates_ref.1) | copy-start | bytes 147460
  0.0 16.1 %copy-start.5 = (s32[256]{0:T(256)S(1)}, s32[256]{0:T(256)}, u32[]{:S(2)}) copy-start(s32[256]{0:T(256)} %param.14) | copy-start | bytes 3076
  0.0 16.1 %copy-start.9 = (s32[32,384]{1,0:T(8,128)S(1)}, s32[32,384]{1,0:T(8,128)}, u32[]{:S(2)}) copy-start(s32[32,384]{1,0:T(8,128)} %index_ref.5) | copy-start | bytes 147460
  4.2 34.4 %all-to-all-start = ((bf16[32,24,512]{2,1,0:T(8,128)(2,1)}), bf16[32,24,512]{2,1,0:T(8,128)(2,1)S(1)}, u32[]{:S(2)}, u32[]{:S(2)}) async-start(bf16[32,24,512]{2,1,0:T(8,128)(2,1)} %bitcast.30), calls=%async_computation | async-start | bytes 1572864 | tf_op jit(solution)/shard_map/all_to_all | solution.py:369
  15.4 27.2 %collective-permute-start.12 = (bf16[192,4096]{1,0:T(8,128)(2,1)}, bf16[192,4096]{1,0:T(8,128)(2,1)}, u32[]{:S(2)}, u32[]{:S(2)}) collective-permute-start(bf16[192,4096]{1,0:T(8,128)(2,1)} %bitcast.21), channel_id=1, source_target_pairs={{0,1},{1,0},{2,3},{3,2},{4,5},{5,4},{6,7},{7,6},{8,9},{9,8},{10,11... | collective-permute-start | bytes 4718600 | tf_op jit(solution)/shard_map/ppermute | solution.py:346
  15.5 28.9 %collective-permute-start.13 = (bf16[192,4096]{1,0:T(8,128)(2,1)}, bf16[192,4096]{1,0:T(8,128)(2,1)}, u32[]{:S(2)}, u32[]{:S(2)}) collective-permute-start(bf16[192,4096]{1,0:T(8,128)(2,1)} %bitcast.24), channel_id=1, source_target_pairs={{0,1},{1,0},{2,3},{3,2},{4,5},{5,4},{6,7},{7,6},{8,9},{9,8},{10,11... | collective-permute-start | bytes 4718600 | tf_op jit(solution)/shard_map/ppermute | solution.py:346
  16.0 37.7 %collective-permute-start.14 = (bf16[192,4096]{1,0:T(8,128)(2,1)}, bf16[192,4096]{1,0:T(8,128)(2,1)}, u32[]{:S(2)}, u32[]{:S(2)}) collective-permute-start(bf16[192,4096]{1,0:T(8,128)(2,1)} %bitcast.27), channel_id=1, source_target_pairs={{0,1},{1,0},{2,3},{3,2},{4,5},{5,4},{6,7},{7,6},{8,9},{9,8},{10,11... | collective-permute-start | bytes 4718600 | tf_op jit(solution)/shard_map/ppermute | solution.py:346
  16.9 1.3 %copy-start.1 = (bf16[256,4096]{1,0:T(8,128)(2,1)}, bf16[256,4096]{1,0:T(8,128)(2,1)S(1)}, u32[]{:S(2)}) copy-start(bf16[256,4096]{1,0:T(8,128)(2,1)S(1)} %get-tuple-element.133.rows_ref) | copy-start | bytes 6291460
  39.2 10.4 %collective-permute-start.17 = (bf16[72,2048]{1,0:T(8,128)(2,1)S(1)}, bf16[72,2048]{1,0:T(8,128)(2,1)S(1)}, u32[]{:S(2)}, u32[]{:S(2)}) collective-permute-start(bf16[72,2048]{1,0:T(8,128)(2,1)S(1)} %get-tuple-element.98.refs_0_), channel_id=1, source_target_pairs={{0,2},{1,3},{2,4},{3,5},{4,6},{5,7},{6,0},{7,1},{8,10},{9,11},{10,... | collective-permute-start | bytes 884744 | tf_op jit(solution)/shard_map/ppermute | solution.py:290
  40.9 10.0 %collective-permute-start.16 = (bf16[72,2048]{1,0:T(8,128)(2,1)S(1)}, bf16[72,2048]{1,0:T(8,128)(2,1)S(1)}, u32[]{:S(2)}, u32[]{:S(2)}) collective-permute-start(bf16[72,2048]{1,0:T(8,128)(2,1)S(1)} %get-tuple-element.99.refs_1_), channel_id=1, source_target_pairs={{0,6},{1,7},{2,0},{3,1},{4,2},{5,3},{6,4},{7,5},{8,14},{9,15},{10,... | collective-permute-start | bytes 884744 | tf_op jit(solution)/shard_map/ppermute | solution.py:290
  42.5 15.8 %collective-permute-start.15 = (bf16[72,2048]{1,0:T(8,128)(2,1)S(1)}, bf16[72,2048]{1,0:T(8,128)(2,1)S(1)}, u32[]{:S(2)}, u32[]{:S(2)}) collective-permute-start(bf16[72,2048]{1,0:T(8,128)(2,1)S(1)} %get-tuple-element.98.refs_0_), channel_id=1, source_target_pairs={{0,6},{1,7},{2,0},{3,1},{4,2},{5,3},{6,4},{7,5},{8,14},{9,15},{10,... | collective-permute-start | bytes 884744 | tf_op jit(solution)/shard_map/ppermute | solution.py:290
  44.3 14.0 %collective-permute-start.18 = (bf16[72,2048]{1,0:T(8,128)(2,1)S(1)}, bf16[72,2048]{1,0:T(8,128)(2,1)S(1)}, u32[]{:S(2)}, u32[]{:S(2)}) collective-permute-start(bf16[72,2048]{1,0:T(8,128)(2,1)S(1)} %get-tuple-element.99.refs_1_), channel_id=1, source_target_pairs={{0,2},{1,3},{2,4},{3,5},{4,6},{5,7},{6,0},{7,1},{8,10},{9,11},{10,... | collective-permute-start | bytes 884744 | tf_op jit(solution)/shard_map/ppermute | solution.py:290
  49.6 14.7 %collective-permute-start.19 = (bf16[72,2048]{1,0:T(8,128)(2,1)S(1)}, bf16[72,2048]{1,0:T(8,128)(2,1)S(1)}, u32[]{:S(2)}, u32[]{:S(2)}) collective-permute-start(bf16[72,2048]{1,0:T(8,128)(2,1)S(1)} %collective-permute-done.17.refs_2_), channel_id=1, source_target_pairs={{0,2},{1,3},{2,4},{3,5},{4,6},{5,7},{6,0},{7,1},{8,10},{9,11},{10,... | collective-permute-start | bytes 884744 | tf_op jit(solution)/shard_map/ppermute | solution.py:290
  50.8 13.5 %collective-permute-start.20 = (bf16[72,2048]{1,0:T(8,128)(2,1)S(1)}, bf16[72,2048]{1,0:T(8,128)(2,1)S(1)}, u32[]{:S(2)}, u32[]{:S(2)}) collective-permute-start(bf16[72,2048]{1,0:T(8,128)(2,1)S(1)} %collective-permute-done.16.refs_1_), channel_id=1, source_target_pairs={{0,6},{1,7},{2,0},{3,1},{4,2},{5,3},{6,4},{7,5},{8,14},{9,15},{10,... | collective-permute-start | bytes 884744 | tf_op jit(solution)/shard_map/ppermute | solution.py:290
  61.0 9.3 %collective-permute-start.22 = (bf16[72,2048]{1,0:T(8,128)(2,1)S(1)}, bf16[72,2048]{1,0:T(8,128)(2,1)S(1)}, u32[]{:S(2)}, u32[]{:S(2)}) collective-permute-start(bf16[72,2048]{1,0:T(8,128)(2,1)S(1)} %get-tuple-element.113), channel_id=1, source_target_pairs={{0,2},{1,3},{2,4},{3,5},{4,6},{5,7},{6,0},{7,1},{8,10},{9,11},{10,... | collective-permute-start | bytes 884744 | tf_op jit(solution)/shard_map/ppermute | solution.py:290
  61.3 9.1 %collective-permute-start.23 = (bf16[72,2048]{1,0:T(8,128)(2,1)S(1)}, bf16[72,2048]{1,0:T(8,128)(2,1)S(1)}, u32[]{:S(2)}, u32[]{:S(2)}) collective-permute-start(bf16[72,2048]{1,0:T(8,128)(2,1)S(1)} %get-tuple-element.117), channel_id=1, source_target_pairs={{0,6},{1,7},{2,0},{3,1},{4,2},{5,3},{6,4},{7,5},{8,14},{9,15},{10,... | collective-permute-start | bytes 884744 | tf_op jit(solution)/shard_map/ppermute | solution.py:290
  64.3 21.0 %copy-start.7 = (bf16[1,4096,192]{1,2,0:T(8,128)(2,1)S(1)}, bf16[1,4096,192]{1,2,0:T(8,128)(2,1)}, u32[]{:S(2)}) copy-start(bf16[1,4096,192]{1,2,0:T(8,128)(2,1)} %param.16) | copy-start | bytes 4718596
  64.3 21.0 %copy-start.8 = (bf16[1,192,4096]{2,1,0:T(8,128)(2,1)S(1)}, bf16[1,192,4096]{2,1,0:T(8,128)(2,1)}, u32[]{:S(2)}) copy-start(bf16[1,192,4096]{2,1,0:T(8,128)(2,1)} %param.17) | copy-start | bytes 4718596
  66.8 18.6 %copy-start.6 = (bf16[1,4096,192]{1,2,0:T(8,128)(2,1)S(1)}, bf16[1,4096,192]{1,2,0:T(8,128)(2,1)}, u32[]{:S(2)}) copy-start(bf16[1,4096,192]{1,2,0:T(8,128)(2,1)} %param.15) | copy-start | bytes 4718596
  66.8 10.5 %collective-permute-start.21 = (bf16[72,2048]{1,0:T(8,128)(2,1)S(1)}, bf16[72,2048]{1,0:T(8,128)(2,1)S(1)}, u32[]{:S(2)}, u32[]{:S(2)}) collective-permute-start(bf16[72,2048]{1,0:T(8,128)(2,1)S(1)} %get-tuple-element.116), channel_id=1, source_target_pairs={{0,2},{1,3},{2,4},{3,5},{4,6},{5,7},{6,0},{7,1},{8,10},{9,11},{10,... | collective-permute-start | bytes 884744 | tf_op jit(solution)/shard_map/ppermute | solution.py:290
  67.4 10.0 %collective-permute-start.25 = (bf16[72,2048]{1,0:T(8,128)(2,1)S(1)}, bf16[72,2048]{1,0:T(8,128)(2,1)S(1)}, u32[]{:S(2)}, u32[]{:S(2)}) collective-permute-start(bf16[72,2048]{1,0:T(8,128)(2,1)S(1)} %get-tuple-element.122), channel_id=1, source_target_pairs={{0,6},{1,7},{2,0},{3,1},{4,2},{5,3},{6,4},{7,5},{8,14},{9,15},{10,... | collective-permute-start | bytes 884744 | tf_op jit(solution)/shard_map/ppermute | solution.py:290
  77.4 8.0 %collective-permute-start.24 = (bf16[72,2048]{1,0:T(8,128)(2,1)S(1)}, bf16[72,2048]{1,0:T(8,128)(2,1)S(1)}, u32[]{:S(2)}, u32[]{:S(2)}) collective-permute-start(bf16[72,2048]{1,0:T(8,128)(2,1)S(1)} %add_convert_fusion.5), channel_id=1, source_target_pairs={{0,2},{1,3},{2,4},{3,5},{4,6},{5,7},{6,0},{7,1},{8,10},{9,11},{10,... | collective-permute-start | bytes 884744 | tf_op jit(solution)/shard_map/ppermute | solution.py:290
  77.5 7.8 %collective-permute-start.26 = (bf16[72,2048]{1,0:T(8,128)(2,1)S(1)}, bf16[72,2048]{1,0:T(8,128)(2,1)S(1)}, u32[]{:S(2)}, u32[]{:S(2)}) collective-permute-start(bf16[72,2048]{1,0:T(8,128)(2,1)S(1)} %add_convert_fusion.4), channel_id=1, source_target_pairs={{0,6},{1,7},{2,0},{3,1},{4,2},{5,3},{6,4},{7,5},{8,14},{9,15},{10,... | collective-permute-start | bytes 884744 | tf_op jit(solution)/shard_map/ppermute | solution.py:290
  85.4 22.8 %copy-start.2 = (bf16[256,4096]{1,0:T(8,128)(2,1)S(1)}, bf16[256,4096]{1,0:T(8,128)(2,1)}, u32[]{:S(2)}) copy-start(bf16[256,4096]{1,0:T(8,128)(2,1)} %copy-done.1) | copy-start | bytes 6291460
